TPU v7x, 256 devices: a whole 4x4x8 slice. The times are simulated.
256 devices in a mesh: group: 32 (over z_hi, x, core), tp: 8 (over z_lo, y).
Axes of the slice: x: 4, y: 4, z: 8 (z_hi: 4, z_lo: 2; z = z_hi * 2 + z_lo), core: 2. Of those that a mesh axis runs over, the one named last changes fastest.
Arguments:
- queries: bfloat16 [16384, 4096], P('group', 'tp'), may hold values from -5 to 5
- fresh_kv: bfloat16 [16384, 2048], P('group', 'tp'), may hold values from -4.5 to 4.5
- page_pool: bfloat16 [3840, 64, 2048], P('group', None, 'tp'), may hold values from -5 to 5
- out_weight: bfloat16 [4096, 8192], P('tp'), may hold values from -0.5 to 0.5
- request_row: int32 [256], replicated, may hold values from 0 to 2047, as said below
- request_len: int32 [256], replicated, may hold values from 129 to 384
- request_pages: int32 [256, 6], replicated, may hold values from 24 to 119, as said below
- resident_len: int32 [2048], replicated, may hold values from 0 to 64, as said below
- prefix_len: int32 [16], replicated, may hold values from 64 to 1536
Outputs:
- hidden: bfloat16 [16384, 8192], P(('group', 'tp'))
Inputs may be any that keep to these rules, and one draw needn't show every extreme that they name: `request_row`: all distinct; each prefill group sends exactly one request to each decode group (the group is request_row // 128). `request_pages`: the rows of one prefill group's requests hold distinct pages, all from 24 on. `resident_len`: exactly 0 on the rows that receive a request, 1 or more on the others.
All inputs are finite; a program needn't handle non-finite values.
Results may differ from a plain program's by a relative error of at most 0.022.
Values may be sent and summed in bfloat16 or wider, within the bound.
No kernel may reach another device: no remote copies, remote signals or barrier semaphores. Data moves between devices by JAX's collectives and lax.ppermute only.
A program may use at most 192 MiB of HBM per device.

v0:
```python
import math

import jax
import jax.numpy as jnp
from jax import lax
from jax.sharding import PartitionSpec as P

HD = 128
POS = 4
PREF = 24


def attend(query_in, key_in, value_in, allowed):
    scores = jnp.einsum(
        "brkgd,bskd->bkgrs", query_in, key_in, preferred_element_type=jnp.float32
    ) / math.sqrt(HD)
    scores = jnp.where(allowed[:, None, None, :, :], scores, -1e30)
    weights = jax.nn.softmax(scores, axis=-1).astype(jnp.bfloat16)
    mixed = jnp.einsum("bkgrs,bskd->brkgd", weights, value_in, preferred_element_type=jnp.float32)
    return mixed.astype(jnp.bfloat16)


def on_device(
    queries,
    fresh_kv,
    page_pool,
    out_weight,
    request_row,
    request_len,
    request_pages,
    resident_len,
    prefix_len,
):
    group_count = lax.axis_size("group")
    prefill_count = group_count // 2
    decode_count = group_count - prefill_count
    group_index = lax.axis_index("group")
    row_count = queries.shape[0]
    pool_pages, page_len, pool_width = page_pool.shape
    pages_most = request_pages.shape[1]
    kv_local = pool_width // (2 * HD)
    q_local = queries.shape[1] // HD
    group_ratio = q_local // kv_local
    decode_rows = row_count // POS
    owner_group = group_index % prefill_count
    dest_group = request_row // decode_rows
    local_dest = lax.dynamic_slice_in_dim(dest_group, owner_group * decode_count, decode_count)
    matches = local_dest[None, :] == jnp.arange(decode_count, dtype=jnp.int32)[:, None]
    chosen = jnp.sum(
        jnp.where(matches, jnp.arange(decode_count, dtype=jnp.int32)[None, :], 0), axis=1
    )
    page_table = lax.dynamic_slice_in_dim(request_pages, owner_group * decode_count, decode_count)[
        chosen
    ]
    empty_slots = jnp.zeros((prefill_count, pages_most, page_len, pool_width), page_pool.dtype)
    outgoing = jnp.concatenate([empty_slots, page_pool[page_table]], axis=0)
    incoming = lax.all_to_all(outgoing, "group", split_axis=0, concat_axis=0, tiled=True)
    query_heads = queries.reshape(row_count, kv_local, group_ratio, HD)
    fresh_heads = fresh_kv.reshape(row_count, kv_local, 2, HD)
    prefix_tokens = PREF * page_len
    context_tokens = pages_most * page_len

    def prefill_side(unused_arg):
        prefix = page_pool[:PREF].reshape(prefix_tokens, kv_local, 2, HD)
        all_keys = jnp.concatenate([prefix, fresh_heads], axis=0)
        key_pos = jnp.arange(prefix_tokens + row_count, dtype=jnp.int32)[None, :]
        row_pos = jnp.arange(row_count, dtype=jnp.int32)[:, None]
        allowed = jnp.where(
            key_pos < prefix_tokens,
            key_pos < prefix_len[owner_group],
            key_pos - prefix_tokens <= row_pos,
        )
        return attend(
            query_heads[None], all_keys[None, :, :, 0], all_keys[None, :, :, 1], allowed[None]
        )[0]

    def decode_side(unused_arg):
        decode_id = jnp.maximum(group_index - prefill_count, 0)
        request_ids = jnp.arange(request_row.shape[0], dtype=jnp.int32)
        row_request = (
            jnp.full((decode_count * decode_rows,), -1, jnp.int32).at[request_row].set(request_ids)
        )
        local_req = lax.dynamic_slice_in_dim(row_request, decode_id * decode_rows, decode_rows)
        arrived = local_req >= 0
        request = jnp.maximum(local_req, 0)
        row_ids = jnp.arange(decode_rows, dtype=jnp.int32)
        step_ids = jnp.arange(pages_most, dtype=jnp.int32)
        remote = (request // decode_count)[:, None] * pages_most + step_ids[None, :]
        resident_pages = group_count * pages_most + jnp.broadcast_to(
            (row_ids % pool_pages)[:, None], (decode_rows, pages_most)
        )
        page_ids = jnp.where(arrived[:, None], remote, resident_pages)
        length = jnp.where(
            arrived,
            request_len[request],
            lax.dynamic_slice_in_dim(resident_len, decode_id * decode_rows, decode_rows),
        )
        combined = jnp.concatenate(
            [incoming.reshape(group_count * pages_most, page_len, pool_width), page_pool], axis=0
        )
        context = combined[page_ids].reshape(decode_rows, context_tokens, kv_local, 2, HD)
        new_keys = fresh_heads.reshape(decode_rows, POS, kv_local, 2, HD)
        all_keys = jnp.concatenate([context, new_keys], axis=1)
        key_pos = jnp.arange(context_tokens + POS, dtype=jnp.int32)[None, None, :]
        step_pos = jnp.arange(POS, dtype=jnp.int32)[None, :, None]
        allowed = jnp.where(
            key_pos < context_tokens,
            key_pos < length[:, None, None],
            key_pos - context_tokens <= step_pos,
        )
        query_rows = query_heads.reshape(decode_rows, POS, kv_local, group_ratio, HD)
        mixed = attend(query_rows, all_keys[:, :, :, 0], all_keys[:, :, :, 1], allowed)
        return mixed.reshape(row_count, kv_local, group_ratio, HD)

    attention = lax.cond(group_index < prefill_count, prefill_side, decode_side, 0).reshape(
        row_count, q_local * HD
    )
    share_rows = row_count // lax.axis_size("tp")
    projected = jnp.dot(attention, out_weight, preferred_element_type=jnp.float32)
    summed = lax.psum(projected.astype(jnp.bfloat16), "tp").astype(jnp.float32)
    my_rows = lax.dynamic_slice_in_dim(summed, lax.axis_index("tp") * share_rows, share_rows, 0)
    return my_rows.astype(jnp.bfloat16)


def solution(mesh):
    in_specs = (
        P("group", "tp"),
        P("group", "tp"),
        P("group", None, "tp"),
        P("tp", None),
        P(),
        P(),
        P(),
        P(),
        P(),
    )
    out_specs = P(("group", "tp"), None)
    return jax.shard_map(
        on_device, mesh=mesh, in_specs=in_specs, out_specs=out_specs, check_vma=False
    )
```

profile of v0, /device:TPU:2, one launch (start us, length us, event | category | flops | bytes accessed | tf_op | source)
XLA Modules:
  0.0 494.1 jit_solution(9901556703390245251)
XLA Ops:
  6.5 0.0 copy-start
  6.5 0.7 copy-done
  7.2 0.1 constant_dynamic-slice_fusion
  7.3 0.1 copy.56
  7.4 0.7 and_select_fusion.2
  8.1 0.1 dynamic_slice.19
  8.2 0.1 select_reduce_fusion
  8.3 0.6 gather_fusion.2
  8.9 0.1 copy.46
  8.9 0.1 copy.47
  9.0 0.1 reshape.356
  9.1 2.9 gather_fusion.3
  12.1 3.3 concatenate.12
  15.4 0.0 copy-start.2
  15.4 0.0 copy-start.3
  15.4 0.0 copy-start.4
  15.4 0.0 copy-start.5
  15.4 0.0 copy-start.6
  15.4 11.8 %all-to-all-start = ((bf16[32,6,64,256]{3,2,1,0:T(8,128)(2,1)}), bf16[32,6,64,256]{3,2,1,0:T(8,128)(2,1)}, u32[]{:S(2)}, u32[]{:S(2)}) async-start(bf16[32,6,64,256]{3,2,1,0:T(8,128)(2,1)} %concatenate.12), calls=%async_computation | async-start | bytes 12582912 | tf_op jit(solution)/shard_map/all_to_all | solution.py:57
  27.2 0.0 all-reduce.3.cloned.1.call-start
  27.3 138.9 %all-to-all-done = bf16[32,6,64,256]{3,2,1,0:T(8,128)(2,1)} async-done(((bf16[32,6,64,256]{3,2,1,0:T(8,128)(2,1)}), bf16[32,6,64,256]{3,2,1,0:T(8,128)(2,1)}, u32[]{:S(2)}, u32[]{:S(2)}) %all-to-all-start) | async-done | bytes 6291488 | tf_op jit(solution)/shard_map/all_to_all | solution.py:57
  166.2 0.0 copy-done.2
  166.2 0.0 copy-done.3
  166.2 0.0 copy-done.4
  166.2 0.0 copy-done.5
  166.2 0.0 copy-done.6
  166.3 17.8 %conditional.1 = (bf16[512,512]{1,0:T(8,128)(2,1)S(1)}) conditional(s32[]{:T(128)} %convert_element_type.36, (bf16[32,6,64,256]{3,2,1,0:T(8,128)(2,1)}, bf16[120,64,256]{2,1,0:T(8,128)(2,1)}, s32[256]{0:T(256)S(1)}, s32[]{:T(128)}, bf16[512,256]{1,0:T(8,128)(2,1)S(1)}, /*index=5*/s32[256]{0:T(256)S(1)}, s32[2048]{0:T(1024)}, ...), branch_computations={%region_1.5_spmd, %region_5.8_spmd} | conditional | flops 2202273792 | bytes 216074400 | solution.py:115
  166.5 0.6 dynamic_slice.14
  167.1 0.6 iota_compare_fusion.1
  167.7 1.9 fusion.4
  169.6 1.2 slice.12
  170.8 0.2 reshape.321
  171.0 0.1 copy.35
  171.1 0.1 copy.48
  171.2 0.2 copy.36
  171.4 0.2 copy.49
  171.6 3.1 fusion.1
  174.8 3.7 fusion
  178.4 5.4 %fusion.5 = bf16[128,4,512]{2,0,1:T(8,128)(2,1)S(1)} fusion(f32[4,512]{1,0:T(4,128)S(1)} %fusion, f32[4,512]{1,0:T(4,128)S(1)} %get-tuple-element.67, f32[2048,512,4]{1,0,2:T(8,128)S(1)} %get-tuple-element.68, pred[512,2048]{0,1:T(8,128)(4,1)S(1)} %fusion.4, bf16[1536,1,2,128]{3,0,2,1:T(8,128)(2,1)S(1)} %copy.35, bf16[512,1,2,128]{3,0,2,1:T(8,128)(2,1)S(1)} %copy.36), kind=kOutput, calls=%fused_computation.14 | convolution fusion | flops 1096024064 | bytes 19415040 | tf_op jit(solution)/shard_map/cond/branch_1_fun/bkgrs,bskd->brkgd/dot_general | solution.py:19
  183.8 0.2 copy.40
  184.1 0.0 copy-start.1
  184.1 10.1 %convolution_convert_fusion = bf16[512,8192]{1,0:T(8,128)(2,1)} fusion(bf16[512,512]{1,0:T(8,128)(2,1)S(1)} %get-tuple-element.75, bf16[512,8192]{1,0:T(8,128)(2,1)} %param.14), kind=kOutput, calls=%fused_computation.65 | convolution fusion | flops 4299161600 | bytes 17301504 | tf_op jit(solution)/shard_map/dot_general | solution.py:119
  194.1 0.0 all-reduce.3.cloned.1.call-update
  194.2 290.9 %all-reduce.3.cloned.1.call-done = bf16[512,8192]{1,0:T(8,128)(2,1)} async-done(((bf16[512,8192]{1,0:T(8,128)(2,1)}), bf16[512,8192]{1,0:T(8,128)(2,1)}) %all-reduce.3.cloned.1.call-update) | async-done | bytes 8388624 | tf_op jit(solution)/shard_map/psum | solution.py:120
  485.0 2.3 convert_convert_fusion
  487.3 0.0 copy-done.1
  (5 shorter events, 0.0 us)
Async XLA Ops:
  6.5 0.7 copy-start
  15.4 150.8 %copy-start.2 = (s32[256]{0:T(256)S(1)}, s32[256]{0:T(256)}, u32[]{:S(2)}) copy-start(s32[256]{0:T(256)} %param.16) | copy-start | bytes 3076
  15.4 150.8 %copy-start.3 = (bf16[512,512]{1,0:T(8,128)(2,1)S(1)}, bf16[512,512]{1,0:T(8,128)(2,1)}, u32[]{:S(2)}) copy-start(bf16[512,512]{1,0:T(8,128)(2,1)} %param.11) | copy-start | bytes 1572868
  15.4 150.8 %copy-start.4 = (bf16[512,256]{1,0:T(8,128)(2,1)S(1)}, bf16[512,256]{1,0:T(8,128)(2,1)}, u32[]{:S(2)}) copy-start(bf16[512,256]{1,0:T(8,128)(2,1)} %param.12) | copy-start | bytes 786436
  15.4 150.8 %copy-start.5 = (s32[256]{0:T(256)S(1)}, s32[256]{0:T(256)}, u32[]{:S(2)}) copy-start(s32[256]{0:T(256)} %param.15) | copy-start | bytes 3076
  15.4 150.8 %copy-start.6 = (s32[16]{0:T(128)S(1)}, s32[16]{0:T(128)}, u32[]{:S(2)}) copy-start(s32[16]{0:T(128)} %param.19) | copy-start | bytes 196
  15.4 150.8 %all-to-all-start = ((bf16[32,6,64,256]{3,2,1,0:T(8,128)(2,1)}), bf16[32,6,64,256]{3,2,1,0:T(8,128)(2,1)}, u32[]{:S(2)}, u32[]{:S(2)}) async-start(bf16[32,6,64,256]{3,2,1,0:T(8,128)(2,1)} %concatenate.12), calls=%async_computation | async-start | bytes 12582912 | tf_op jit(solution)/shard_map/all_to_all | solution.py:57
  27.2 457.8 %all-reduce.3.cloned.1.call-start = ((), (), s32[]{:S(2)}) async-start(), calls=%async_computation.1 | async-start | bytes 16777216 | tf_op jit(solution)/shard_map/psum | solution.py:120
  184.1 303.2 %copy-start.1 = (s32[256,6]{0,1:T(8,128)S(1)}, s32[256,6]{0,1:T(8,128)}, u32[]{:S(2)}) copy-start(s32[256,6]{0,1:T(8,128)} %param.17) | copy-start | bytes 18436
Sparse Core Ops, SparseCore 0:
  194.3 290.7 all-reduce.2
where the time goes:
time: 497 us; the launch traced here: 494 us
  waiting for transfers between devices  430 us (87%)
  matrix products  18.6 us (4%)
  between operations  13.5 us (3%)
  starting transfers between devices  11.8 us (2%)
  local copies, waits for them, and re-layouts  10.8 us (2%)
  other arithmetic  9.26 us (2%)
    psum x1, waiting for transfers between devices, on_device(): summed = lax.psum(projected.astype(jnp.bfloat16), 'tp').astype(jnp.float32)  291 us
    all_to_all x1, waiting for transfers between devices, on_device(): lax.all_to_all(outgoing, 'group', split_axis=0, concat_axis=0, tiled=True)  139 us
    all_to_all x1, starting transfers between devices, on_device(): lax.all_to_all(outgoing, 'group', split_axis=0, concat_axis=0, tiled=True)  11.8 us
    dot_general x1, matrix products, on_device(): jnp.dot(attention, out_weight, preferred_element_type=jnp.float32)  10.1 us
  transfers between devices with their start and end apart: 2, of which 2 were waited for; matrix products, arithmetic and copies ran while one was open for 0% of the time, Pallas kernels for 0%

commit v1 on v0

v1 whole, which is shorter than its diff:
```python
import functools
import math

import jax
import jax.numpy as jnp
from jax import lax
from jax.experimental import pallas as pl
from jax.experimental.pallas import tpu as pltpu
from jax.sharding import PartitionSpec as P

HD = 128
POS = 4
PREF = 24
HEADS = 4
NEG = -1e30
SCALE2 = math.log2(math.e) / math.sqrt(HD)
BF = jnp.bfloat16
F32 = jnp.float32


def nt_dot(a, b):
    return lax.dot_general(a, b, (((1,), (1,)), ((), ())), preferred_element_type=F32)


def nn_dot(a, b):
    return jnp.dot(a, b, preferred_element_type=F32)


def soft_mix(pieces):
    top = functools.reduce(
        jnp.maximum, [jnp.max(s, axis=-1, keepdims=True) for s, _ in pieces]
    )
    total = 0.0
    mixed = 0.0
    for s, v in pieces:
        p = jnp.exp2((s - top) * SCALE2)
        total = total + jnp.sum(p, axis=-1, keepdims=True)
        mixed = mixed + nn_dot(p.astype(BF), v)
    return (mixed / total).astype(BF)


def local_kernel(info, queries, fresh, pool, lens, out, *, rows, page_len, pool_pages):
    is_prefill, my_y, my_z, prefix = info[0], info[1], info[2], info[3]

    def place(row):
        dest = row // 64
        dist_y = lax.rem(lax.rem(dest, 4) - my_y + 4, 4)
        dist_z = jnp.abs(dest // 4 - my_z)
        return pl.multiple_of((dist_y * 2 + dist_z) * 64 + lax.rem(row, 64), 32)

    prefix_tokens = PREF * page_len

    @pl.when(is_prefill == 1)
    def _():
        span = 64

        def chunk(i, carry):
            row = pl.multiple_of(i * span, span)
            where_to = place(row)
            key_p = pool[0:PREF, :, 0:HD].reshape(prefix_tokens, HD)
            val_p = pool[0:PREF, :, HD : 2 * HD].reshape(prefix_tokens, HD)
            ok_p = lax.broadcasted_iota(jnp.int32, (1, prefix_tokens), 1) < prefix
            row_id = lax.broadcasted_iota(jnp.int32, (span, rows), 0) + row
            ok_f = lax.broadcasted_iota(jnp.int32, (span, rows), 1) <= row_id
            for h in range(HEADS):
                q = queries[pl.ds(row, span), h * HD : (h + 1) * HD]
                s_p = jnp.where(ok_p, nt_dot(q, key_p), NEG)
                s_f = jnp.where(ok_f, nt_dot(q, fresh[:, 0:HD]), NEG)
                o = soft_mix([(s_p, val_p), (s_f, fresh[:, HD : 2 * HD])])
                out[pl.ds(where_to, span), h * HD : (h + 1) * HD] = o
            return carry

        lax.fori_loop(0, rows // span, chunk, 0)

    @pl.when(is_prefill == 0)
    def _():
        each = 8
        span = each * POS
        stack = span * HEADS
        width = each * page_len
        row_id = lax.rem(lax.broadcasted_iota(jnp.int32, (stack, width), 0), span) // POS
        same = lax.broadcasted_iota(jnp.int32, (stack, width), 1) // page_len == row_id
        f_row = lax.rem(lax.broadcasted_iota(jnp.int32, (stack, span), 0), span)
        f_col = lax.broadcasted_iota(jnp.int32, (stack, span), 1)
        f_ok = jnp.logical_and(f_col // POS == f_row // POS, f_col <= f_row)

        def chunk(i, carry):
            row = pl.multiple_of(i * span, span)
            first = lax.rem(i * each, pool_pages)
            where_to = place(row)
            q = jnp.concatenate(
                [queries[pl.ds(row, span), h * HD : (h + 1) * HD] for h in range(HEADS)], axis=0
            )
            key_r = pool[pl.ds(first, each), :, 0:HD].reshape(width, HD)
            val_r = pool[pl.ds(first, each), :, HD : 2 * HD].reshape(width, HD)
            ok = jnp.logical_and(same, lens[pl.ds(i, 1), :] > 0)
            s_r = jnp.where(ok, nt_dot(q, key_r), NEG)
            s_f = jnp.where(f_ok, nt_dot(q, fresh[pl.ds(row, span), 0:HD]), NEG)
            o = soft_mix([(s_r, val_r), (s_f, fresh[pl.ds(row, span), HD : 2 * HD])])
            for h in range(HEADS):
                out[pl.ds(where_to, span), h * HD : (h + 1) * HD] = o[h * span : (h + 1) * span]
            return carry

        lax.fori_loop(0, rows // span, chunk, 0)


def handed_kernel(info, pages, lengths, pool, sent, out, *, count, most, page_len):
    @pl.when(info[0] == 1)
    def _():
        stack = POS * HEADS
        width = most * page_len
        col = lax.broadcasted_iota(jnp.int32, (1, width), 1)
        f_row = lax.broadcasted_iota(jnp.int32, (stack, 8), 0) // HEADS
        f_col = lax.broadcasted_iota(jnp.int32, (stack, 8), 1)
        f_ok = f_col <= f_row

        def one(i, carry):
            q = sent[i, 0:stack, :]
            new = sent[i, stack : stack + 16, :].astype(F32)
            key_n = new[0:8].astype(BF)
            val_n = new[8:16].astype(BF)
            ids = [pages[i, n] for n in range(most)]
            key_c = jnp.concatenate([pool[p, :, 0:HD] for p in ids], axis=0)
            val_c = jnp.concatenate([pool[p, :, HD : 2 * HD] for p in ids], axis=0)
            s_c = jnp.where(col < lengths[i], nt_dot(q, key_c), NEG)
            s_n = jnp.where(f_ok, nt_dot(q, key_n), NEG)
            out[i] = soft_mix([(s_c, val_c), (s_n, val_n)])
            return carry

        lax.fori_loop(0, count, one, 0, unroll=4)


def add(*terms):
    total = terms[0].astype(F32)
    for term in terms[1:]:
        total = total + term.astype(F32)
    return total.astype(BF)


def on_device(
    queries,
    fresh_kv,
    page_pool,
    out_weight,
    request_row,
    request_len,
    request_pages,
    resident_len,
    prefix_len,
):
    group_count = lax.axis_size("group")
    tp_count = lax.axis_size("tp")
    half = group_count // 2
    group = lax.axis_index("group")
    tp = lax.axis_index("tp")
    my_y, my_z = tp % 4, tp // 4
    rows = queries.shape[0]
    pool_pages, page_len, _ = page_pool.shape
    most = request_pages.shape[1]
    decode_rows = rows // POS
    is_prefill = group < half
    peer = group % half

    def y_step(x, step):
        return lax.ppermute(x, "tp", [(t, t // 4 * 4 + (t + step) % 4) for t in range(tp_count)])

    def z_swap(x):
        return lax.ppermute(x, "tp", [(t, (t + 4) % tp_count) for t in range(tp_count)])

    row_table = request_row.reshape(half, half)
    dest = row_table // decode_rows
    to_me = dest == peer
    my_rows = jnp.sum(jnp.where(to_me, row_table % decode_rows, 0), axis=1)
    own_dest = lax.dynamic_index_in_dim(dest, peer, 0, keepdims=False)
    match = own_dest[None, :] == jnp.arange(half, dtype=jnp.int32)[:, None]
    own_pages = lax.dynamic_index_in_dim(
        request_pages.reshape(half, half, most), peer, 0, keepdims=False
    )
    own_len = lax.dynamic_index_in_dim(request_len.reshape(half, half), peer, 0, keepdims=False)
    pages = jnp.sum(jnp.where(match[:, :, None], own_pages[None], 0), axis=1)
    lengths = jnp.sum(jnp.where(match, own_len[None], 0), axis=1)

    wanted = (my_rows[:, None] * POS + jnp.arange(POS, dtype=jnp.int32)[None, :]).reshape(-1)
    pick = (wanted[:, None] == jnp.arange(rows, dtype=jnp.int32)[None, :]).astype(BF)
    picked_q = jnp.dot(pick, queries, preferred_element_type=F32).astype(BF)
    picked_f = jnp.dot(pick, fresh_kv, preferred_element_type=F32).astype(BF)
    picked_f = picked_f.reshape(half, POS, 2, HD)
    fill = jnp.zeros((half, 8 - POS, HD), BF)
    parcel = jnp.concatenate(
        [
            picked_q.reshape(half, POS * HEADS, HD),
            picked_f[:, :, 0],
            fill,
            picked_f[:, :, 1],
            fill,
        ],
        axis=1,
    )
    outgoing = jnp.concatenate([parcel, parcel], axis=0)
    sent = lax.all_to_all(outgoing, "group", split_axis=0, concat_axis=0, tiled=True)[half:]

    info = jnp.stack(
        [
            is_prefill.astype(jnp.int32),
            my_y.astype(jnp.int32),
            my_z.astype(jnp.int32),
            prefix_len[peer],
        ]
    )
    my_resident = lax.dynamic_slice_in_dim(resident_len, peer * decode_rows, decode_rows)
    seen = jnp.arange(page_len, dtype=jnp.int32)[None, :] < my_resident[:, None]
    seen = seen.astype(F32).reshape(decode_rows // 8, 8 * page_len)
    smem = pl.BlockSpec(memory_space=pltpu.SMEM)
    vmem = pl.BlockSpec(memory_space=pltpu.VMEM)
    params = pltpu.CompilerParams(vmem_limit_bytes=40 * 1024 * 1024)
    local = pl.pallas_call(
        functools.partial(local_kernel, rows=rows, page_len=page_len, pool_pages=pool_pages),
        out_shape=jax.ShapeDtypeStruct((rows, HEADS * HD), BF),
        in_specs=[smem, vmem, vmem, vmem, vmem],
        out_specs=vmem,
        compiler_params=params,
        cost_estimate=pl.CostEstimate(
            flops=4 * 2048 * 2048 * 128, bytes_accessed=5 << 20, transcendentals=1 << 22
        ),
        name="local_attention",
    )(info, queries, fresh_kv, page_pool, seen)
    handed = pl.pallas_call(
        functools.partial(handed_kernel, count=half, most=most, page_len=page_len),
        out_shape=jax.ShapeDtypeStruct((half, POS * HEADS, HD), BF),
        in_specs=[smem, smem, smem, vmem, vmem],
        out_specs=vmem,
        compiler_params=params,
        name="handed_attention",
    )(info, pages, lengths, page_pool, sent)

    back = jnp.concatenate([handed, handed], axis=0)
    back = lax.all_to_all(back, "group", split_axis=0, concat_axis=0, tiled=True)[:half]
    back = back.reshape(half * POS, HEADS * HD)

    dest_t = wanted // 64
    spot = (((dest_t % 4 - my_y) % 4) * 2 + jnp.abs(dest_t // 4 - my_z)) * 64 + wanted % 64
    put = jnp.logical_and(
        jnp.arange(rows, dtype=jnp.int32)[:, None] == spot[None, :], jnp.logical_not(is_prefill)
    )
    moved = jnp.dot(put.astype(BF), back, preferred_element_type=F32).astype(BF)
    attention = jnp.where(jnp.any(put, axis=1)[:, None], moved, local)

    def along_y(blocks):
        mid = blocks[0].shape[-1] // 2
        far_r = y_step(blocks[2][..., :mid], 1)
        far_l = y_step(blocks[2][..., mid:], -1)
        right = jnp.concatenate([add(blocks[1][..., :mid], far_r), blocks[1][..., mid:]], -1)
        left = jnp.concatenate([blocks[3][..., :mid], add(blocks[3][..., mid:], far_l)], -1)
        return add(blocks[0], y_step(right, 1), y_step(left, -1))

    share = rows // tp_count
    done = []
    begin = 0
    for first, wide in (("y", 4608), ("z", 3584)):
        part = jnp.dot(
            attention, out_weight[:, begin : begin + wide], preferred_element_type=F32
        ).astype(BF)
        part = part.reshape(4, 2, share, wide)
        begin += wide
        if first == "y":
            mine = along_y([part[d] for d in range(4)])
            done.append(add(mine[0], z_swap(mine[1])))
        else:
            mine = add(part[:, 0], z_swap(part[:, 1]))
            done.append(along_y([mine[d] for d in range(4)]))
    return jnp.concatenate(done, axis=-1)


def solution(mesh):
    in_specs = (
        P("group", "tp"),
        P("group", "tp"),
        P("group", None, "tp"),
        P("tp", None),
        P(),
        P(),
        P(),
        P(),
        P(),
    )
    out_specs = P(("group", "tp"), None)
    return jax.shard_map(
        on_device, mesh=mesh, in_specs=in_specs, out_specs=out_specs, check_vma=False
    )
```

time: 497 us -> 152 us (0.31)
  waiting for transfers between devices: 430 us -> 70 us
  Pallas kernels: 0 us -> 22.1 us
  starting transfers between devices: 11.8 us -> 32.7 us
  between operations: 13.5 us -> 0.44 us
  matrix products: 18.6 us -> 12.2 us
    psum x1 -> x0, waiting for transfers between devices: 291 us -> none  [on_device(): summed = lax.psum(projected.astype(jnp.bfloat16), 'tp').astype(jnp.float32)]
    all_to_all x1, waiting for transfers between devices: 139 us -> 8.51 us  [on_device(): lax.all_to_all(outgoing, 'group', split_axis=0, concat_axis=0, tiled=True)]
    ppermute x0 -> x10, waiting for transfers between devices: none -> 61.5 us  [the longest x8 44 us: y_step(): lax.ppermute(x, 'tp', [(t, t // 4 * 4 + (t + step) % 4) for t in range(tp...]
    pallas_call x0 -> x2, Pallas kernels: none -> 22.1 us  [the longest x1 16.9 us: on_device(): pl.pallas_call(functools.partial(local_kernel, rows=rows, page_len=page_l...]
    ppermute x0 -> x10, starting transfers between devices: none -> 15.4 us  [the longest x8 14 us: y_step(): lax.ppermute(x, 'tp', [(t, t // 4 * 4 + (t + step) % 4) for t in range(tp...]
    dot_general x3 -> x5, matrix products: 18.6 us -> 12.2 us  [the longest x2 9.34 us: on_device(): jnp.dot(attention, out_weight[:, begin:begin + wide], preferred_element_t...]
    all_to_all x0 -> x1, starting transfers between devices: none -> 5.66 us  [on_device(): lax.all_to_all(back, 'group', split_axis=0, concat_axis=0, tiled=True)]
  transfers between devices with their start and end apart: 2 -> 12, of which waited for: 2 -> 10; matrix products, arithmetic and copies ran while one was open for 0% -> 6% of each run, Pallas kernels for 0% -> 11%
where the time goes in v1:
time: 152 us; the launch traced here: 151 us
  waiting for transfers between devices  70 us (46%)
  starting transfers between devices  32.7 us (22%)
  Pallas kernels  22.1 us (15%)
  matrix products  12.2 us (8%)
  local copies, waits for them, and re-layouts  8.13 us (5%)
  other arithmetic  5.52 us (4%)
    ppermute x8, waiting for transfers between devices, y_step(): lax.ppermute(x, 'tp', [(t, t // 4 * 4 + (t + step) % 4) for t in range(tp...  44 us
    ppermute x2, waiting for transfers between devices, z_swap(): lax.ppermute(x, 'tp', [(t, (t + 4) % tp_count) for t in range(tp_count)])  17.5 us
    pallas_call x1, Pallas kernels, on_device(): pl.pallas_call(functools.partial(local_kernel, rows=rows, page_len=page_l...  16.9 us
    ppermute x8, starting transfers between devices, y_step(): lax.ppermute(x, 'tp', [(t, t // 4 * 4 + (t + step) % 4) for t in range(tp...  14 us
    all_to_all x1, starting transfers between devices, on_device(): lax.all_to_all(outgoing, 'group', split_axis=0, concat_axis=0, tiled=True)  11.6 us
    dot_general x2, matrix products, on_device(): jnp.dot(attention, out_weight[:, begin:begin + wide], preferred_element_t...  9.34 us
    all_to_all x1, waiting for transfers between devices, on_device(): lax.all_to_all(outgoing, 'group', split_axis=0, concat_axis=0, tiled=True)  8.51 us
    all_to_all x1, starting transfers between devices, on_device(): lax.all_to_all(back, 'group', split_axis=0, concat_axis=0, tiled=True)  5.66 us
  transfers between devices with their start and end apart: 12, of which 10 were waited for; matrix products, arithmetic and copies ran while one was open for 6% of the time, Pallas kernels for 11%

profile of v1, /device:TPU:2, one launch (start us, length us, event | category | flops | bytes accessed | tf_op | source)
XLA Modules:
  0.0 151.2 jit_solution(16731245755581362956)
XLA Ops:
  0.0 0.8 reshape.165
  0.8 0.1 fusion.17
  1.1 1.2 convolution_convert_fusion.4
  2.4 1.3 convolution_convert_fusion.3
  3.7 0.1 concatenate.24
  3.8 0.7 pad_maximum_fusion.5
  4.6 11.6 %all-to-all-start = ((bf16[32,32,128]{2,1,0:T(8,128)(2,1)}), bf16[32,32,128]{2,1,0:T(8,128)(2,1)S(1)}, u32[]{:S(2)}, u32[]{:S(2)}) async-start(bf16[32,32,128]{2,1,0:T(8,128)(2,1)} %pad_maximum_fusion.5), calls=%async_computation | async-start | bytes 524288 | tf_op jit(solution)/shard_map/all_to_all | solution.py:200
  16.3 0.8 dynamic_slice.21
  17.2 0.6 dynamic_slice.17
  17.8 0.1 select_reduce_fusion.1.lengths
  18.1 0.2 select_reduce_fusion
  18.5 0.6 pad_add_fusion.info
  19.1 8.5 %all-to-all-done = bf16[32,32,128]{2,1,0:T(8,128)(2,1)S(1)} async-done(((bf16[32,32,128]{2,1,0:T(8,128)(2,1)}), bf16[32,32,128]{2,1,0:T(8,128)(2,1)S(1)}, u32[]{:S(2)}, u32[]{:S(2)}) %all-to-all-start) | async-done | bytes 262176 | tf_op jit(solution)/shard_map/all_to_all | solution.py:200
  27.7 2.1 %copy-done = bf16[120,64,256]{2,1,0:T(8,128)(2,1)S(1)} copy-done((bf16[120,64,256]{2,1,0:T(8,128)(2,1)S(1)}, bf16[120,64,256]{2,1,0:T(8,128)(2,1)}, u32[]{:S(2)}) %copy-start) | copy-done | bytes 3932184
  29.8 5.3 %handed_attention.1 = bf16[16,16,128]{2,1,0:T(8,128)(2,1)S(1)} custom-call(s32[4]{0:T(128)S(1)} %pad_add_fusion.info, s32[16,6]{1,0:T(8,128)S(1)} %copy.20.pages, s32[16]{0:T(128)S(1)} %select_reduce_fusion.1.lengths, bf16[120,64,256]{2,1,0:T(8,128)(2,1)S(1)} %copy-done, bf16[16,32,128]{2,1,0:T(8,128)(2,1)S(1)} %slice.126.sent), custom_call_target="tpu_custom_call" | custom-call | tf_op jit(solution)/shard_map/handed_attention/pallas_call | solution.py:227
  35.1 0.7 pad_maximum_fusion.6
  35.8 5.7 %all-to-all-start.1 = ((bf16[32,16,128]{2,1,0:T(8,128)(2,1)}), bf16[32,16,128]{2,1,0:T(8,128)(2,1)S(1)}, u32[]{:S(2)}, u32[]{:S(2)}) async-start(bf16[32,16,128]{2,1,0:T(8,128)(2,1)} %pad_maximum_fusion.6), calls=%async_computation.1 | async-start | bytes 262144 | tf_op jit(solution)/shard_map/all_to_all | solution.py:237
  41.4 0.1 fusion.11
  41.6 2.1 %copy-done.1 = bf16[120,64,256]{2,1,0:T(8,128)(2,1)S(1)} copy-done((bf16[120,64,256]{2,1,0:T(8,128)(2,1)S(1)}, bf16[120,64,256]{2,1,0:T(8,128)(2,1)}, u32[]{:S(2)}) %copy-start.1) | copy-done | bytes 3932184
  43.7 16.9 %local_attention.1 = bf16[512,512]{1,0:T(8,128)(2,1)S(1)} custom-call(s32[4]{0:T(128)S(1)} %pad_add_fusion.info, bf16[512,512]{1,0:T(8,128)(2,1)S(1)} %copy-done.2, bf16[512,256]{1,0:T(8,128)(2,1)S(1)} %copy-done.3, bf16[120,64,256]{2,1,0:T(8,128)(2,1)S(1)} %copy-done.1, f32[16,512]{1,0:T(8,128)S(1)} %compare_convert_fusion.lens), custom_call_target="tpu_custom_call" | custom-call | flops 2147483648 | bytes 5242880 | tf_op jit(solution)/shard_map/local_attention/pallas_call | solution.py:216
  60.6 0.4 fusion.5
  61.0 5.2 %convolution_convert_fusion = bf16[512,4608]{1,0:T(8,128)(2,1)S(1)} fusion(bf16[512,512]{1,0:T(8,128)(2,1)S(1)} %fusion.5, bf16[512,8192]{1,0:T(8,128)(2,1)} %param.12), kind=kOutput, calls=%fused_computation | convolution fusion | flops 2418278400 | bytes 9961472 | tf_op jit(solution)/shard_map/dot_general | solution.py:260
  66.3 0.3 fusion.27
  66.7 3.1 %collective-permute-start.2 = (bf16[2,64,2304]{2,1,0:T(8,128)(2,1)S(1)}, bf16[2,64,2304]{2,1,0:T(8,128)(2,1)S(1)}, u32[]{:S(2)}, u32[]{:S(2)}) collective-permute-start(bf16[2,64,2304]{2,1,0:T(8,128)(2,1)S(1)} %get-tuple-element.13), channel_id=1, source_target_pairs={{0,3},{1,0},{2,1},{3,2},{4,7},{5,4},{6,5},{7,6},{8,11},{9,8},{10,9... | collective-permute-start | bytes 1769480 | tf_op jit(solution)/shard_map/ppermute | solution.py:165
  69.9 4.1 %convolution_convert_fusion.1 = bf16[512,3584]{1,0:T(8,128)(2,1)S(1)} fusion(bf16[512,512]{1,0:T(8,128)(2,1)S(1)} %fusion.5, bf16[512,8192]{1,0:T(8,128)(2,1)} %param.12), kind=kOutput, calls=%fused_computation.1 | convolution fusion | flops 1880883200 | bytes 7864320 | tf_op jit(solution)/shard_map/dot_general | solution.py:260
  74.1 8.6 %collective-permute-done.2 = bf16[2,64,2304]{2,1,0:T(8,128)(2,1)S(1)} collective-permute-done((bf16[2,64,2304]{2,1,0:T(8,128)(2,1)S(1)}, bf16[2,64,2304]{2,1,0:T(8,128)(2,1)S(1)}, u32[]{:S(2)}, u32[]{:S(2)}) %collective-permute-start.2) | collective-permute-done | bytes 589856 | tf_op jit(solution)/shard_map/ppermute | solution.py:165
  82.7 0.2 add_convert_fusion
  82.9 3.8 %collective-permute-start.3 = (bf16[2,64,4608]{2,1,0:T(8,128)(2,1)S(1)}, bf16[2,64,4608]{2,1,0:T(8,128)(2,1)S(1)}, u32[]{:S(2)}, u32[]{:S(2)}) collective-permute-start(bf16[2,64,4608]{2,1,0:T(8,128)(2,1)S(1)} %pad_maximum_fusion.1), channel_id=1, source_target_pairs={{0,3},{1,0},{2,1},{3,2},{4,7},{5,4},{6,5},{7,6},{8,11},{9,8},{10,9... | collective-permute-start | bytes 3538952 | tf_op jit(solution)/shard_map/ppermute | solution.py:165
  86.7 0.1 add_convert_fusion.1
  87.0 0.1 slice_bitcast_fusion
  87.1 0.8 collective-permute-start.5
  88.0 23.4 %collective-permute-done.3 = bf16[2,64,4608]{2,1,0:T(8,128)(2,1)S(1)} collective-permute-done((bf16[2,64,4608]{2,1,0:T(8,128)(2,1)S(1)}, bf16[2,64,4608]{2,1,0:T(8,128)(2,1)S(1)}, u32[]{:S(2)}, u32[]{:S(2)}) %collective-permute-start.3) | collective-permute-done | bytes 1179680 | tf_op jit(solution)/shard_map/ppermute | solution.py:165
  111.4 3.7 %collective-permute-done.1 = bf16[2,64,4608]{2,1,0:T(8,128)(2,1)S(1)} collective-permute-done((bf16[2,64,4608]{2,1,0:T(8,128)(2,1)S(1)}, bf16[2,64,4608]{2,1,0:T(8,128)(2,1)S(1)}, u32[]{:S(2)}, u32[]{:S(2)}) %collective-permute-start.1) | collective-permute-done | bytes 1179680 | tf_op jit(solution)/shard_map/ppermute | solution.py:165
  115.1 0.4 fusion.4
  115.5 12.8 %collective-permute-done.5 = bf16[4,64,3584]{2,1,0:T(8,128)(2,1)S(1)} collective-permute-done((bf16[4,64,3584]{2,1,0:T(8,128)(2,1)S(1)}, bf16[4,64,3584]{2,1,0:T(8,128)(2,1)S(1)}, u32[]{:S(2)}, u32[]{:S(2)}) %collective-permute-start.5) | collective-permute-done | bytes 1835040 | tf_op jit(solution)/shard_map/ppermute | solution.py:168
  128.4 0.4 fusion.1
  128.8 0.1 slice_bitcast_fusion.6
  129.0 3.0 %collective-permute-start.8 = (bf16[64,1792]{1,0:T(8,128)(2,1)S(1)}, bf16[64,1792]{1,0:T(8,128)(2,1)S(1)}, u32[]{:S(2)}, u32[]{:S(2)}) collective-permute-start(bf16[64,1792]{1,0:T(8,128)(2,1)S(1)} %get-tuple-element.15), channel_id=1, source_target_pairs={{0,3},{1,0},{2,1},{3,2},{4,7},{5,4},{6,5},{7,6},{8,11},{9,8},{10,9... | collective-permute-start | bytes 688136 | tf_op jit(solution)/shard_map/ppermute | solution.py:165
  132.0 0.6 collective-permute-start.4
  132.8 2.7 %collective-permute-done.8 = bf16[64,1792]{1,0:T(8,128)(2,1)S(1)} collective-permute-done((bf16[64,1792]{1,0:T(8,128)(2,1)S(1)}, bf16[64,1792]{1,0:T(8,128)(2,1)S(1)}, u32[]{:S(2)}, u32[]{:S(2)}) %collective-permute-start.8) | collective-permute-done | bytes 229408 | tf_op jit(solution)/shard_map/ppermute | solution.py:165
  135.6 3.8 %collective-permute-start.9 = (bf16[64,3584]{1,0:T(8,128)(2,1)S(1)}, bf16[64,3584]{1,0:T(8,128)(2,1)S(1)}, u32[]{:S(2)}, u32[]{:S(2)}) collective-permute-start(bf16[64,3584]{1,0:T(8,128)(2,1)S(1)} %pad_maximum_fusion.4), channel_id=1, source_target_pairs={{0,3},{1,0},{2,1},{3,2},{4,7},{5,4},{6,5},{7,6},{8,11},{9,8},{10,9... | collective-permute-start | bytes 1376264 | tf_op jit(solution)/shard_map/ppermute | solution.py:165
  139.4 0.6 collective-permute-done.6
  140.2 4.7 %collective-permute-done.4 = bf16[64,4608]{1,0:T(8,128)(2,1)S(1)} collective-permute-done((bf16[64,4608]{1,0:T(8,128)(2,1)S(1)}, bf16[64,4608]{1,0:T(8,128)(2,1)S(1)}, u32[]{:S(2)}, u32[]{:S(2)}) %collective-permute-start.4) | collective-permute-done | bytes 589856 | tf_op jit(solution)/shard_map/ppermute | solution.py:168
  144.9 0.1 fusion.6
  145.1 1.0 collective-permute-done.9
  146.0 3.9 %collective-permute-done.7 = bf16[64,3584]{1,0:T(8,128)(2,1)S(1)} collective-permute-done((bf16[64,3584]{1,0:T(8,128)(2,1)S(1)}, bf16[64,3584]{1,0:T(8,128)(2,1)S(1)}, u32[]{:S(2)}, u32[]{:S(2)}) %collective-permute-start.7) | collective-permute-done | bytes 458784 | tf_op jit(solution)/shard_map/ppermute | solution.py:165
  150.0 0.2 fusion.8
  150.1 1.0 pad_maximum_fusion.2
  (56 shorter events, 2.0 us)
Async XLA Ops:
  0.0 17.2 %copy-start.5 = (s32[256]{0:T(256)S(1)}, s32[256]{0:T(256)}, u32[]{:S(2)}) copy-start(s32[256]{0:T(256)} %param.14) | copy-start | bytes 3076
  0.0 17.2 %copy-start.6 = (s32[16]{0:T(128)S(1)}, s32[16]{0:T(128)}, u32[]{:S(2)}) copy-start(s32[16]{0:T(128)} %param.17) | copy-start | bytes 196
  0.0 17.9 %copy-start.4 = (s32[256,6]{0,1:T(8,128)S(1)}, s32[256,6]{0,1:T(8,128)}, u32[]{:S(2)}) copy-start(s32[256,6]{0,1:T(8,128)} %param.15) | copy-start | bytes 18436
  4.6 23.1 %all-to-all-start = ((bf16[32,32,128]{2,1,0:T(8,128)(2,1)}), bf16[32,32,128]{2,1,0:T(8,128)(2,1)S(1)}, u32[]{:S(2)}, u32[]{:S(2)}) async-start(bf16[32,32,128]{2,1,0:T(8,128)(2,1)} %pad_maximum_fusion.5), calls=%async_computation | async-start | bytes 524288 | tf_op jit(solution)/shard_map/all_to_all | solution.py:200
  27.7 2.1 %copy-start = (bf16[120,64,256]{2,1,0:T(8,128)(2,1)S(1)}, bf16[120,64,256]{2,1,0:T(8,128)(2,1)}, u32[]{:S(2)}) copy-start(bf16[120,64,256]{2,1,0:T(8,128)(2,1)} %pool.3) | copy-start | bytes 11796484
  29.8 11.8 %copy-start.2 = (bf16[512,512]{1,0:T(8,128)(2,1)S(1)}, bf16[512,512]{1,0:T(8,128)(2,1)}, u32[]{:S(2)}) copy-start(bf16[512,512]{1,0:T(8,128)(2,1)} %queries.1) | copy-start | bytes 1572868
  29.8 11.8 %copy-start.3 = (bf16[512,256]{1,0:T(8,128)(2,1)S(1)}, bf16[512,256]{1,0:T(8,128)(2,1)}, u32[]{:S(2)}) copy-start(bf16[512,256]{1,0:T(8,128)(2,1)} %fresh.1) | copy-start | bytes 786436
  35.8 24.8 %all-to-all-start.1 = ((bf16[32,16,128]{2,1,0:T(8,128)(2,1)}), bf16[32,16,128]{2,1,0:T(8,128)(2,1)S(1)}, u32[]{:S(2)}, u32[]{:S(2)}) async-start(bf16[32,16,128]{2,1,0:T(8,128)(2,1)} %pad_maximum_fusion.6), calls=%async_computation.1 | async-start | bytes 262144 | tf_op jit(solution)/shard_map/all_to_all | solution.py:237
  41.6 2.1 %copy-start.1 = (bf16[120,64,256]{2,1,0:T(8,128)(2,1)S(1)}, bf16[120,64,256]{2,1,0:T(8,128)(2,1)}, u32[]{:S(2)}) copy-start(bf16[120,64,256]{2,1,0:T(8,128)(2,1)} %pool.3) | copy-start | bytes 11796484
  66.7 16.0 %collective-permute-start.2 = (bf16[2,64,2304]{2,1,0:T(8,128)(2,1)S(1)}, bf16[2,64,2304]{2,1,0:T(8,128)(2,1)S(1)}, u32[]{:S(2)}, u32[]{:S(2)}) collective-permute-start(bf16[2,64,2304]{2,1,0:T(8,128)(2,1)S(1)} %get-tuple-element.13), channel_id=1, source_target_pairs={{0,3},{1,0},{2,1},{3,2},{4,7},{5,4},{6,5},{7,6},{8,11},{9,8},{10,9... | collective-permute-start | bytes 1769480 | tf_op jit(solution)/shard_map/ppermute | solution.py:165
  69.8 16.8 %collective-permute-start = (bf16[2,64,2304]{2,1,0:T(8,128)(2,1)S(1)}, bf16[2,64,2304]{2,1,0:T(8,128)(2,1)S(1)}, u32[]{:S(2)}, u32[]{:S(2)}) collective-permute-start(bf16[2,64,2304]{2,1,0:T(8,128)(2,1)S(1)} %get-tuple-element.12), channel_id=1, source_target_pairs={{0,1},{1,2},{2,3},{3,0},{4,5},{5,6},{6,7},{7,4},{8,9},{9,10},{10,1... | collective-permute-start | bytes 1769480 | tf_op jit(solution)/shard_map/ppermute | solution.py:165
  82.9 28.5 %collective-permute-start.3 = (bf16[2,64,4608]{2,1,0:T(8,128)(2,1)S(1)}, bf16[2,64,4608]{2,1,0:T(8,128)(2,1)S(1)}, u32[]{:S(2)}, u32[]{:S(2)}) collective-permute-start(bf16[2,64,4608]{2,1,0:T(8,128)(2,1)S(1)} %pad_maximum_fusion.1), channel_id=1, source_target_pairs={{0,3},{1,0},{2,1},{3,2},{4,7},{5,4},{6,5},{7,6},{8,11},{9,8},{10,9... | collective-permute-start | bytes 3538952 | tf_op jit(solution)/shard_map/ppermute | solution.py:165
  86.9 28.2 %collective-permute-start.1 = (bf16[2,64,4608]{2,1,0:T(8,128)(2,1)S(1)}, bf16[2,64,4608]{2,1,0:T(8,128)(2,1)S(1)}, u32[]{:S(2)}, u32[]{:S(2)}) collective-permute-start(bf16[2,64,4608]{2,1,0:T(8,128)(2,1)S(1)} %pad_maximum_fusion), channel_id=1, source_target_pairs={{0,1},{1,2},{2,3},{3,0},{4,5},{5,6},{6,7},{7,4},{8,9},{9,10},{10,1... | collective-permute-start | bytes 3538952 | tf_op jit(solution)/shard_map/ppermute | solution.py:165
  87.1 41.2 %collective-permute-start.5 = (bf16[4,64,3584]{2,1,0:T(8,128)(2,1)S(1)}, bf16[4,64,3584]{2,1,0:T(8,128)(2,1)S(1)}, u32[]{:S(2)}, u32[]{:S(2)}) collective-permute-start(bf16[4,64,3584]{2,1,0:T(8,128)(2,1)S(1)} %slice_bitcast_fusion), channel_id=1, source_target_pairs={{0,4},{1,5},{2,6},{3,7},{4,0},{5,1},{6,2},{7,3},{8,12},{9,13},{10,... | collective-permute-start | bytes 5505032 | tf_op jit(solution)/shard_map/ppermute | solution.py:168
  129.0 6.6 %collective-permute-start.8 = (bf16[64,1792]{1,0:T(8,128)(2,1)S(1)}, bf16[64,1792]{1,0:T(8,128)(2,1)S(1)}, u32[]{:S(2)}, u32[]{:S(2)}) collective-permute-start(bf16[64,1792]{1,0:T(8,128)(2,1)S(1)} %get-tuple-element.15), channel_id=1, source_target_pairs={{0,3},{1,0},{2,1},{3,2},{4,7},{5,4},{6,5},{7,6},{8,11},{9,8},{10,9... | collective-permute-start | bytes 688136 | tf_op jit(solution)/shard_map/ppermute | solution.py:165
  132.0 12.9 %collective-permute-start.4 = (bf16[64,4608]{1,0:T(8,128)(2,1)S(1)}, bf16[64,4608]{1,0:T(8,128)(2,1)S(1)}, u32[]{:S(2)}, u32[]{:S(2)}) collective-permute-start(bf16[64,4608]{1,0:T(8,128)(2,1)S(1)} %slice_bitcast_fusion.2), channel_id=1, source_target_pairs={{0,4},{1,5},{2,6},{3,7},{4,0},{5,1},{6,2},{7,3},{8,12},{9,13},{10,... | collective-permute-start | bytes 1769480 | tf_op jit(solution)/shard_map/ppermute | solution.py:168
  132.7 7.3 %collective-permute-start.6 = (bf16[64,1792]{1,0:T(8,128)(2,1)S(1)}, bf16[64,1792]{1,0:T(8,128)(2,1)S(1)}, u32[]{:S(2)}, u32[]{:S(2)}) collective-permute-start(bf16[64,1792]{1,0:T(8,128)(2,1)S(1)} %get-tuple-element.14), channel_id=1, source_target_pairs={{0,1},{1,2},{2,3},{3,0},{4,5},{5,6},{6,7},{7,4},{8,9},{9,10},{10,1... | collective-permute-start | bytes 688136 | tf_op jit(solution)/shard_map/ppermute | solution.py:165
  135.6 10.4 %collective-permute-start.9 = (bf16[64,3584]{1,0:T(8,128)(2,1)S(1)}, bf16[64,3584]{1,0:T(8,128)(2,1)S(1)}, u32[]{:S(2)}, u32[]{:S(2)}) collective-permute-start(bf16[64,3584]{1,0:T(8,128)(2,1)S(1)} %pad_maximum_fusion.4), channel_id=1, source_target_pairs={{0,3},{1,0},{2,1},{3,2},{4,7},{5,4},{6,5},{7,6},{8,11},{9,8},{10,9... | collective-permute-start | bytes 1376264 | tf_op jit(solution)/shard_map/ppermute | solution.py:165
  140.1 9.8 %collective-permute-start.7 = (bf16[64,3584]{1,0:T(8,128)(2,1)S(1)}, bf16[64,3584]{1,0:T(8,128)(2,1)S(1)}, u32[]{:S(2)}, u32[]{:S(2)}) collective-permute-start(bf16[64,3584]{1,0:T(8,128)(2,1)S(1)} %pad_maximum_fusion.3), channel_id=1, source_target_pairs={{0,1},{1,2},{2,3},{3,0},{4,5},{5,6},{6,7},{7,4},{8,9},{9,10},{10,1... | collective-permute-start | bytes 1376264 | tf_op jit(solution)/shard_map/ppermute | solution.py:165

commit v2 on v0

v2 whole, which is shorter than its diff:
```python
import functools
import math

import jax
import jax.numpy as jnp
from jax import lax
from jax.experimental import pallas as pl
from jax.experimental.pallas import tpu as pltpu
from jax.sharding import PartitionSpec as P

HD = 128
POS = 4
PREF = 24
HEADS = 4
NEG = -1e30
LARGE = 54
SMALL = 54
COLS = (768, 4608, 2816)
LATE = 2816
FRONT = 54
SCALE2 = math.log2(math.e) / math.sqrt(HD)
BF = jnp.bfloat16
F32 = jnp.float32


def nt_dot(a, b):
    return lax.dot_general(a, b, (((1,), (1,)), ((), ())), preferred_element_type=F32)


def nn_dot(a, b):
    return jnp.dot(a, b, preferred_element_type=F32)


def soft_mix(pieces):
    top = functools.reduce(
        jnp.maximum, [jnp.max(s, axis=-1, keepdims=True) for s, _ in pieces]
    )
    total = 0.0
    mixed = 0.0
    for s, v in pieces:
        p = jnp.exp2((s - top) * SCALE2)
        total = total + jnp.sum(p, axis=-1, keepdims=True)
        mixed = mixed + nn_dot(p.astype(BF), v)
    return (mixed / total).astype(BF)


def wanted_rows(table, group, half, decode_rows):
    slots = half * HEADS * POS
    peer = lax.rem(group, half)
    slot = lax.broadcasted_iota(jnp.int32, (slots, half * half), 0)
    request = lax.broadcasted_iota(jnp.int32, (slots, half * half), 1)
    row = table[...]
    mine = jnp.logical_and(
        request // half == slot // (HEADS * POS), row // decode_rows == peer
    )
    first = jnp.sum(jnp.where(mine, lax.rem(row, decode_rows) * POS, 0), axis=1, keepdims=True)
    return first + lax.rem(lax.broadcasted_iota(jnp.int32, (slots, 1), 0), POS)


def pick_kernel(table, queries, fresh, out, *, half, decode_rows):
    rows = queries.shape[0]
    slots = half * HEADS * POS
    want = wanted_rows(table, lax.axis_index("group"), half, decode_rows)
    pick = (want == lax.broadcasted_iota(jnp.int32, (slots, rows), 1)).astype(F32).astype(BF)
    head = lax.rem(lax.broadcasted_iota(jnp.int32, (slots, HD), 0) // POS, HEADS)
    got_q = nn_dot(pick, queries[...])
    got_f = nn_dot(pick, fresh[...])
    one_q = got_q[:, 0:HD]
    for h in range(1, HEADS):
        one_q = jnp.where(head == h, got_q[:, h * HD : (h + 1) * HD], one_q)
    one_f = jnp.where(head == 0, got_f[:, 0:HD], got_f[:, HD : 2 * HD])
    one_f = jnp.where(head < 2, one_f, 0.0)
    for n in range(2):
        out[n * slots : (n + 1) * slots, 0:HD] = one_q.astype(BF)
        out[n * slots : (n + 1) * slots, HD : 2 * HD] = one_f.astype(BF)


def stacked(ref, row, span):
    return jnp.concatenate(
        [ref[pl.ds(row, span), h * HD : (h + 1) * HD] for h in range(HEADS)], axis=0
    )


def fresh_mask(span):
    row = lax.rem(lax.broadcasted_iota(jnp.int32, (span * HEADS, span), 0), span)
    col = lax.broadcasted_iota(jnp.int32, (span * HEADS, span), 1)
    return jnp.logical_and(col // POS == row // POS, col <= row)


def turn(dist):
    return jnp.where(dist == 0, 3, jnp.where(dist == 1, 1, jnp.where(dist == 2, 0, 2)))


def local_kernel(prefix_len, resident_len, queries, fresh, pool, out, held, sems, *, half, part):
    group = lax.axis_index("group")
    tp = lax.axis_index("tp")
    peer = lax.rem(group, half)
    my_y = lax.rem(tp, 4)
    rows = queries.shape[0]
    pool_pages, page_len, _ = pool.shape
    each = 8
    parts = pool_pages // each

    def fetch(n):
        return pltpu.make_async_copy(
            pool.at[pl.ds(n * each, each)], held.at[pl.ds(n * each, each)], sems.at[n]
        )

    def place(row):
        dist_y = lax.rem(lax.rem(row // 64, 4) - my_y + 4, 4)
        return pl.multiple_of(turn(dist_y) * 64 + lax.rem(row, 64), 32)

    @pl.when(group < half)
    def _():
        prefix_tokens = PREF * page_len
        for n in range(PREF // each):
            fetch(n).start()
        for n in range(PREF // each):
            fetch(n).wait()
        prefix = prefix_len[peer]
        span = 64
        stack = span * HEADS
        ok_p = lax.broadcasted_iota(jnp.int32, (1, prefix_tokens), 1) < prefix
        row_id = lax.rem(lax.broadcasted_iota(jnp.int32, (stack, rows), 0), span)
        ahead = lax.broadcasted_iota(jnp.int32, (stack, rows), 1) - row_id

        def chunk(i, carry):
            row = pl.multiple_of(i * span, span)
            where_to = place(row)
            q = stacked(queries, row, span)
            key_p = held[0:PREF, :, 0:HD].reshape(prefix_tokens, HD)
            val_p = held[0:PREF, :, HD : 2 * HD].reshape(prefix_tokens, HD)
            s_p = jnp.where(ok_p, nt_dot(q, key_p), NEG)
            s_f = jnp.where(ahead <= row, nt_dot(q, fresh[:, 0:HD]), NEG)
            o = soft_mix([(s_p, val_p), (s_f, fresh[:, HD : 2 * HD])])
            for h in range(HEADS):
                out[pl.ds(where_to, span), h * HD : (h + 1) * HD] = o[h * span : (h + 1) * span]
            return carry

        lax.fori_loop(part * (rows // span // 2), (part + 1) * (rows // span // 2), chunk, 0)

    @pl.when(group >= half)
    def _():
        steps = rows // POS // each
        mine = range(part * (steps // 2), min((part + 1) * (steps // 2), parts))
        if part == 1:
            fetch(0).start()
        for n in mine:
            fetch(n).start()
        if part == 1:
            fetch(0).wait()
        span = each * POS
        stack = span * HEADS
        width = each * page_len
        decode_rows = rows // POS
        row_id = lax.rem(lax.broadcasted_iota(jnp.int32, (stack, width), 0), span) // POS
        col = lax.broadcasted_iota(jnp.int32, (stack, width), 1)
        same = col // page_len == row_id
        slot = lax.broadcasted_iota(jnp.int32, (1, width), 1)
        f_ok = fresh_mask(span)

        def chunk(i, carry):
            @pl.when(i < parts)
            def _():
                fetch(i).wait()

            row = pl.multiple_of(i * span, span)
            first = lax.rem(i, parts) * each
            where_to = place(row)
            q = stacked(queries, row, span)
            key_r = held[pl.ds(first, each), :, 0:HD].reshape(width, HD)
            val_r = held[pl.ds(first, each), :, HD : 2 * HD].reshape(width, HD)
            length = jnp.zeros((1, width), jnp.int32)
            for e in range(each):
                length = jnp.where(
                    slot // page_len == e, resident_len[peer * decode_rows + i * each + e], length
                )
            seen = lax.rem(slot, page_len) < length
            s_r = jnp.where(jnp.logical_and(same, seen), nt_dot(q, key_r), NEG)
            s_f = jnp.where(f_ok, nt_dot(q, fresh[pl.ds(row, span), 0:HD]), NEG)
            o = soft_mix([(s_r, val_r), (s_f, fresh[pl.ds(row, span), HD : 2 * HD])])
            for h in range(HEADS):
                out[pl.ds(where_to, span), h * HD : (h + 1) * HD] = o[h * span : (h + 1) * span]
            return carry

        lax.fori_loop(part * (rows // span // 2), (part + 1) * (rows // span // 2), chunk, 0)


def handed_kernel(
    table, lengths, pages, all_pages, sent, out, slots, pool, sems, *, half, decode_rows
):
    group = lax.axis_index("group")
    most = pages.shape[0]
    page_len = pool.shape[1]
    each = 4
    stack = HEADS * POS
    span = each * stack
    width = each * most * page_len

    @pl.when(group >= half)
    def _():
        out[...] = jnp.zeros_like(out)

    @pl.when(group < half)
    def _():
        parts = sems.shape[0]
        each_part = pool.shape[0] // parts

        def fetch(n):
            at = pl.ds(n * each_part, each_part)
            return pltpu.make_async_copy(all_pages.at[at], pool.at[at], sems.at[n])

        for n in range(parts):
            fetch(n).start()
        for i in range(half):
            slots[table[group * half + i] // decode_rows] = group * half + i
        row_id = lax.broadcasted_iota(jnp.int32, (span, width), 0) // stack
        col = lax.broadcasted_iota(jnp.int32, (span, width), 1)
        same = col // (most * page_len) == row_id
        slot = lax.broadcasted_iota(jnp.int32, (1, width), 1)
        f_row = lax.broadcasted_iota(jnp.int32, (span, span), 0)
        f_col = lax.broadcasted_iota(jnp.int32, (span, span), 1)
        f_ok = jnp.logical_and(
            f_row // stack == f_col // stack, lax.rem(f_col, stack) <= lax.rem(f_row, POS)
        )
        for n in range(parts):
            fetch(n).wait()
        for b in range(half // each):
            length = jnp.zeros((1, width), jnp.int32)
            ids = []
            for e in range(each):
                request = slots[b * each + e]
                ids += [pages[n, request] for n in range(most)]
                length = jnp.where(slot // (most * page_len) == e, lengths[request], length)
            seen = lax.rem(slot, most * page_len) < length
            new = sent[(half // each + b) * span : (half // each + b + 1) * span, :]
            q = new[:, 0:HD]
            key_n = new[:, HD : 2 * HD]
            val_n = pltpu.roll(key_n.astype(F32), span - POS, 0).astype(BF)
            key_c = jnp.concatenate([pool[n, :, 0:HD] for n in ids], axis=0)
            val_c = jnp.concatenate([pool[n, :, HD : 2 * HD] for n in ids], axis=0)
            s_c = jnp.where(jnp.logical_and(same, seen), nt_dot(q, key_c), NEG)
            s_n = jnp.where(f_ok, nt_dot(q, key_n), NEG)
            o = soft_mix([(s_c, val_c), (s_n, val_n)])
            for n in range(2):
                out[(n * half // each + b) * span : (n * half // each + b + 1) * span, :] = o


def front_kernel(
    table, first, second, back, weight, x13, x0, near, far, y_r, y_l, a1, held, sems, *, half, decode_rows
):
    group = lax.axis_index("group")
    tp = lax.axis_index("tp")
    my_z = tp // 4
    rows, wide = first.shape
    slots = half * HEADS * POS
    count, _, part = held.shape

    def fetch(n):
        begin = (n + 1) * part if n < count - 1 else 0
        return pltpu.make_async_copy(
            weight.at[:, pl.ds(begin, part)], held.at[n], sems.at[n]
        )

    for n in range(count):
        fetch(n).start()

    @pl.when(my_z == 0)
    def _():
        near[...] = first[...]
        far[...] = second[...]

    @pl.when(my_z == 1)
    def _():
        near[...] = second[...]
        far[...] = first[...]

    @pl.when(group >= half)
    def _():
        want = wanted_rows(table, group, half, decode_rows)
        dest = want // 64
        dist_y = lax.rem(lax.rem(dest, 4) - lax.rem(tp, 4) + 4, 4)
        spot = turn(dist_y) * 64 + lax.rem(want, 64)
        dist_z = jnp.abs(dest // 4 - my_z)
        here = lax.broadcasted_iota(jnp.int32, (slots, rows), 1)
        head = lax.rem(lax.broadcasted_iota(jnp.int32, (slots, HD), 0) // POS, HEADS)
        came = back[0:slots, :].astype(F32)
        came = [jnp.where(head == h, came, 0.0).astype(BF) for h in range(HEADS)]
        for dist, out in ((0, near), (1, far)):
            put = jnp.logical_and(spot == here, dist_z == dist).astype(F32).astype(BF)

            def spread(x):
                return lax.dot_general(
                    put, x, (((0,), (0,)), ((), ())), preferred_element_type=F32
                )

            hit = spread(jnp.ones((slots, HD), BF)) > 0.5
            for h in range(HEADS):
                at = slice(h * HD, (h + 1) * HD)
                out[:, at] = jnp.where(hit, spread(came[h]), out[:, at].astype(F32)).astype(BF)

    share = rows // 4
    x2 = jnp.concatenate([near[0:share], far[0:share]], axis=0)
    for n in range(count - 1):
        fetch(n).wait()
        piece = nn_dot(x2, held[n]).astype(BF)
        out, at = (y_r, n) if n < (count - 1) // 2 else (y_l, n - (count - 1) // 2)
        out[:, at * part : (at + 1) * part] = piece
    fetch(count - 1).wait()
    a1[...] = nn_dot(far[...], held[count - 1]).astype(BF)
    for n, d in enumerate((1, 2)):
        x13[2 * n * share : (2 * n + 1) * share] = near[d * share : (d + 1) * share]
        x13[(2 * n + 1) * share : (2 * n + 2) * share] = far[d * share : (d + 1) * share]
    x0[0:share] = near[3 * share :]
    x0[share:] = far[3 * share :]


def add(*terms):
    total = terms[0].astype(F32)
    for term in terms[1:]:
        total = total + term.astype(F32)
    return total.astype(BF)


def on_device(
    queries,
    fresh_kv,
    page_pool,
    out_weight,
    request_row,
    request_len,
    request_pages,
    resident_len,
    prefix_len,
):
    half = lax.axis_size("group") // 2
    tp_count = lax.axis_size("tp")
    rows, wide = queries.shape
    kv_wide = fresh_kv.shape[1]
    pool_pages, page_len, _ = page_pool.shape
    most = request_pages.shape[1]
    decode_rows = rows // POS
    slots = half * HEADS * POS
    smem = pl.BlockSpec(memory_space=pltpu.SMEM)
    vmem = pl.BlockSpec(memory_space=pltpu.VMEM)
    anywhere = pl.BlockSpec(memory_space=pl.ANY)
    large = pltpu.CompilerParams(vmem_limit_bytes=LARGE * 1024 * 1024)
    small = pltpu.CompilerParams(vmem_limit_bytes=SMALL * 1024 * 1024)

    def y_step(x, step):
        return lax.ppermute(x, "tp", [(t, t // 4 * 4 + (t + step) % 4) for t in range(tp_count)])

    def z_swap(x):
        return lax.ppermute(x, "tp", [(t, (t + 4) % tp_count) for t in range(tp_count)])

    table = request_row.reshape(1, half * half)
    parcel = pl.pallas_call(
        functools.partial(pick_kernel, half=half, decode_rows=decode_rows),
        out_shape=jax.ShapeDtypeStruct((2 * slots, kv_wide), BF),
        in_specs=[vmem] * 3,
        out_specs=vmem,
        compiler_params=large,
        name="pick_rows",
    )(table, queries, fresh_kv)
    sent = lax.all_to_all(parcel, "group", split_axis=0, concat_axis=0, tiled=True)

    def attend_half(part):
        return pl.pallas_call(
            functools.partial(local_kernel, half=half, part=part),
            out_shape=jax.ShapeDtypeStruct((rows // 2, wide), BF),
            in_specs=[smem, smem, vmem, vmem, anywhere],
            out_specs=vmem,
            scratch_shapes=[
                pltpu.VMEM(page_pool.shape, BF),
                pltpu.SemaphoreType.DMA((pool_pages // 8,)),
            ],
            compiler_params=large,
            cost_estimate=pl.CostEstimate(
                flops=8 * 2048 * 2048 * 128, bytes_accessed=5 << 20, transcendentals=1 << 21
            ),
            name="local_attention",
        )(prefix_len, resident_len, queries, fresh_kv, page_pool)

    first = attend_half(0)
    sent, first = lax.optimization_barrier((sent, first))
    handed = pl.pallas_call(
        functools.partial(handed_kernel, half=half, decode_rows=decode_rows),
        out_shape=jax.ShapeDtypeStruct((2 * slots, HD), BF),
        in_specs=[smem, smem, smem, anywhere, vmem],
        out_specs=vmem,
        scratch_shapes=[
            pltpu.SMEM((half,), jnp.int32),
            pltpu.VMEM(page_pool.shape, BF),
            pltpu.SemaphoreType.DMA((pool_pages // 8,)),
        ],
        compiler_params=small,
        name="handed_attention",
    )(request_row, request_len, request_pages.T, page_pool, sent)
    back = lax.all_to_all(handed, "group", split_axis=0, concat_axis=0, tiled=True)
    second = attend_half(1)
    share = rows // tp_count
    cols_a, cols_y, cols_b = COLS
    pieces = cols_y // cols_a + 1

    def made(*shape):
        return jax.ShapeDtypeStruct(shape, BF)

    x13, x0, near, far, y2_r, y2_l, a1 = pl.pallas_call(
        functools.partial(front_kernel, half=half, decode_rows=decode_rows),
        out_shape=(
            made(4 * share, wide),
            made(2 * share, wide),
            made(4 * share, wide),
            made(4 * share, wide),
            made(2 * share, cols_y // 2),
            made(2 * share, cols_y // 2),
            made(4 * share, cols_a),
        ),
        in_specs=[vmem] * 4 + [anywhere],
        out_specs=(vmem,) * 7,
        scratch_shapes=[
            pltpu.VMEM((pieces, wide, cols_a), BF),
            pltpu.SemaphoreType.DMA((pieces,)),
        ],
        compiler_params=pltpu.CompilerParams(vmem_limit_bytes=FRONT * 1024 * 1024),
        name="front_products",
    )(table, first, second, back, out_weight)

    cuts = {"a": (0, cols_a), "y": (cols_a, cols_a + cols_y), "b": (cols_a + cols_y, sum(COLS))}

    def blocks(x):
        return x.reshape(-1, share, x.shape[1])

    def products(given, names):
        parts = []
        for name in names:
            begin, end = cuts[name[0]]
            part = jnp.dot(
                given[name], out_weight[:, begin:end], preferred_element_type=F32
            ).astype(BF)
            part, given = lax.optimization_barrier((part, given))
            parts.append(blocks(part))
        return parts, given

    def start_far(far):
        mid = far.shape[-1] // 2
        return y_step(far[..., :mid], 1), y_step(far[..., mid:], -1)

    def start_near(next_r, next_l, far_r, far_l):
        mid = far_r.shape[-1]
        right = jnp.concatenate([add(next_r[..., :mid], far_r), next_r[..., mid:]], -1)
        left = jnp.concatenate([next_l[..., :mid], add(next_l[..., mid:], far_l)], -1)
        return y_step(right, 1), y_step(left, -1)

    far_y = y_step(blocks(y2_r), 1), y_step(blocks(y2_l), -1)
    come_a = z_swap(blocks(a1))
    given = {"y13": x13, "b1": far, "a0": near, "y0": x0, "b0": near}
    (y13, b1), given = products(given, ("y13", "b1"))
    far_y, come_a, given, y13, b1 = lax.optimization_barrier((far_y, come_a, given, y13, b1))

    near_y = start_near(y13[0:2], y13[2:4], *far_y)
    come_b = z_swap(b1)
    (a0, y0, b0), given = products(given, ("a0", "y0", "b0"))
    mine_a = add(a0, come_a)
    far_a = start_far(mine_a[0])
    near_y, come_b, far_a, y0, b0 = lax.optimization_barrier((near_y, come_b, far_a, y0, b0))

    mine_y = add(y0, *near_y)
    soon = cols_y - LATE
    come_y = z_swap(mine_y[1][:, :soon])
    mine_b = add(b0, come_b)
    far_b = start_far(mine_b[0])
    near_a = start_near(mine_a[1], mine_a[2], *far_a)
    come_y, far_b, near_a, mine_y, mine_b = lax.optimization_barrier(
        (come_y, far_b, near_a, mine_y, mine_b)
    )

    late_y = z_swap(mine_y[1][:, soon:])
    near_b = start_near(mine_b[1], mine_b[2], *far_b)
    return jnp.concatenate(
        [
            add(mine_a[3], *near_a),
            add(mine_y[0][:, :soon], come_y),
            add(mine_y[0][:, soon:], late_y),
            add(mine_b[3], *near_b),
        ],
        axis=-1,
    )


def solution(mesh):
    in_specs = (
        P("group", "tp"),
        P("group", "tp"),
        P("group", None, "tp"),
        P("tp", None),
        P(),
        P(),
        P(),
        P(),
        P(),
    )
    out_specs = P(("group", "tp"), None)
    return jax.shard_map(
        on_device, mesh=mesh, in_specs=in_specs, out_specs=out_specs, check_vma=False
    )
```

time: 497 us -> 133 us (0.27)
  waiting for transfers between devices: 430 us -> 48.2 us
  starting transfers between devices: 11.8 us -> 42 us
  Pallas kernels: 0 us -> 28.7 us
  between operations: 13.5 us -> 0.38 us
  matrix products: 18.6 us -> 8.81 us
  local copies, waits for them, and re-layouts: 10.8 us -> 1.79 us
  other arithmetic: 9.26 us -> 2.88 us
    psum x1 -> x0, waiting for transfers between devices: 291 us -> none  [on_device(): summed = lax.psum(projected.astype(jnp.bfloat16), 'tp').astype(jnp.float32)]
    all_to_all x1 -> x2, waiting for transfers between devices: 139 us -> 5.41 us  [the longest x1 3.8 us: on_device(): lax.all_to_all(parcel, 'group', split_axis=0, concat_axis=0, tiled=True)]
    ppermute x0 -> x16, waiting for transfers between devices: none -> 42.8 us  [the longest x12 25.4 us: y_step(): lax.ppermute(x, 'tp', [(t, t // 4 * 4 + (t + step) % 4) for t in range(tp...]
    pallas_call x0 -> x5, Pallas kernels: none -> 28.7 us  [the longest x2 15.3 us: attend_half(): pl.pallas_call(functools.partial(local_kernel, half=half, part=part), out...]
    ppermute x0 -> x16, starting transfers between devices: none -> 24.7 us  [the longest x12 20.7 us: y_step(): lax.ppermute(x, 'tp', [(t, t // 4 * 4 + (t + step) % 4) for t in range(tp...]
    dot_general x3 -> x5, matrix products: 18.6 us -> 8.81 us  [products(): jnp.dot(given[name], out_weight[:, begin:end], preferred_element_type=F32)]
    all_to_all x1 -> x2, starting transfers between devices: 11.8 us -> 17.3 us  [the longest x1 11.6 us: on_device(): lax.all_to_all(parcel, 'group', split_axis=0, concat_axis=0, tiled=True)]
  transfers between devices with their start and end apart: 2 -> 18, of which waited for: 2 -> 9; matrix products, arithmetic and copies ran while one was open for 0% -> 7% of each run, Pallas kernels for 0% -> 12%
where the time goes in v2:
time: 133 us
  waiting for transfers between devices  48.2 us (36%)
  starting transfers between devices  42 us (32%)
  Pallas kernels  28.7 us (22%)
  matrix products  8.81 us (7%)
  other arithmetic  2.88 us (2%)
  local copies, waits for them, and re-layouts  1.79 us (1%)
    ppermute x12, waiting for transfers between devices, y_step(): lax.ppermute(x, 'tp', [(t, t // 4 * 4 + (t + step) % 4) for t in range(tp...  25.4 us
    ppermute x12, starting transfers between devices, y_step(): lax.ppermute(x, 'tp', [(t, t // 4 * 4 + (t + step) % 4) for t in range(tp...  20.7 us
    ppermute x4, waiting for transfers between devices, z_swap(): lax.ppermute(x, 'tp', [(t, (t + 4) % tp_count) for t in range(tp_count)])  17.4 us
    pallas_call x2, Pallas kernels, attend_half(): pl.pallas_call(functools.partial(local_kernel, half=half, part=part), out...  15.3 us
    all_to_all x1, starting transfers between devices, on_device(): lax.all_to_all(parcel, 'group', split_axis=0, concat_axis=0, tiled=True)  11.6 us
    dot_general x5, matrix products, products(): jnp.dot(given[name], out_weight[:, begin:end], preferred_element_type=F32)  8.81 us
    all_to_all x1, starting transfers between devices, on_device(): lax.all_to_all(handed, 'group', split_axis=0, concat_axis=0, tiled=True)  5.68 us
    pallas_call x1, Pallas kernels, on_device(): pl.pallas_call(functools.partial(handed_kernel, half=half, decode_rows=de...  5.57 us
  transfers between devices with their start and end apart: 18, of which 9 were waited for; matrix products, arithmetic and copies ran while one was open for 7% of the time, Pallas kernels for 12%

profile of v2, /device:TPU:2, one launch (start us, length us, event | category | flops | bytes accessed | tf_op | source)
XLA Modules:
  0.0 132.7 jit_solution(11711911917904362442)
XLA Ops:
  0.0 2.3 %pick_rows.1 = bf16[512,256]{1,0:T(8,128)(2,1)} custom-call(s32[1,256]{1,0:T(1,128)} %bitcast.57, bf16[512,512]{1,0:T(8,128)(2,1)} %queries.5, bf16[512,256]{1,0:T(8,128)(2,1)} %fresh.5), custom_call_target="tpu_custom_call" | custom-call | tf_op jit(solution)/shard_map/pick_rows/pallas_call | solution.py:357
  2.3 11.6 %all-to-all-start = ((bf16[32,16,256]{2,1,0:T(8,128)(2,1)}), bf16[32,16,256]{2,1,0:T(8,128)(2,1)S(1)}, u32[]{:S(2)}, u32[]{:S(2)}) async-start(bf16[32,16,256]{2,1,0:T(8,128)(2,1)} %bitcast.52), calls=%async_computation | async-start | bytes 524288 | tf_op jit(solution)/shard_map/all_to_all | solution.py:365
  13.9 7.7 %local_attention.2.first = bf16[256,512]{1,0:T(8,128)(2,1)} custom-call(s32[16]{0:T(128)} %prefix_len.3, s32[2048]{0:T(1024)} %resident_len.3, bf16[512,512]{1,0:T(8,128)(2,1)} %queries.5, bf16[512,256]{1,0:T(8,128)(2,1)} %fresh.5, bf16[120,64,256]{2,1,0:T(8,128)(2,1)} %all_pages.1), custom_call_target="tpu_custom_call" | custom-call | flops 4294967296 | bytes 5242880 | tf_op jit(solution)/shard_map/local_attention/pallas_call | solution.py:368
  21.6 3.8 %all-to-all-done = bf16[32,16,256]{2,1,0:T(8,128)(2,1)S(1)} async-done(((bf16[32,16,256]{2,1,0:T(8,128)(2,1)}), bf16[32,16,256]{2,1,0:T(8,128)(2,1)S(1)}, u32[]{:S(2)}, u32[]{:S(2)}) %all-to-all-start) | async-done | bytes 262176 | tf_op jit(solution)/shard_map/all_to_all | solution.py:365
  25.4 0.7 copy-done
  26.1 5.6 %handed_attention.1 = bf16[512,128]{1,0:T(8,128)(2,1)} custom-call(s32[256]{0:T(256)} %table.1, s32[256]{0:T(256)} %lengths.1, s32[6,256]{1,0:T(8,128)} %bitcast.59, bf16[120,64,256]{2,1,0:T(8,128)(2,1)} %all_pages.1, bf16[512,256]{1,0:T(8,128)(2,1)} %bitcast.53), custom_call_target="tpu_custom_call" | custom-call | tf_op jit(solution)/shard_map/handed_attention/pallas_call | solution.py:386
  31.6 5.7 %all-to-all-start.1 = ((bf16[32,16,128]{2,1,0:T(8,128)(2,1)}), bf16[32,16,128]{2,1,0:T(8,128)(2,1)S(1)}, u32[]{:S(2)}, u32[]{:S(2)}) async-start(bf16[32,16,128]{2,1,0:T(8,128)(2,1)} %bitcast.55), calls=%async_computation.1 | async-start | bytes 262144 | tf_op jit(solution)/shard_map/all_to_all | solution.py:399
  37.3 7.7 %local_attention.3.second = bf16[256,512]{1,0:T(8,128)(2,1)} custom-call(s32[16]{0:T(128)} %prefix_len.3, s32[2048]{0:T(1024)} %resident_len.3, bf16[512,512]{1,0:T(8,128)(2,1)} %queries.5, bf16[512,256]{1,0:T(8,128)(2,1)} %fresh.5, bf16[120,64,256]{2,1,0:T(8,128)(2,1)} %all_pages.1), custom_call_target="tpu_custom_call" | custom-call | flops 4294967296 | bytes 5242880 | tf_op jit(solution)/shard_map/local_attention/pallas_call | solution.py:368
  45.0 1.6 %all-to-all-done.1 = bf16[32,16,128]{2,1,0:T(8,128)(2,1)S(1)} async-done(((bf16[32,16,128]{2,1,0:T(8,128)(2,1)}), bf16[32,16,128]{2,1,0:T(8,128)(2,1)S(1)}, u32[]{:S(2)}, u32[]{:S(2)}) %all-to-all-start.1) | async-done | bytes 131104 | tf_op jit(solution)/shard_map/all_to_all | solution.py:399
  46.6 0.6 copy-done.1
  47.2 5.6 %front_products.1 = (bf16[256,512]{1,0:T(8,128)(2,1)}, bf16[128,512]{1,0:T(8,128)(2,1)}, bf16[256,512]{1,0:T(8,128)(2,1)}, bf16[256,512]{1,0:T(8,128)(2,1)}, bf1...) custom-call(s32[1,256]{1,0:T(1,128)} %bitcast.58, ...), custom_call_target="tpu_custom_call" | custom-call | tf_op jit(solution)/shard_map/front_products/pallas_call | solution.py:408
  52.8 1.7 %collective-permute-start = (bf16[2,64,2304]{2,1,0:T(8,128)(2,1)}, bf16[2,64,2304]{2,1,0:T(8,128)(2,1)S(1)}, u32[]{:S(2)}, u32[]{:S(2)}) collective-permute-start(bf16[2,64,2304]{2,1,0:T(8,128)(2,1)} %bitcast.62), channel_id=1, source_target_pairs={{0,1},{1,2},{2,3},{3,0},{4,5},{5,6},{6,7},{7,4},{8,9},{9,10},{10,1... | collective-permute-start | bytes 1769480 | tf_op jit(solution)/shard_map/ppermute | solution.py:351
  54.5 1.7 %collective-permute-start.1 = (bf16[2,64,2304]{2,1,0:T(8,128)(2,1)}, bf16[2,64,2304]{2,1,0:T(8,128)(2,1)S(1)}, u32[]{:S(2)}, u32[]{:S(2)}) collective-permute-start(bf16[2,64,2304]{2,1,0:T(8,128)(2,1)} %bitcast.61), channel_id=1, source_target_pairs={{0,3},{1,0},{2,1},{3,2},{4,7},{5,4},{6,5},{7,6},{8,11},{9,8},{10,9... | collective-permute-start | bytes 1769480 | tf_op jit(solution)/shard_map/ppermute | solution.py:351
  56.1 0.5 collective-permute-start.2
  56.7 3.8 %convolution_convert_fusion = bf16[256,4608]{1,0:T(8,128)(2,1)S(1)} fusion(bf16[256,512]{1,0:T(8,128)(2,1)} %get-tuple-element.56, bf16[512,8192]{1,0:T(8,128)(2,1)} %weight.1), kind=kOutput, calls=%fused_computation | convolution fusion | flops 1209139200 | bytes 7340032 | tf_op jit(solution)/shard_map/dot_general | solution.py:438
  60.5 2.9 %convolution_convert_fusion.3 = bf16[256,2816]{1,0:T(8,128)(2,1)S(1)} fusion(bf16[256,512]{1,0:T(8,128)(2,1)S(1)} %copy-done.3, bf16[512,8192]{1,0:T(8,128)(2,1)} %weight.1), kind=kOutput, calls=%fused_computation.5 | convolution fusion | flops 738918400 | bytes 4587520 | tf_op jit(solution)/shard_map/dot_general | solution.py:438
  63.4 4.0 %collective-permute-done.2 = bf16[4,64,768]{2,1,0:T(8,128)(2,1)S(1)} collective-permute-done((bf16[4,64,768]{2,1,0:T(8,128)(2,1)}, bf16[4,64,768]{2,1,0:T(8,128)(2,1)S(1)}, u32[]{:S(2)}, u32[]{:S(2)}) %collective-permute-start.2) | collective-permute-done | bytes 393248 | tf_op jit(solution)/shard_map/ppermute | solution.py:354
  67.4 2.7 %collective-permute-done = bf16[2,64,2304]{2,1,0:T(8,128)(2,1)S(1)} collective-permute-done((bf16[2,64,2304]{2,1,0:T(8,128)(2,1)}, bf16[2,64,2304]{2,1,0:T(8,128)(2,1)S(1)}, u32[]{:S(2)}, u32[]{:S(2)}) %collective-permute-start) | collective-permute-done | bytes 589856 | tf_op jit(solution)/shard_map/ppermute | solution.py:351
  70.2 0.3 add_convert_fusion.2
  70.5 0.1 pad_maximum_fusion
  70.5 1.7 %collective-permute-start.3 = (bf16[2,64,4608]{2,1,0:T(8,128)(2,1)S(1)}, bf16[2,64,4608]{2,1,0:T(8,128)(2,1)S(1)}, u32[]{:S(2)}, u32[]{:S(2)}) collective-permute-start(bf16[2,64,4608]{2,1,0:T(8,128)(2,1)S(1)} %pad_maximum_fusion), channel_id=1, source_target_pairs={{0,1},{1,2},{2,3},{3,0},{4,5},{5,6},{6,7},{7,4},{8,9},{9,10},{10,1... | collective-permute-start | bytes 3538952 | tf_op jit(solution)/shard_map/ppermute | solution.py:351
  72.3 1.7 %collective-permute-start.4 = (bf16[2,64,4608]{2,1,0:T(8,128)(2,1)S(1)}, bf16[2,64,4608]{2,1,0:T(8,128)(2,1)S(1)}, u32[]{:S(2)}, u32[]{:S(2)}) collective-permute-start(bf16[2,64,4608]{2,1,0:T(8,128)(2,1)S(1)} %pad_maximum_fusion.1), channel_id=1, source_target_pairs={{0,3},{1,0},{2,1},{3,2},{4,7},{5,4},{6,5},{7,6},{8,11},{9,8},{10,9... | collective-permute-start | bytes 3538952 | tf_op jit(solution)/shard_map/ppermute | solution.py:351
  74.0 1.3 collective-permute-start.5
  75.3 0.4 convolution_convert_fusion.4
  75.7 0.1 fusion.4
  75.9 0.4 collective-permute-start.6
  76.3 2.9 %collective-permute-start.7 = (bf16[64,384]{1,0:T(8,128)(2,1)S(1)}, bf16[64,384]{1,0:T(8,128)(2,1)S(1)}, u32[]{:S(2)}, u32[]{:S(2)}) collective-permute-start(bf16[64,384]{1,0:T(8,128)(2,1)S(1)} %get-tuple-element.110), channel_id=1, source_target_pairs={{0,3},{1,0},{2,1},{3,2},{4,7},{5,4},{6,5},{7,6},{8,11},{9,8},{10,9... | collective-permute-start | bytes 147464 | tf_op jit(solution)/shard_map/ppermute | solution.py:351
  79.2 0.8 convolution_convert_fusion.1
  80.0 0.9 convolution_convert_fusion.2
  80.9 19.5 %collective-permute-done.6 = bf16[64,384]{1,0:T(8,128)(2,1)S(1)} collective-permute-done((bf16[64,384]{1,0:T(8,128)(2,1)S(1)}, bf16[64,384]{1,0:T(8,128)(2,1)S(1)}, u32[]{:S(2)}, u32[]{:S(2)}) %collective-permute-start.6) | collective-permute-done | bytes 49184 | tf_op jit(solution)/shard_map/ppermute | solution.py:351
  100.5 6.2 %collective-permute-done.5 = bf16[4,64,2816]{2,1,0:T(8,128)(2,1)S(1)} collective-permute-done((bf16[4,64,2816]{2,1,0:T(8,128)(2,1)S(1)}, bf16[4,64,2816]{2,1,0:T(8,128)(2,1)S(1)}, u32[]{:S(2)}, u32[]{:S(2)}) %collective-permute-start.5) | collective-permute-done | bytes 1441824 | tf_op jit(solution)/shard_map/ppermute | solution.py:354
  106.7 0.4 add_convert_fusion.1
  107.2 1.7 %collective-permute-start.8 = (bf16[64,1792]{1,0:T(8,128)(2,1)S(1)}, bf16[64,1792]{1,0:T(8,128)(2,1)S(1)}, u32[]{:S(2)}, u32[]{:S(2)}) collective-permute-start(bf16[64,1792]{1,0:T(8,128)(2,1)S(1)} %slice.150), channel_id=1, source_target_pairs={{0,4},{1,5},{2,6},{3,7},{4,0},{5,1},{6,2},{7,3},{8,12},{9,13},{10,... | collective-permute-start | bytes 688136 | tf_op jit(solution)/shard_map/ppermute | solution.py:354
  108.9 0.3 add_convert_fusion
  109.3 0.4 collective-permute-start.9
  109.8 2.9 %collective-permute-start.10 = (bf16[64,1408]{1,0:T(8,128)(2,1)S(1)}, bf16[64,1408]{1,0:T(8,128)(2,1)S(1)}, u32[]{:S(2)}, u32[]{:S(2)}) collective-permute-start(bf16[64,1408]{1,0:T(8,128)(2,1)S(1)} %get-tuple-element.108), channel_id=1, source_target_pairs={{0,3},{1,0},{2,1},{3,2},{4,7},{5,4},{6,5},{7,6},{8,11},{9,8},{10,9... | collective-permute-start | bytes 540680 | tf_op jit(solution)/shard_map/ppermute | solution.py:351
  112.7 0.1 collective-permute-start.11
  112.8 3.5 %collective-permute-start.12 = (bf16[64,768]{1,0:T(8,128)(2,1)S(1)}, bf16[64,768]{1,0:T(8,128)(2,1)S(1)}, u32[]{:S(2)}, u32[]{:S(2)}) collective-permute-start(bf16[64,768]{1,0:T(8,128)(2,1)S(1)} %pad_maximum_fusion.6), channel_id=1, source_target_pairs={{0,3},{1,0},{2,1},{3,2},{4,7},{5,4},{6,5},{7,6},{8,11},{9,8},{10,9... | collective-permute-start | bytes 294920 | tf_op jit(solution)/shard_map/ppermute | solution.py:351
  116.3 2.3 %collective-permute-done.11 = bf16[64,768]{1,0:T(8,128)(2,1)S(1)} collective-permute-done((bf16[64,768]{1,0:T(8,128)(2,1)S(1)}, bf16[64,768]{1,0:T(8,128)(2,1)S(1)}, u32[]{:S(2)}, u32[]{:S(2)}) %collective-permute-start.11) | collective-permute-done | bytes 98336 | tf_op jit(solution)/shard_map/ppermute | solution.py:351
  118.8 3.6 %collective-permute-start.15 = (bf16[64,2816]{1,0:T(8,128)(2,1)S(1)}, bf16[64,2816]{1,0:T(8,128)(2,1)S(1)}, u32[]{:S(2)}, u32[]{:S(2)}) collective-permute-start(bf16[64,2816]{1,0:T(8,128)(2,1)S(1)} %pad_maximum_fusion.4), channel_id=1, source_target_pairs={{0,3},{1,0},{2,1},{3,2},{4,7},{5,4},{6,5},{7,6},{8,11},{9,8},{10,9... | collective-permute-start | bytes 1081352 | tf_op jit(solution)/shard_map/ppermute | solution.py:351
  122.5 0.1 collective-permute-start.14
  122.6 0.1 slice_bitcast_fusion.2
  122.7 0.5 collective-permute-start.13
  123.3 7.2 %collective-permute-done.13 = bf16[64,2816]{1,0:T(8,128)(2,1)S(1)} collective-permute-done((bf16[64,2816]{1,0:T(8,128)(2,1)S(1)}, bf16[64,2816]{1,0:T(8,128)(2,1)S(1)}, u32[]{:S(2)}, u32[]{:S(2)}) %collective-permute-start.13) | collective-permute-done | bytes 360480 | tf_op jit(solution)/shard_map/ppermute | solution.py:354
  130.5 0.1 add_convert_fusion.4
  130.6 0.9 collective-permute-done.14
  131.5 0.1 fusion.7
  131.7 1.0 pad_maximum_fusion.2
  (46 shorter events, 0.8 us)
Async XLA Ops:
  2.3 23.1 %all-to-all-start = ((bf16[32,16,256]{2,1,0:T(8,128)(2,1)}), bf16[32,16,256]{2,1,0:T(8,128)(2,1)S(1)}, u32[]{:S(2)}, u32[]{:S(2)}) async-start(bf16[32,16,256]{2,1,0:T(8,128)(2,1)} %bitcast.52), calls=%async_computation | async-start | bytes 524288 | tf_op jit(solution)/shard_map/all_to_all | solution.py:365
  25.4 0.7 copy-start
  31.6 15.0 %all-to-all-start.1 = ((bf16[32,16,128]{2,1,0:T(8,128)(2,1)}), bf16[32,16,128]{2,1,0:T(8,128)(2,1)S(1)}, u32[]{:S(2)}, u32[]{:S(2)}) async-start(bf16[32,16,128]{2,1,0:T(8,128)(2,1)} %bitcast.55), calls=%async_computation.1 | async-start | bytes 262144 | tf_op jit(solution)/shard_map/all_to_all | solution.py:399
  46.6 0.6 copy-start.1
  52.8 17.2 %collective-permute-start = (bf16[2,64,2304]{2,1,0:T(8,128)(2,1)}, bf16[2,64,2304]{2,1,0:T(8,128)(2,1)S(1)}, u32[]{:S(2)}, u32[]{:S(2)}) collective-permute-start(bf16[2,64,2304]{2,1,0:T(8,128)(2,1)} %bitcast.62), channel_id=1, source_target_pairs={{0,1},{1,2},{2,3},{3,0},{4,5},{5,6},{6,7},{7,4},{8,9},{9,10},{10,1... | collective-permute-start | bytes 1769480 | tf_op jit(solution)/shard_map/ppermute | solution.py:351
  54.5 15.6 %collective-permute-start.1 = (bf16[2,64,2304]{2,1,0:T(8,128)(2,1)}, bf16[2,64,2304]{2,1,0:T(8,128)(2,1)S(1)}, u32[]{:S(2)}, u32[]{:S(2)}) collective-permute-start(bf16[2,64,2304]{2,1,0:T(8,128)(2,1)} %bitcast.61), channel_id=1, source_target_pairs={{0,3},{1,0},{2,1},{3,2},{4,7},{5,4},{6,5},{7,6},{8,11},{9,8},{10,9... | collective-permute-start | bytes 1769480 | tf_op jit(solution)/shard_map/ppermute | solution.py:351
  56.1 11.3 %collective-permute-start.2 = (bf16[4,64,768]{2,1,0:T(8,128)(2,1)}, bf16[4,64,768]{2,1,0:T(8,128)(2,1)S(1)}, u32[]{:S(2)}, u32[]{:S(2)}) collective-permute-start(bf16[4,64,768]{2,1,0:T(8,128)(2,1)} %bitcast.63), channel_id=1, source_target_pairs={{0,4},{1,5},{2,6},{3,7},{4,0},{5,1},{6,2},{7,3},{8,12},{9,13},{10,... | collective-permute-start | bytes 1179656 | tf_op jit(solution)/shard_map/ppermute | solution.py:354
  56.7 3.9 %copy-start.3 = (bf16[256,512]{1,0:T(8,128)(2,1)S(1)}, bf16[256,512]{1,0:T(8,128)(2,1)}, u32[]{:S(2)}) copy-start(bf16[256,512]{1,0:T(8,128)(2,1)} %get-tuple-element.60) | copy-start | bytes 786436
  60.5 14.8 %slice-start = ((s8[8388608]{0:T(1024)(128)(4,1)}), s8[4194304]{0:T(1024)(128)(4,1)S(1)}, s32[]{:S(2)}) async-start(s8[8388608]{0:T(1024)(128)(4,1)} %bitcast.46), calls=%async_computation.2 | async-start | bytes 8388608
  70.2 5.2 %slice-start.1 = ((s8[8388608]{0:T(1024)(128)(4,1)}), s8[4194304]{0:T(1024)(128)(4,1)S(1)}, s32[]{:S(2)}) async-start(s8[8388608]{0:T(1024)(128)(4,1)} %bitcast.46), calls=%async_computation.3 | async-start | bytes 8388608
  70.5 4.9 %copy-start.2 = (bf16[256,512]{1,0:T(8,128)(2,1)S(1)}, bf16[256,512]{1,0:T(8,128)(2,1)}, u32[]{:S(2)}) copy-start(bf16[256,512]{1,0:T(8,128)(2,1)} %get-tuple-element.81) | copy-start | bytes 786436
  70.5 29.9 %collective-permute-start.3 = (bf16[2,64,4608]{2,1,0:T(8,128)(2,1)S(1)}, bf16[2,64,4608]{2,1,0:T(8,128)(2,1)S(1)}, u32[]{:S(2)}, u32[]{:S(2)}) collective-permute-start(bf16[2,64,4608]{2,1,0:T(8,128)(2,1)S(1)} %pad_maximum_fusion), channel_id=1, source_target_pairs={{0,1},{1,2},{2,3},{3,0},{4,5},{5,6},{6,7},{7,4},{8,9},{9,10},{10,1... | collective-permute-start | bytes 3538952 | tf_op jit(solution)/shard_map/ppermute | solution.py:351
  72.3 6.9 %copy-start.4 = (bf16[128,512]{1,0:T(8,128)(2,1)S(1)}, bf16[128,512]{1,0:T(8,128)(2,1)}, u32[]{:S(2)}) copy-start(bf16[128,512]{1,0:T(8,128)(2,1)} %get-tuple-element.78) | copy-start | bytes 393220
  72.3 28.2 %collective-permute-start.4 = (bf16[2,64,4608]{2,1,0:T(8,128)(2,1)S(1)}, bf16[2,64,4608]{2,1,0:T(8,128)(2,1)S(1)}, u32[]{:S(2)}, u32[]{:S(2)}) collective-permute-start(bf16[2,64,4608]{2,1,0:T(8,128)(2,1)S(1)} %pad_maximum_fusion.1), channel_id=1, source_target_pairs={{0,3},{1,0},{2,1},{3,2},{4,7},{5,4},{6,5},{7,6},{8,11},{9,8},{10,9... | collective-permute-start | bytes 3538952 | tf_op jit(solution)/shard_map/ppermute | solution.py:351
  74.0 32.6 %collective-permute-start.5 = (bf16[4,64,2816]{2,1,0:T(8,128)(2,1)S(1)}, bf16[4,64,2816]{2,1,0:T(8,128)(2,1)S(1)}, u32[]{:S(2)}, u32[]{:S(2)}) collective-permute-start(bf16[4,64,2816]{2,1,0:T(8,128)(2,1)S(1)} %bitcast.60), channel_id=1, source_target_pairs={{0,4},{1,5},{2,6},{3,7},{4,0},{5,1},{6,2},{7,3},{8,12},{9,13},{10,... | collective-permute-start | bytes 4325384 | tf_op jit(solution)/shard_map/ppermute | solution.py:354
  75.9 24.6 %collective-permute-start.6 = (bf16[64,384]{1,0:T(8,128)(2,1)S(1)}, bf16[64,384]{1,0:T(8,128)(2,1)S(1)}, u32[]{:S(2)}, u32[]{:S(2)}) collective-permute-start(bf16[64,384]{1,0:T(8,128)(2,1)S(1)} %get-tuple-element.111), channel_id=1, source_target_pairs={{0,1},{1,2},{2,3},{3,0},{4,5},{5,6},{6,7},{7,4},{8,9},{9,10},{10,1... | collective-permute-start | bytes 147464 | tf_op jit(solution)/shard_map/ppermute | solution.py:351
  76.3 24.2 %collective-permute-start.7 = (bf16[64,384]{1,0:T(8,128)(2,1)S(1)}, bf16[64,384]{1,0:T(8,128)(2,1)S(1)}, u32[]{:S(2)}, u32[]{:S(2)}) collective-permute-start(bf16[64,384]{1,0:T(8,128)(2,1)S(1)} %get-tuple-element.110), channel_id=1, source_target_pairs={{0,3},{1,0},{2,1},{3,2},{4,7},{5,4},{6,5},{7,6},{8,11},{9,8},{10,9... | collective-permute-start | bytes 147464 | tf_op jit(solution)/shard_map/ppermute | solution.py:351
  107.2 11.4 %collective-permute-start.8 = (bf16[64,1792]{1,0:T(8,128)(2,1)S(1)}, bf16[64,1792]{1,0:T(8,128)(2,1)S(1)}, u32[]{:S(2)}, u32[]{:S(2)}) collective-permute-start(bf16[64,1792]{1,0:T(8,128)(2,1)S(1)} %slice.150), channel_id=1, source_target_pairs={{0,4},{1,5},{2,6},{3,7},{4,0},{5,1},{6,2},{7,3},{8,12},{9,13},{10,... | collective-permute-start | bytes 688136 | tf_op jit(solution)/shard_map/ppermute | solution.py:354
  109.3 9.3 %collective-permute-start.9 = (bf16[64,1408]{1,0:T(8,128)(2,1)S(1)}, bf16[64,1408]{1,0:T(8,128)(2,1)S(1)}, u32[]{:S(2)}, u32[]{:S(2)}) collective-permute-start(bf16[64,1408]{1,0:T(8,128)(2,1)S(1)} %get-tuple-element.109), channel_id=1, source_target_pairs={{0,1},{1,2},{2,3},{3,0},{4,5},{5,6},{6,7},{7,4},{8,9},{9,10},{10,1... | collective-permute-start | bytes 540680 | tf_op jit(solution)/shard_map/ppermute | solution.py:351
  109.8 8.8 %collective-permute-start.10 = (bf16[64,1408]{1,0:T(8,128)(2,1)S(1)}, bf16[64,1408]{1,0:T(8,128)(2,1)S(1)}, u32[]{:S(2)}, u32[]{:S(2)}) collective-permute-start(bf16[64,1408]{1,0:T(8,128)(2,1)S(1)} %get-tuple-element.108), channel_id=1, source_target_pairs={{0,3},{1,0},{2,1},{3,2},{4,7},{5,4},{6,5},{7,6},{8,11},{9,8},{10,9... | collective-permute-start | bytes 540680 | tf_op jit(solution)/shard_map/ppermute | solution.py:351
  112.7 5.9 %collective-permute-start.11 = (bf16[64,768]{1,0:T(8,128)(2,1)S(1)}, bf16[64,768]{1,0:T(8,128)(2,1)S(1)}, u32[]{:S(2)}, u32[]{:S(2)}) collective-permute-start(bf16[64,768]{1,0:T(8,128)(2,1)S(1)} %pad_maximum_fusion.5), channel_id=1, source_target_pairs={{0,1},{1,2},{2,3},{3,0},{4,5},{5,6},{6,7},{7,4},{8,9},{9,10},{10,1... | collective-permute-start | bytes 294920 | tf_op jit(solution)/shard_map/ppermute | solution.py:351
  112.8 5.8 %collective-permute-start.12 = (bf16[64,768]{1,0:T(8,128)(2,1)S(1)}, bf16[64,768]{1,0:T(8,128)(2,1)S(1)}, u32[]{:S(2)}, u32[]{:S(2)}) collective-permute-start(bf16[64,768]{1,0:T(8,128)(2,1)S(1)} %pad_maximum_fusion.6), channel_id=1, source_target_pairs={{0,3},{1,0},{2,1},{3,2},{4,7},{5,4},{6,5},{7,6},{8,11},{9,8},{10,9... | collective-permute-start | bytes 294920 | tf_op jit(solution)/shard_map/ppermute | solution.py:351
  118.8 11.8 %collective-permute-start.15 = (bf16[64,2816]{1,0:T(8,128)(2,1)S(1)}, bf16[64,2816]{1,0:T(8,128)(2,1)S(1)}, u32[]{:S(2)}, u32[]{:S(2)}) collective-permute-start(bf16[64,2816]{1,0:T(8,128)(2,1)S(1)} %pad_maximum_fusion.4), channel_id=1, source_target_pairs={{0,3},{1,0},{2,1},{3,2},{4,7},{5,4},{6,5},{7,6},{8,11},{9,8},{10,9... | collective-permute-start | bytes 1081352 | tf_op jit(solution)/shard_map/ppermute | solution.py:351
  122.5 9.0 %collective-permute-start.14 = (bf16[64,2816]{1,0:T(8,128)(2,1)S(1)}, bf16[64,2816]{1,0:T(8,128)(2,1)S(1)}, u32[]{:S(2)}, u32[]{:S(2)}) collective-permute-start(bf16[64,2816]{1,0:T(8,128)(2,1)S(1)} %pad_maximum_fusion.3), channel_id=1, source_target_pairs={{0,1},{1,2},{2,3},{3,0},{4,5},{5,6},{6,7},{7,4},{8,9},{9,10},{10,1... | collective-permute-start | bytes 1081352 | tf_op jit(solution)/shard_map/ppermute | solution.py:351
  122.7 7.8 %collective-permute-start.13 = (bf16[64,2816]{1,0:T(8,128)(2,1)S(1)}, bf16[64,2816]{1,0:T(8,128)(2,1)S(1)}, u32[]{:S(2)}, u32[]{:S(2)}) collective-permute-start(bf16[64,2816]{1,0:T(8,128)(2,1)S(1)} %slice.162), channel_id=1, source_target_pairs={{0,4},{1,5},{2,6},{3,7},{4,0},{5,1},{6,2},{7,3},{8,12},{9,13},{10,... | collective-permute-start | bytes 1081352 | tf_op jit(solution)/shard_map/ppermute | solution.py:354

commit v3 on v2

v3 whole, which is shorter than its diff:
```python
import functools
import math

import jax
import jax.numpy as jnp
from jax import lax
from jax.experimental import pallas as pl
from jax.experimental.pallas import tpu as pltpu
from jax.sharding import PartitionSpec as P

HD = 128
POS = 4
PREF = 24
HEADS = 4
NEG = -1e30
COLS_Y = 4608
PIECE = 256
EARLY = 1024
FIRST = 5
LIMIT = 54
LESS = 52
SCALE2 = math.log2(math.e) / math.sqrt(HD)
BF = jnp.bfloat16
F32 = jnp.float32


def nt_dot(a, b):
    return lax.dot_general(a, b, (((1,), (1,)), ((), ())), preferred_element_type=F32)


def nn_dot(a, b):
    return jnp.dot(a, b, preferred_element_type=F32)


def soft_mix(pieces):
    top = functools.reduce(
        jnp.maximum, [jnp.max(s, axis=-1, keepdims=True) for s, _ in pieces]
    )
    total = 0.0
    mixed = 0.0
    for s, v in pieces:
        p = jnp.exp2((s - top) * SCALE2)
        total = total + jnp.sum(p, axis=-1, keepdims=True)
        mixed = mixed + nn_dot(p.astype(BF), v)
    return (mixed / total).astype(BF)


def wanted_rows(table, group, half, decode_rows):
    slots = half * HEADS * POS
    peer = lax.rem(group, half)
    slot = lax.broadcasted_iota(jnp.int32, (slots, half * half), 0)
    request = lax.broadcasted_iota(jnp.int32, (slots, half * half), 1)
    row = table[...]
    mine = jnp.logical_and(
        request // half == slot // (HEADS * POS), row // decode_rows == peer
    )
    first = jnp.sum(jnp.where(mine, lax.rem(row, decode_rows) * POS, 0), axis=1, keepdims=True)
    return first + lax.rem(lax.broadcasted_iota(jnp.int32, (slots, 1), 0), POS)


def load(pairs, sems):
    copies = [pltpu.make_async_copy(a, b, sems.at[n]) for n, (a, b) in enumerate(pairs)]
    for copy in copies:
        copy.start()
    return copies


def pick_kernel(table, all_q, all_f, out, queries, fresh, sems, *, half, decode_rows):
    copies = load([(all_q, queries), (all_f, fresh)], sems)
    rows = queries.shape[0]
    slots = half * HEADS * POS
    want = wanted_rows(table, lax.axis_index("group"), half, decode_rows)
    pick = (want == lax.broadcasted_iota(jnp.int32, (slots, rows), 1)).astype(F32).astype(BF)
    head = lax.rem(lax.broadcasted_iota(jnp.int32, (slots, HD), 0) // POS, HEADS)
    for copy in copies:
        copy.wait()
    got_q = nn_dot(pick, queries[...])
    got_f = nn_dot(pick, fresh[...])
    one_q = got_q[:, 0:HD]
    for h in range(1, HEADS):
        one_q = jnp.where(head == h, got_q[:, h * HD : (h + 1) * HD], one_q)
    one_f = jnp.where(head == 0, got_f[:, 0:HD], got_f[:, HD : 2 * HD])
    one_f = jnp.where(head < 2, one_f, 0.0)
    for n in range(2):
        out[n * slots : (n + 1) * slots, 0:HD] = one_q.astype(BF)
        out[n * slots : (n + 1) * slots, HD : 2 * HD] = one_f.astype(BF)


def stacked(ref, row, span):
    return jnp.concatenate(
        [ref[pl.ds(row, span), h * HD : (h + 1) * HD] for h in range(HEADS)], axis=0
    )


def fresh_mask(span):
    row = lax.rem(lax.broadcasted_iota(jnp.int32, (span * HEADS, span), 0), span)
    col = lax.broadcasted_iota(jnp.int32, (span * HEADS, span), 1)
    return jnp.logical_and(col // POS == row // POS, col <= row)


def local_kernel(
    prefix_len, resident_len, *refs, half, decode_rows, part, cut
):
    if part == 0:
        table, pages, all_q, all_f, pool, out, gathered, *scratch = refs
    else:
        all_q, all_f, pool, out, *scratch = refs
    queries, fresh, held, io_sems, sems, *more = scratch
    copies = load([(all_q, queries), (all_f, fresh)], io_sems)

    group = lax.axis_index("group")
    peer = lax.rem(group, half)
    rows = queries.shape[0]
    begin, end = (0, cut) if part == 0 else (cut, rows)
    pool_pages, page_len, _ = pool.shape
    each = 8
    parts = pool_pages // each

    def fetch(n):
        return pltpu.make_async_copy(
            pool.at[pl.ds(n * each, each)], held.at[pl.ds(n * each, each)], sems.at[n]
        )

    def side_copies():
        if part == 1:
            return []
        most = pages.shape[0]
        return [
            pltpu.make_async_copy(
                pool.at[pages[n, more[1][d]]], gathered.at[d * most + n], more[0].at[d, n]
            )
            for d in range(half)
            for n in range(most)
        ]

    @pl.when(group < half)
    def _():
        prefix_tokens = PREF * page_len
        for n in range(PREF // each):
            fetch(n).start()
        if part == 0:
            for i in range(half):
                more[1][table[group * half + i] // decode_rows] = group * half + i
        for copy in side_copies():
            copy.start()
        for copy in copies:
            copy.wait()
        for n in range(PREF // each):
            fetch(n).wait()
        prefix = prefix_len[peer]
        span = 64
        stack = span * HEADS
        ok_p = lax.broadcasted_iota(jnp.int32, (1, prefix_tokens), 1) < prefix
        row_id = lax.rem(lax.broadcasted_iota(jnp.int32, (stack, rows), 0), span)
        ahead = lax.broadcasted_iota(jnp.int32, (stack, rows), 1) - row_id

        def chunk(i, carry):
            row = pl.multiple_of(i * span, span)
            q = stacked(queries, row, span)
            key_p = held[0:PREF, :, 0:HD].reshape(prefix_tokens, HD)
            val_p = held[0:PREF, :, HD : 2 * HD].reshape(prefix_tokens, HD)
            s_p = jnp.where(ok_p, nt_dot(q, key_p), NEG)
            s_f = jnp.where(ahead <= row, nt_dot(q, fresh[:, 0:HD]), NEG)
            o = soft_mix([(s_p, val_p), (s_f, fresh[:, HD : 2 * HD])])
            for h in range(HEADS):
                out[pl.ds(row - begin, span), h * HD : (h + 1) * HD] = o[h * span : (h + 1) * span]
            return carry

        lax.fori_loop(begin // span, end // span, chunk, 0)
        for copy in side_copies():
            copy.wait()

    @pl.when(group >= half)
    def _():
        span = each * POS
        if part == 1:
            fetch(0).start()
        for n in range(begin // span, min(end // span, parts)):
            fetch(n).start()
        if part == 1:
            fetch(0).wait()
        for copy in copies:
            copy.wait()
        stack = span * HEADS
        width = each * page_len
        row_id = lax.rem(lax.broadcasted_iota(jnp.int32, (stack, width), 0), span) // POS
        col = lax.broadcasted_iota(jnp.int32, (stack, width), 1)
        same = col // page_len == row_id
        slot = lax.broadcasted_iota(jnp.int32, (1, width), 1)
        f_ok = fresh_mask(span)

        def chunk(i, carry):
            @pl.when(i < parts)
            def _():
                fetch(i).wait()

            row = pl.multiple_of(i * span, span)
            first = lax.rem(i, parts) * each
            q = stacked(queries, row, span)
            key_r = held[pl.ds(first, each), :, 0:HD].reshape(width, HD)
            val_r = held[pl.ds(first, each), :, HD : 2 * HD].reshape(width, HD)
            length = jnp.zeros((1, width), jnp.int32)
            for e in range(each):
                length = jnp.where(
                    slot // page_len == e, resident_len[peer * decode_rows + i * each + e], length
                )
            seen = lax.rem(slot, page_len) < length
            s_r = jnp.where(jnp.logical_and(same, seen), nt_dot(q, key_r), NEG)
            s_f = jnp.where(f_ok, nt_dot(q, fresh[pl.ds(row, span), 0:HD]), NEG)
            o = soft_mix([(s_r, val_r), (s_f, fresh[pl.ds(row, span), HD : 2 * HD])])
            for h in range(HEADS):
                out[pl.ds(row - begin, span), h * HD : (h + 1) * HD] = o[h * span : (h + 1) * span]
            return carry

        lax.fori_loop(begin // span, end // span, chunk, 0)


def handed_kernel(table, lengths, all_pages, sent, out, slots, pool, sems, *, half, decode_rows, most):
    group = lax.axis_index("group")
    page_len = pool.shape[1]
    each = 4
    stack = HEADS * POS
    span = each * stack
    width = each * most * page_len

    @pl.when(group >= half)
    def _():
        out[...] = jnp.zeros_like(out)

    @pl.when(group < half)
    def _():
        def fetch(b):
            at = pl.ds(b * each * most, each * most)
            return pltpu.make_async_copy(all_pages.at[at], pool.at[at], sems.at[b])

        for b in range(half // each):
            fetch(b).start()
        for i in range(half):
            slots[table[group * half + i] // decode_rows] = group * half + i
        row_id = lax.broadcasted_iota(jnp.int32, (span, width), 0) // stack
        col = lax.broadcasted_iota(jnp.int32, (span, width), 1)
        same = col // (most * page_len) == row_id
        slot = lax.broadcasted_iota(jnp.int32, (1, width), 1)
        f_row = lax.broadcasted_iota(jnp.int32, (span, span), 0)
        f_col = lax.broadcasted_iota(jnp.int32, (span, span), 1)
        f_ok = jnp.logical_and(
            f_row // stack == f_col // stack, lax.rem(f_col, stack) <= lax.rem(f_row, POS)
        )
        for b in range(half // each):
            length = jnp.zeros((1, width), jnp.int32)
            for e in range(each):
                request = slots[b * each + e]
                length = jnp.where(slot // (most * page_len) == e, lengths[request], length)
            seen = lax.rem(slot, most * page_len) < length
            new = sent[(half // each + b) * span : (half // each + b + 1) * span, :]
            q = new[:, 0:HD]
            key_n = new[:, HD : 2 * HD]
            val_n = pltpu.roll(key_n.astype(F32), span - POS, 0).astype(BF)
            fetch(b).wait()
            own = slice(b * each * most, (b + 1) * each * most)
            key_c = pool[own, :, 0:HD].reshape(width, HD)
            val_c = pool[own, :, HD : 2 * HD].reshape(width, HD)
            s_c = jnp.where(jnp.logical_and(same, seen), nt_dot(q, key_c), NEG)
            s_n = jnp.where(f_ok, nt_dot(q, key_n), NEG)
            o = soft_mix([(s_c, val_c), (s_n, val_n)])
            for n in range(2):
                out[(n * half // each + b) * span : (n * half // each + b + 1) * span, :] = o


def front_kernel(
    table, first, second, back, weight, z_out, r_out, l_out, x_near, x_far, x13, x0, *scratch, half, decode_rows
):
    whole, held, sems, z_part, y_r, y_l, out_sems = scratch
    group = lax.axis_index("group")
    tp = lax.axis_index("tp")
    my_y, my_z = lax.rem(tp, 4), tp // 4
    cut = first.shape[0]
    rows = whole.shape[0]
    slots = half * HEADS * POS
    count, _, part = held.shape
    mid = y_r.shape[1] // part
    z_count = count - 2 * mid

    def fetch(n):
        begin = (2 * mid + n if n < z_count else n - z_count) * part
        return pltpu.make_async_copy(
            weight.at[:, pl.ds(begin, part)], held.at[n], sems.at[n]
        )

    for n in range(count):
        fetch(n).start()
    whole[0:cut] = first[...]
    whole[cut:] = second[...]

    @pl.when(group >= half)
    def _():
        want = wanted_rows(table, group, half, decode_rows)
        here = lax.broadcasted_iota(jnp.int32, (slots, rows), 1)
        put = (want == here).astype(F32).astype(BF)
        head = lax.rem(lax.broadcasted_iota(jnp.int32, (slots, HD), 0) // POS, HEADS)
        came = back[0:slots, :].astype(F32)

        def spread(x):
            return lax.dot_general(put, x, (((0,), (0,)), ((), ())), preferred_element_type=F32)

        hit = spread(jnp.ones((slots, HD), BF)) > 0.5
        for h in range(HEADS):
            at = slice(h * HD, (h + 1) * HD)
            moved = spread(jnp.where(head == h, came, 0.0).astype(BF))
            whole[:, at] = jnp.where(hit, moved, whole[:, at].astype(F32)).astype(BF)

    share = 64

    def block(dist, far):
        dest = (my_z + far - 2 * my_z * far) * 4 + lax.rem(my_y + dist, 4)
        return whole[pl.ds(pl.multiple_of(dest * share, share), share), :]

    for dist in range(4):
        x_near[dist * share : (dist + 1) * share] = block(dist, 0)
        x_far[dist * share : (dist + 1) * share] = block(dist, 1)
    for n, dist in enumerate((1, 3)):
        for far in range(2):
            x13[(2 * n + far) * share : (2 * n + far + 1) * share] = block(dist, far)
    for far in range(2):
        x0[far * share : (far + 1) * share] = block(0, far)
    x2 = jnp.concatenate([block(2, 0), block(2, 1)], axis=0)
    copies = []
    for x, begin, held_out, out in (
        (x_far[...], 0, z_part, z_out),
        (x2, z_count, y_r, r_out),
        (x2, z_count + mid, y_l, l_out),
    ):
        for n in range(held_out.shape[1] // part):
            fetch(begin + n).wait()
            held_out[:, n * part : (n + 1) * part] = nn_dot(x, held[begin + n]).astype(BF)
        copies.append(pltpu.make_async_copy(held_out, out, out_sems.at[len(copies)]))
        copies[-1].start()
    for copy in copies:
        copy.wait()


def add(*terms):
    total = terms[0].astype(F32)
    for term in terms[1:]:
        total = total + term.astype(F32)
    return total.astype(BF)


def on_device(
    queries,
    fresh_kv,
    page_pool,
    out_weight,
    request_row,
    request_len,
    request_pages,
    resident_len,
    prefix_len,
):
    half = lax.axis_size("group") // 2
    tp_count = lax.axis_size("tp")
    rows, wide = queries.shape
    kv_wide = fresh_kv.shape[1]
    pool_pages, page_len, _ = page_pool.shape
    most = request_pages.shape[1]
    decode_rows = rows // POS
    slots = half * HEADS * POS
    smem = pl.BlockSpec(memory_space=pltpu.SMEM)
    vmem = pl.BlockSpec(memory_space=pltpu.VMEM)
    hbm = pl.BlockSpec(memory_space=pltpu.HBM)
    params = pltpu.CompilerParams(vmem_limit_bytes=LIMIT * 1024 * 1024)
    less = pltpu.CompilerParams(vmem_limit_bytes=LESS * 1024 * 1024)
    dma = pltpu.SemaphoreType.DMA
    inputs = [pltpu.VMEM(queries.shape, BF), pltpu.VMEM(fresh_kv.shape, BF)]

    def made(*shape):
        return jax.ShapeDtypeStruct(shape, BF)

    def y_step(x, step):
        return lax.ppermute(x, "tp", [(t, t // 4 * 4 + (t + step) % 4) for t in range(tp_count)])

    def z_swap(x):
        return lax.ppermute(x, "tp", [(t, (t + 4) % tp_count) for t in range(tp_count)])

    table = request_row.reshape(1, half * half)
    parcel = pl.pallas_call(
        functools.partial(pick_kernel, half=half, decode_rows=decode_rows),
        out_shape=made(2 * slots, kv_wide),
        in_specs=[vmem, hbm, hbm],
        out_specs=vmem,
        scratch_shapes=[*inputs, dma((2,))],
        compiler_params=params,
        name="pick_rows",
    )(table, queries, fresh_kv)
    sent = lax.all_to_all(parcel, "group", split_axis=0, concat_axis=0, tiled=True)

    cut = FIRST * rows // 8
    by_name = request_pages.T

    def attend(part, given, specs, extra, extra_specs, scratch):
        return pl.pallas_call(
            functools.partial(
                local_kernel, half=half, decode_rows=decode_rows, part=part, cut=cut
            ),
            out_shape=[made(cut if part == 0 else rows - cut, wide), *extra],
            in_specs=[smem, smem, *specs],
            out_specs=[vmem, *extra_specs],
            scratch_shapes=[
                *inputs,
                pltpu.VMEM(page_pool.shape, BF),
                dma((2,)),
                dma((pool_pages // 8,)),
                *scratch,
            ],
            compiler_params=params,
            cost_estimate=pl.CostEstimate(
                flops=8 * 2048 * 2048 * 128, bytes_accessed=5 << 20, transcendentals=1 << 21
            ),
            name="local_attention",
        )(prefix_len, resident_len, *given)

    first, gathered = attend(
        0,
        (request_row, by_name, queries, fresh_kv, page_pool),
        [smem, smem, hbm, hbm, hbm],
        [made(half * most, page_len, kv_wide)],
        [vmem],
        [dma((half, most)), pltpu.SMEM((half,), jnp.int32)],
    )
    sent, first = lax.optimization_barrier((sent, first))
    handed = pl.pallas_call(
        functools.partial(handed_kernel, half=half, decode_rows=decode_rows, most=most),
        out_shape=made(2 * slots, HD),
        in_specs=[smem, smem, hbm, vmem],
        out_specs=vmem,
        scratch_shapes=[
            pltpu.SMEM((half,), jnp.int32),
            pltpu.VMEM((half * most, page_len, kv_wide), BF),
            dma((4,)),
        ],
        compiler_params=less,
        name="handed_attention",
    )(request_row, request_len, gathered, sent)
    back = lax.all_to_all(handed, "group", split_axis=0, concat_axis=0, tiled=True)
    (second,) = attend(1, (queries, fresh_kv, page_pool), [hbm, hbm, hbm], [], [], [])
    share = rows // tp_count
    pieces = (COLS_Y + EARLY) // PIECE
    sizes = [(4 * share, EARLY), (2 * share, COLS_Y // 2), (2 * share, COLS_Y // 2)]
    z1_a, y2_r, y2_l, x_near, x_far, x13, x0 = pl.pallas_call(
        functools.partial(front_kernel, half=half, decode_rows=decode_rows),
        out_shape=[
            *(made(*size) for size in sizes),
            made(4 * share, wide),
            made(4 * share, wide),
            made(4 * share, wide),
            made(2 * share, wide),
        ],
        in_specs=[vmem] * 4 + [hbm],
        out_specs=[hbm] * 3 + [vmem] * 4,
        scratch_shapes=[
            pltpu.VMEM((rows, wide), BF),
            pltpu.VMEM((pieces, wide, PIECE), BF),
            dma((pieces,)),
            *(pltpu.VMEM(size, BF) for size in sizes),
            dma((3,)),
        ],
        compiler_params=less,
        name="front_products",
    )(table, first, second, back, out_weight)

    def blocks(x):
        return x.reshape(-1, share, x.shape[1])

    cuts = {"y": (0, COLS_Y), "b": (COLS_Y + EARLY, None), "z": (COLS_Y, None)}

    def products(given, names):
        parts = []
        for name in names:
            begin, end = cuts[name[0]]
            weight = out_weight[:, begin:end]
            part = jnp.dot(given[name], weight, preferred_element_type=F32).astype(BF)
            part, given = lax.optimization_barrier((part, given))
            parts.append(blocks(part))
        return parts, given

    def start_far(far):
        mid = far.shape[-1] // 2
        return y_step(far[..., :mid], 1), y_step(far[..., mid:], -1)

    def start_near(next_r, next_l, far_r, far_l):
        mid = far_r.shape[-1]
        right = jnp.concatenate([add(next_r[..., :mid], far_r), next_r[..., mid:]], -1)
        left = jnp.concatenate([next_l[..., :mid], add(next_l[..., mid:], far_l)], -1)
        return y_step(right, 1), y_step(left, -1)

    come_a = z_swap(blocks(z1_a))
    far_y = y_step(blocks(y2_r), 1), y_step(blocks(y2_l), -1)
    given = {"y13": x13, "b1": x_far, "y0": x0, "z0": x_near}
    (y13, z1_b), given = products(given, ("y13", "b1"))
    far_y, come_a, z1_b, given, y13 = lax.optimization_barrier((far_y, come_a, z1_b, given, y13))
    come_b = z_swap(z1_b)
    near_y = start_near(y13[0:2], y13[2:4], *far_y)
    (y0, z0), given = products(given, ("y0", "z0"))
    near_y, come_b, y0, z0 = lax.optimization_barrier((near_y, come_b, y0, z0))
    mine_y = add(y0, *near_y)
    come_y = z_swap(mine_y[1])
    mine_z = add(z0, jnp.concatenate([come_a, come_b], axis=-1))
    far_z = start_far(mine_z[2])
    near_z = start_near(mine_z[1], mine_z[3], *far_z)
    return jnp.concatenate([add(mine_y[0], come_y), add(mine_z[0], *near_z)], axis=-1)


def solution(mesh):
    in_specs = (
        P("group", "tp"),
        P("group", "tp"),
        P("group", None, "tp"),
        P("tp", None),
        P(),
        P(),
        P(),
        P(),
        P(),
    )
    out_specs = P(("group", "tp"), None)
    return jax.shard_map(
        on_device, mesh=mesh, in_specs=in_specs, out_specs=out_specs, check_vma=False
    )
```

time: 133 us -> 132 us (level)
  starting transfers between devices: 42 us -> 34.7 us
  Pallas kernels: 28.7 us -> 33.4 us
  waiting for transfers between devices: 48.2 us -> 50.3 us
    ppermute x12 -> x8, waiting for transfers between devices: 25.4 us -> 36.7 us  [y_step(): lax.ppermute(x, 'tp', [(t, t // 4 * 4 + (t + step) % 4) for t in range(tp...]
    ppermute x12 -> x8, starting transfers between devices: 20.7 us -> 13.2 us  [y_step(): lax.ppermute(x, 'tp', [(t, t // 4 * 4 + (t + step) % 4) for t in range(tp...]
    ppermute x4 -> x3, waiting for transfers between devices: 17.4 us -> 10.9 us  [z_swap(): lax.ppermute(x, 'tp', [(t, (t + 4) % tp_count) for t in range(tp_count)])]
    all_to_all x1, waiting for transfers between devices: 3.8 us -> 0.01 us  [on_device(): lax.all_to_all(parcel, 'group', split_axis=0, concat_axis=0, tiled=True)]
    pallas_call x2, Pallas kernels: 15.3 us -> 18.6 us  [attend(): pl.pallas_call(functools.partial(local_kernel, half=half, decode_rows=dec...]
    pallas_call x1, Pallas kernels: 5.57 us -> 7.11 us  [on_device(): pl.pallas_call(functools.partial(front_kernel, half=half, decode_rows=dec...]
    ppermute x4 -> x3, starting transfers between devices: 4.01 us -> 3.05 us  [z_swap(): lax.ppermute(x, 'tp', [(t, (t + 4) % tp_count) for t in range(tp_count)])]
    dot_general x5 -> x4, matrix products: 8.81 us -> 8.49 us  [products(): part = jnp.dot(given[name], weight, preferred_element_type=F32).astype(BF)]
  transfers between devices with their start and end apart: 18 -> 13, of which waited for: 9 -> 11; matrix products, arithmetic and copies ran while one was open for 7% -> 7% of each run, Pallas kernels for 12% -> 14%
where the time goes in v3:
time: 132 us; the launch traced here: 131 us
  waiting for transfers between devices  50.3 us (38%)
  starting transfers between devices  34.7 us (26%)
  Pallas kernels  33.4 us (25%)
  matrix products  8.49 us (6%)
  other arithmetic  2.89 us (2%)
    ppermute x8, waiting for transfers between devices, y_step(): lax.ppermute(x, 'tp', [(t, t // 4 * 4 + (t + step) % 4) for t in range(tp...  36.7 us
    pallas_call x2, Pallas kernels, attend(): pl.pallas_call(functools.partial(local_kernel, half=half, decode_rows=dec...  18.6 us
    ppermute x8, starting transfers between devices, y_step(): lax.ppermute(x, 'tp', [(t, t // 4 * 4 + (t + step) % 4) for t in range(tp...  13.2 us
    all_to_all x1, starting transfers between devices, on_device(): lax.all_to_all(parcel, 'group', split_axis=0, concat_axis=0, tiled=True)  11.6 us
    ppermute x3, waiting for transfers between devices, z_swap(): lax.ppermute(x, 'tp', [(t, (t + 4) % tp_count) for t in range(tp_count)])  10.9 us
    dot_general x4, matrix products, products(): part = jnp.dot(given[name], weight, preferred_element_type=F32).astype(BF)  8.49 us
    pallas_call x1, Pallas kernels, on_device(): pl.pallas_call(functools.partial(front_kernel, half=half, decode_rows=dec...  7.11 us
    all_to_all x1, starting transfers between devices, on_device(): lax.all_to_all(handed, 'group', split_axis=0, concat_axis=0, tiled=True)  6.78 us
  transfers between devices with their start and end apart: 13, of which 11 were waited for; matrix products, arithmetic and copies ran while one was open for 7% of the time, Pallas kernels for 14%

profile of v3, /device:TPU:2, one launch (start us, length us, event | category | flops | bytes accessed | tf_op | source)
XLA Modules:
  0.0 131.2 jit_solution(7192342823717222117)
XLA Ops:
  0.0 2.9 %pick_rows.1 = bf16[512,256]{1,0:T(8,128)(2,1)} custom-call(s32[1,256]{1,0:T(1,128)} %bitcast.37, bf16[512,512]{1,0:T(8,128)(2,1)} %refs_0_.3, bf16[512,256]{1,0:T(8,128)(2,1)} %refs_1_.1), custom_call_target="tpu_custom_call" | custom-call | tf_op jit(solution)/shard_map/pick_rows/pallas_call | solution.py:386
  2.9 11.6 %all-to-all-start = ((bf16[32,16,256]{2,1,0:T(8,128)(2,1)}), bf16[32,16,256]{2,1,0:T(8,128)(2,1)S(1)}, u32[]{:S(2)}, u32[]{:S(2)}) async-start(bf16[32,16,256]{2,1,0:T(8,128)(2,1)} %bitcast.45), calls=%async_computation | async-start | bytes 524288 | tf_op jit(solution)/shard_map/all_to_all | solution.py:395
  14.6 12.1 %local_attention.2 = (bf16[320,512]{1,0:T(8,128)(2,1)}, bf16[96,64,256]{2,1,0:T(8,128)(2,1)}) custom-call(s32[16]{0:T(128)} %prefix_len.3, s32[2048]{0:T(1024)} %resident_len.3, s32[256]{0:T(256)} %table.1, s32[6,256]{1,0:T(8,128)} %bitcast.50, bf16[512,512]{1,0:T(8,128)(2,1)} %refs_0_.3, bf16[512,256]{1,0:T(8,128)(2,1)} %refs_1_.1, ...), custom_call_target="tpu_custom_call" | custom-call | flops 4294967296 | bytes 5242880 | tf_op jit(solution)/shard_map/local_attention/pallas_call | solution.py:401
  26.7 4.7 %handed_attention.1 = bf16[512,128]{1,0:T(8,128)(2,1)} custom-call(s32[256]{0:T(256)S(1)} %copy-done.2, s32[256]{0:T(256)S(1)} %copy-done.3, bf16[96,64,256]{2,1,0:T(8,128)(2,1)} %get-tuple-element.40.all_pages, bf16[512,256]{1,0:T(8,128)(2,1)S(1)} %bitcast.35), custom_call_target="tpu_custom_call" | custom-call | tf_op jit(solution)/shard_map/handed_attention/pallas_call | solution.py:431
  31.4 6.8 %all-to-all-start.1 = ((bf16[32,16,128]{2,1,0:T(8,128)(2,1)}), bf16[32,16,128]{2,1,0:T(8,128)(2,1)S(1)}, u32[]{:S(2)}, u32[]{:S(2)}) async-start(bf16[32,16,128]{2,1,0:T(8,128)(2,1)} %bitcast.4), calls=%async_computation.1 | async-start | bytes 262144 | tf_op jit(solution)/shard_map/all_to_all | solution.py:444
  38.2 6.6 %local_attention.3.second = bf16[192,512]{1,0:T(8,128)(2,1)} custom-call(s32[16]{0:T(128)} %prefix_len.3, s32[2048]{0:T(1024)} %resident_len.3, bf16[512,512]{1,0:T(8,128)(2,1)} %refs_0_.3, bf16[512,256]{1,0:T(8,128)(2,1)} %refs_1_.1, bf16[120,64,256]{2,1,0:T(8,128)(2,1)} %refs_2_.3), custom_call_target="tpu_custom_call" | custom-call | flops 4294967296 | bytes 5242880 | tf_op jit(solution)/shard_map/local_attention/pallas_call | solution.py:401
  44.8 2.7 %all-to-all-done.1 = bf16[32,16,128]{2,1,0:T(8,128)(2,1)S(1)} async-done(((bf16[32,16,128]{2,1,0:T(8,128)(2,1)}), bf16[32,16,128]{2,1,0:T(8,128)(2,1)S(1)}, u32[]{:S(2)}, u32[]{:S(2)}) %all-to-all-start.1) | async-done | bytes 131104 | tf_op jit(solution)/shard_map/all_to_all | solution.py:444
  47.5 0.9 copy-done.1
  48.4 7.1 %front_products.1 = (bf16[256,1024]{1,0:T(8,128)(2,1)}, bf16[128,2304]{1,0:T(8,128)(2,1)}, bf16[128,2304]{1,0:T(8,128)(2,1)}, bf16[256,512]{1,0:T(8,128)(2,1)S(1...) custom-call(s32[1,256]{1,0:T(1,128)S(1)} %bitcast.38, ...), custom_call_target="tpu_custom_call" | custom-call | tf_op jit(solution)/shard_map/front_products/pallas_call | solution.py:449
  55.5 1.1 collective-permute-start.2
  56.6 3.0 %collective-permute-start.1 = (bf16[2,64,2304]{2,1,0:T(8,128)(2,1)}, bf16[2,64,2304]{2,1,0:T(8,128)(2,1)S(1)}, u32[]{:S(2)}, u32[]{:S(2)}) collective-permute-start(bf16[2,64,2304]{2,1,0:T(8,128)(2,1)} %bitcast.48), channel_id=1, source_target_pairs={{0,3},{1,0},{2,1},{3,2},{4,7},{5,4},{6,5},{7,6},{8,11},{9,8},{10,9... | collective-permute-start | bytes 1769480 | tf_op jit(solution)/shard_map/ppermute | solution.py:380
  59.6 3.7 %convolution_convert_fusion = bf16[256,4608]{1,0:T(8,128)(2,1)S(1)} fusion(bf16[256,512]{1,0:T(8,128)(2,1)S(1)} %get-tuple-element.45, bf16[512,8192]{1,0:T(8,128)(2,1)} %weight.1), kind=kOutput, calls=%fused_computation | convolution fusion | flops 1209139200 | bytes 7340032 | tf_op jit(solution)/shard_map/dot_general | solution.py:481
  63.3 0.0 slice-start
  63.3 2.7 %convolution_convert_fusion.3 = bf16[256,2560]{1,0:T(8,128)(2,1)S(1)} fusion(bf16[256,512]{1,0:T(8,128)(2,1)S(1)} %get-tuple-element.49, bf16[512,8192]{1,0:T(8,128)(2,1)} %weight.1), kind=kOutput, calls=%fused_computation.5 | convolution fusion | flops 671744000 | bytes 4194304 | tf_op jit(solution)/shard_map/dot_general | solution.py:481
  66.1 4.3 %collective-permute-done.2 = bf16[4,64,1024]{2,1,0:T(8,128)(2,1)S(1)} collective-permute-done((bf16[4,64,1024]{2,1,0:T(8,128)(2,1)}, bf16[4,64,1024]{2,1,0:T(8,128)(2,1)S(1)}, u32[]{:S(2)}, u32[]{:S(2)}) %collective-permute-start.2) | collective-permute-done | bytes 524320 | tf_op jit(solution)/shard_map/ppermute | solution.py:383
  70.4 2.8 %collective-permute-done.1 = bf16[2,64,2304]{2,1,0:T(8,128)(2,1)S(1)} collective-permute-done((bf16[2,64,2304]{2,1,0:T(8,128)(2,1)}, bf16[2,64,2304]{2,1,0:T(8,128)(2,1)S(1)}, u32[]{:S(2)}, u32[]{:S(2)}) %collective-permute-start.1) | collective-permute-done | bytes 589856 | tf_op jit(solution)/shard_map/ppermute | solution.py:380
  73.2 3.3 %collective-permute-done = bf16[2,64,2304]{2,1,0:T(8,128)(2,1)S(1)} collective-permute-done((bf16[2,64,2304]{2,1,0:T(8,128)(2,1)}, bf16[2,64,2304]{2,1,0:T(8,128)(2,1)S(1)}, u32[]{:S(2)}, u32[]{:S(2)}) %collective-permute-start) | collective-permute-done | bytes 589856 | tf_op jit(solution)/shard_map/ppermute | solution.py:380
  76.5 0.1 fusion.7
  76.6 0.0 slice-start.1
  76.6 0.3 add_convert_fusion.2
  76.9 0.1 pad_maximum_fusion
  77.0 0.1 collective-permute-start.3
  77.1 1.0 collective-permute-start.5
  78.2 0.1 pad_maximum_fusion.1
  78.2 3.2 %collective-permute-start.4 = (bf16[2,64,4608]{2,1,0:T(8,128)(2,1)S(1)}, bf16[2,64,4608]{2,1,0:T(8,128)(2,1)S(1)}, u32[]{:S(2)}, u32[]{:S(2)}) collective-permute-start(bf16[2,64,4608]{2,1,0:T(8,128)(2,1)S(1)} %pad_maximum_fusion.1), channel_id=1, source_target_pairs={{0,3},{1,0},{2,1},{3,2},{4,7},{5,4},{6,5},{7,6},{8,11},{9,8},{10,9... | collective-permute-start | bytes 3538952 | tf_op jit(solution)/shard_map/ppermute | solution.py:380
  81.5 0.9 convolution_convert_fusion.1
  82.3 1.2 convolution_convert_fusion.2
  83.5 22.2 %collective-permute-done.3 = bf16[2,64,4608]{2,1,0:T(8,128)(2,1)S(1)} collective-permute-done((bf16[2,64,4608]{2,1,0:T(8,128)(2,1)S(1)}, bf16[2,64,4608]{2,1,0:T(8,128)(2,1)S(1)}, u32[]{:S(2)}, u32[]{:S(2)}) %collective-permute-start.3) | collective-permute-done | bytes 1179680 | tf_op jit(solution)/shard_map/ppermute | solution.py:380
  105.7 0.0 collective-permute-done.4
  105.7 1.7 %collective-permute-done.5 = bf16[4,64,2560]{2,1,0:T(8,128)(2,1)S(1)} collective-permute-done((bf16[4,64,2560]{2,1,0:T(8,128)(2,1)S(1)}, bf16[4,64,2560]{2,1,0:T(8,128)(2,1)S(1)}, u32[]{:S(2)}, u32[]{:S(2)}) %collective-permute-start.5) | collective-permute-done | bytes 1310752 | tf_op jit(solution)/shard_map/ppermute | solution.py:383
  107.4 0.5 add_convert_fusion
  107.8 0.1 slice_bitcast_fusion.4
  108.0 2.9 %collective-permute-start.9 = (bf16[64,1792]{1,0:T(8,128)(2,1)S(1)}, bf16[64,1792]{1,0:T(8,128)(2,1)S(1)}, u32[]{:S(2)}, u32[]{:S(2)}) collective-permute-start(bf16[64,1792]{1,0:T(8,128)(2,1)S(1)} %get-tuple-element.79), channel_id=1, source_target_pairs={{0,3},{1,0},{2,1},{3,2},{4,7},{5,4},{6,5},{7,6},{8,11},{9,8},{10,9... | collective-permute-start | bytes 688136 | tf_op jit(solution)/shard_map/ppermute | solution.py:380
  110.9 0.4 add_convert_fusion.1
  111.4 0.9 collective-permute-start.6
  112.4 0.1 collective-permute-start.7
  112.5 2.0 %collective-permute-done.9 = bf16[64,1792]{1,0:T(8,128)(2,1)S(1)} collective-permute-done((bf16[64,1792]{1,0:T(8,128)(2,1)S(1)}, bf16[64,1792]{1,0:T(8,128)(2,1)S(1)}, u32[]{:S(2)}, u32[]{:S(2)}) %collective-permute-start.9) | collective-permute-done | bytes 229408 | tf_op jit(solution)/shard_map/ppermute | solution.py:380
  114.5 0.1 add_convert_fusion.4
  114.6 3.8 %collective-permute-start.10 = (bf16[64,3584]{1,0:T(8,128)(2,1)S(1)}, bf16[64,3584]{1,0:T(8,128)(2,1)S(1)}, u32[]{:S(2)}, u32[]{:S(2)}) collective-permute-start(bf16[64,3584]{1,0:T(8,128)(2,1)S(1)} %pad_maximum_fusion.4), channel_id=1, source_target_pairs={{0,3},{1,0},{2,1},{3,2},{4,7},{5,4},{6,5},{7,6},{8,11},{9,8},{10,9... | collective-permute-start | bytes 1376264 | tf_op jit(solution)/shard_map/ppermute | solution.py:380
  118.3 1.4 %collective-permute-done.7 = bf16[64,1792]{1,0:T(8,128)(2,1)S(1)} collective-permute-done((bf16[64,1792]{1,0:T(8,128)(2,1)S(1)}, bf16[64,1792]{1,0:T(8,128)(2,1)S(1)}, u32[]{:S(2)}, u32[]{:S(2)}) %collective-permute-start.7) | collective-permute-done | bytes 229408 | tf_op jit(solution)/shard_map/ppermute | solution.py:380
  119.7 0.1 add_convert_fusion.5
  119.8 0.1 collective-permute-start.8
  119.9 4.8 %collective-permute-done.6 = bf16[64,4608]{1,0:T(8,128)(2,1)S(1)} collective-permute-done((bf16[64,4608]{1,0:T(8,128)(2,1)S(1)}, bf16[64,4608]{1,0:T(8,128)(2,1)S(1)}, u32[]{:S(2)}, u32[]{:S(2)}) %collective-permute-start.6) | collective-permute-done | bytes 589856 | tf_op jit(solution)/shard_map/ppermute | solution.py:383
  124.7 0.2 fusion.4
  124.9 0.5 collective-permute-done.10
  125.4 4.6 %collective-permute-done.8 = bf16[64,3584]{1,0:T(8,128)(2,1)S(1)} collective-permute-done((bf16[64,3584]{1,0:T(8,128)(2,1)S(1)}, bf16[64,3584]{1,0:T(8,128)(2,1)S(1)}, u32[]{:S(2)}, u32[]{:S(2)}) %collective-permute-start.8) | collective-permute-done | bytes 458784 | tf_op jit(solution)/shard_map/ppermute | solution.py:380
  130.0 0.2 fusion.6
  130.2 1.0 pad_maximum_fusion.2
  (18 shorter events, 0.2 us)
Async XLA Ops:
  2.9 23.8 %all-to-all-start = ((bf16[32,16,256]{2,1,0:T(8,128)(2,1)}), bf16[32,16,256]{2,1,0:T(8,128)(2,1)S(1)}, u32[]{:S(2)}, u32[]{:S(2)}) async-start(bf16[32,16,256]{2,1,0:T(8,128)(2,1)} %bitcast.45), calls=%async_computation | async-start | bytes 524288 | tf_op jit(solution)/shard_map/all_to_all | solution.py:395
  14.5 12.1 %copy-start.2 = (s32[256]{0:T(256)S(1)}, s32[256]{0:T(256)}, u32[]{:S(2)}) copy-start(s32[256]{0:T(256)} %table.1) | copy-start | bytes 3076
  14.5 12.1 %copy-start.3 = (s32[256]{0:T(256)S(1)}, s32[256]{0:T(256)}, u32[]{:S(2)}) copy-start(s32[256]{0:T(256)} %lengths.1) | copy-start | bytes 3076
  31.4 16.1 %all-to-all-start.1 = ((bf16[32,16,128]{2,1,0:T(8,128)(2,1)}), bf16[32,16,128]{2,1,0:T(8,128)(2,1)S(1)}, u32[]{:S(2)}, u32[]{:S(2)}) async-start(bf16[32,16,128]{2,1,0:T(8,128)(2,1)} %bitcast.4), calls=%async_computation.1 | async-start | bytes 262144 | tf_op jit(solution)/shard_map/all_to_all | solution.py:444
  38.2 9.3 %copy-start = (bf16[320,512]{1,0:T(8,128)(2,1)S(1)}, bf16[320,512]{1,0:T(8,128)(2,1)}, u32[]{:S(2)}) copy-start(bf16[320,512]{1,0:T(8,128)(2,1)} %get-tuple-element.39.first) | copy-start | bytes 983044
  47.5 0.9 copy-start.1
  55.5 14.9 %collective-permute-start.2 = (bf16[4,64,1024]{2,1,0:T(8,128)(2,1)}, bf16[4,64,1024]{2,1,0:T(8,128)(2,1)S(1)}, u32[]{:S(2)}, u32[]{:S(2)}) collective-permute-start(bf16[4,64,1024]{2,1,0:T(8,128)(2,1)} %bitcast.49), channel_id=1, source_target_pairs={{0,4},{1,5},{2,6},{3,7},{4,0},{5,1},{6,2},{7,3},{8,12},{9,13},{10,... | collective-permute-start | bytes 1572872 | tf_op jit(solution)/shard_map/ppermute | solution.py:383
  56.6 16.7 %collective-permute-start.1 = (bf16[2,64,2304]{2,1,0:T(8,128)(2,1)}, bf16[2,64,2304]{2,1,0:T(8,128)(2,1)S(1)}, u32[]{:S(2)}, u32[]{:S(2)}) collective-permute-start(bf16[2,64,2304]{2,1,0:T(8,128)(2,1)} %bitcast.48), channel_id=1, source_target_pairs={{0,3},{1,0},{2,1},{3,2},{4,7},{5,4},{6,5},{7,6},{8,11},{9,8},{10,9... | collective-permute-start | bytes 1769480 | tf_op jit(solution)/shard_map/ppermute | solution.py:380
  59.6 16.9 %collective-permute-start = (bf16[2,64,2304]{2,1,0:T(8,128)(2,1)}, bf16[2,64,2304]{2,1,0:T(8,128)(2,1)S(1)}, u32[]{:S(2)}, u32[]{:S(2)}) collective-permute-start(bf16[2,64,2304]{2,1,0:T(8,128)(2,1)} %bitcast.47), channel_id=1, source_target_pairs={{0,1},{1,2},{2,3},{3,0},{4,5},{5,6},{6,7},{7,4},{8,9},{9,10},{10,1... | collective-permute-start | bytes 1769480 | tf_op jit(solution)/shard_map/ppermute | solution.py:380
  63.3 18.1 %slice-start = ((s8[8388608]{0:T(1024)(128)(4,1)}), s8[4194304]{0:T(1024)(128)(4,1)S(1)}, s32[]{:S(2)}) async-start(s8[8388608]{0:T(1024)(128)(4,1)} %bitcast.39), calls=%async_computation.2 | async-start | bytes 8388608
  76.6 4.8 %slice-start.1 = ((s8[8388608]{0:T(1024)(128)(4,1)}), s8[4194304]{0:T(1024)(128)(4,1)S(1)}, s32[]{:S(2)}) async-start(s8[8388608]{0:T(1024)(128)(4,1)} %bitcast.39), calls=%async_computation.3 | async-start | bytes 8388608
  77.0 28.7 %collective-permute-start.3 = (bf16[2,64,4608]{2,1,0:T(8,128)(2,1)S(1)}, bf16[2,64,4608]{2,1,0:T(8,128)(2,1)S(1)}, u32[]{:S(2)}, u32[]{:S(2)}) collective-permute-start(bf16[2,64,4608]{2,1,0:T(8,128)(2,1)S(1)} %pad_maximum_fusion), channel_id=1, source_target_pairs={{0,1},{1,2},{2,3},{3,0},{4,5},{5,6},{6,7},{7,4},{8,9},{9,10},{10,1... | collective-permute-start | bytes 3538952 | tf_op jit(solution)/shard_map/ppermute | solution.py:380
  77.1 30.3 %collective-permute-start.5 = (bf16[4,64,2560]{2,1,0:T(8,128)(2,1)S(1)}, bf16[4,64,2560]{2,1,0:T(8,128)(2,1)S(1)}, u32[]{:S(2)}, u32[]{:S(2)}) collective-permute-start(bf16[4,64,2560]{2,1,0:T(8,128)(2,1)S(1)} %bitcast.46), channel_id=1, source_target_pairs={{0,4},{1,5},{2,6},{3,7},{4,0},{5,1},{6,2},{7,3},{8,12},{9,13},{10,... | collective-permute-start | bytes 3932168 | tf_op jit(solution)/shard_map/ppermute | solution.py:383
  78.2 27.4 %collective-permute-start.4 = (bf16[2,64,4608]{2,1,0:T(8,128)(2,1)S(1)}, bf16[2,64,4608]{2,1,0:T(8,128)(2,1)S(1)}, u32[]{:S(2)}, u32[]{:S(2)}) collective-permute-start(bf16[2,64,4608]{2,1,0:T(8,128)(2,1)S(1)} %pad_maximum_fusion.1), channel_id=1, source_target_pairs={{0,3},{1,0},{2,1},{3,2},{4,7},{5,4},{6,5},{7,6},{8,11},{9,8},{10,9... | collective-permute-start | bytes 3538952 | tf_op jit(solution)/shard_map/ppermute | solution.py:380
  108.0 6.5 %collective-permute-start.9 = (bf16[64,1792]{1,0:T(8,128)(2,1)S(1)}, bf16[64,1792]{1,0:T(8,128)(2,1)S(1)}, u32[]{:S(2)}, u32[]{:S(2)}) collective-permute-start(bf16[64,1792]{1,0:T(8,128)(2,1)S(1)} %get-tuple-element.79), channel_id=1, source_target_pairs={{0,3},{1,0},{2,1},{3,2},{4,7},{5,4},{6,5},{7,6},{8,11},{9,8},{10,9... | collective-permute-start | bytes 688136 | tf_op jit(solution)/shard_map/ppermute | solution.py:380
  111.4 13.3 %collective-permute-start.6 = (bf16[64,4608]{1,0:T(8,128)(2,1)S(1)}, bf16[64,4608]{1,0:T(8,128)(2,1)S(1)}, u32[]{:S(2)}, u32[]{:S(2)}) collective-permute-start(bf16[64,4608]{1,0:T(8,128)(2,1)S(1)} %slice_bitcast_fusion), channel_id=1, source_target_pairs={{0,4},{1,5},{2,6},{3,7},{4,0},{5,1},{6,2},{7,3},{8,12},{9,13},{10,... | collective-permute-start | bytes 1769480 | tf_op jit(solution)/shard_map/ppermute | solution.py:383
  112.4 7.3 %collective-permute-start.7 = (bf16[64,1792]{1,0:T(8,128)(2,1)S(1)}, bf16[64,1792]{1,0:T(8,128)(2,1)S(1)}, u32[]{:S(2)}, u32[]{:S(2)}) collective-permute-start(bf16[64,1792]{1,0:T(8,128)(2,1)S(1)} %get-tuple-element.78), channel_id=1, source_target_pairs={{0,1},{1,2},{2,3},{3,0},{4,5},{5,6},{6,7},{7,4},{8,9},{9,10},{10,1... | collective-permute-start | bytes 688136 | tf_op jit(solution)/shard_map/ppermute | solution.py:380
  114.6 10.9 %collective-permute-start.10 = (bf16[64,3584]{1,0:T(8,128)(2,1)S(1)}, bf16[64,3584]{1,0:T(8,128)(2,1)S(1)}, u32[]{:S(2)}, u32[]{:S(2)}) collective-permute-start(bf16[64,3584]{1,0:T(8,128)(2,1)S(1)} %pad_maximum_fusion.4), channel_id=1, source_target_pairs={{0,3},{1,0},{2,1},{3,2},{4,7},{5,4},{6,5},{7,6},{8,11},{9,8},{10,9... | collective-permute-start | bytes 1376264 | tf_op jit(solution)/shard_map/ppermute | solution.py:380
  119.8 10.2 %collective-permute-start.8 = (bf16[64,3584]{1,0:T(8,128)(2,1)S(1)}, bf16[64,3584]{1,0:T(8,128)(2,1)S(1)}, u32[]{:S(2)}, u32[]{:S(2)}) collective-permute-start(bf16[64,3584]{1,0:T(8,128)(2,1)S(1)} %pad_maximum_fusion.3), channel_id=1, source_target_pairs={{0,1},{1,2},{2,3},{3,0},{4,5},{5,6},{6,7},{7,4},{8,9},{9,10},{10,1... | collective-permute-start | bytes 1376264 | tf_op jit(solution)/shard_map/ppermute | solution.py:380

commit v4 on v3

--- a/solution.py
+++ b/solution.py
@@ -14,9 +14,9 @@
 HEADS = 4
 NEG = -1e30
 COLS_Y = 4608
-PIECE = 256
-EARLY = 1024
-FIRST = 5
+PIECE = 384
+EARLY = 1152
+FIRST = 4
 LIMIT = 54
 LESS = 52
 SCALE2 = math.log2(math.e) / math.sqrt(HD)
@@ -65,15 +65,12 @@
     return copies
 
 
-def pick_kernel(table, all_q, all_f, out, queries, fresh, sems, *, half, decode_rows):
-    copies = load([(all_q, queries), (all_f, fresh)], sems)
+def pick_kernel(table, queries, fresh, out, *, half, decode_rows):
     rows = queries.shape[0]
     slots = half * HEADS * POS
     want = wanted_rows(table, lax.axis_index("group"), half, decode_rows)
     pick = (want == lax.broadcasted_iota(jnp.int32, (slots, rows), 1)).astype(F32).astype(BF)
     head = lax.rem(lax.broadcasted_iota(jnp.int32, (slots, HD), 0) // POS, HEADS)
-    for copy in copies:
-        copy.wait()
     got_q = nn_dot(pick, queries[...])
     got_f = nn_dot(pick, fresh[...])
     one_q = got_q[:, 0:HD]
@@ -218,7 +215,7 @@
 def handed_kernel(table, lengths, all_pages, sent, out, slots, pool, sems, *, half, decode_rows, most):
     group = lax.axis_index("group")
     page_len = pool.shape[1]
-    each = 4
+    each = 2
     stack = HEADS * POS
     span = each * stack
     width = each * most * page_len
@@ -386,9 +383,8 @@
     parcel = pl.pallas_call(
         functools.partial(pick_kernel, half=half, decode_rows=decode_rows),
         out_shape=made(2 * slots, kv_wide),
-        in_specs=[vmem, hbm, hbm],
+        in_specs=[vmem] * 3,
         out_specs=vmem,
-        scratch_shapes=[*inputs, dma((2,))],
         compiler_params=params,
         name="pick_rows",
     )(table, queries, fresh_kv)
@@ -436,7 +432,7 @@
         scratch_shapes=[
             pltpu.SMEM((half,), jnp.int32),
             pltpu.VMEM((half * most, page_len, kv_wide), BF),
-            dma((4,)),
+            dma((half // 2,)),
         ],
         compiler_params=less,
         name="handed_attention",

time: 132 us -> 129 us (0.977)
  waiting for transfers between devices: 50.3 us -> 47.7 us
    ppermute x3, waiting for transfers between devices: 10.9 us -> 4.89 us  [z_swap(): lax.ppermute(x, 'tp', [(t, (t + 4) % tp_count) for t in range(tp_count)])]
    ppermute x8, waiting for transfers between devices: 36.7 us -> 40.8 us  [y_step(): lax.ppermute(x, 'tp', [(t, t // 4 * 4 + (t + step) % 4) for t in range(tp...]
    pallas_call x1, Pallas kernels: 7.11 us -> 5.66 us  [on_device(): pl.pallas_call(functools.partial(front_kernel, half=half, decode_rows=dec...]
  transfers between devices with their start and end apart: 13 -> 13, of which waited for: 11 -> 11; matrix products, arithmetic and copies ran while one was open for 7% -> 7% of each run, Pallas kernels for 14% -> 15%
where the time goes in v4:
time: 129 us; the launch traced here: 128 us
  waiting for transfers between devices  47.7 us (37%)
  starting transfers between devices  35.1 us (27%)
  Pallas kernels  32.5 us (25%)
  matrix products  8.44 us (7%)
  other arithmetic  2.86 us (2%)
    ppermute x8, waiting for transfers between devices, y_step(): lax.ppermute(x, 'tp', [(t, t // 4 * 4 + (t + step) % 4) for t in range(tp...  40.8 us
    pallas_call x2, Pallas kernels, attend(): pl.pallas_call(functools.partial(local_kernel, half=half, decode_rows=dec...  18.6 us
    ppermute x8, starting transfers between devices, y_step(): lax.ppermute(x, 'tp', [(t, t // 4 * 4 + (t + step) % 4) for t in range(tp...  14.1 us
    all_to_all x1, starting transfers between devices, on_device(): lax.all_to_all(parcel, 'group', split_axis=0, concat_axis=0, tiled=True)  11.6 us
    dot_general x4, matrix products, products(): part = jnp.dot(given[name], weight, preferred_element_type=F32).astype(BF)  8.44 us
    all_to_all x1, starting transfers between devices, on_device(): lax.all_to_all(handed, 'group', split_axis=0, concat_axis=0, tiled=True)  6.29 us
    pallas_call x1, Pallas kernels, on_device(): pl.pallas_call(functools.partial(handed_kernel, half=half, decode_rows=de...  5.88 us
    pallas_call x1, Pallas kernels, on_device(): pl.pallas_call(functools.partial(front_kernel, half=half, decode_rows=dec...  5.66 us
  transfers between devices with their start and end apart: 13, of which 11 were waited for; matrix products, arithmetic and copies ran while one was open for 7% of the time, Pallas kernels for 15%

profile of v4, /device:TPU:2, one launch (start us, length us, event | category | flops | bytes accessed | tf_op | source)
XLA Modules:
  0.0 128.1 jit_solution(10722758365053544684)
XLA Ops:
  0.0 2.3 %pick_rows.1 = bf16[512,256]{1,0:T(8,128)(2,1)} custom-call(s32[1,256]{1,0:T(1,128)} %bitcast.37, bf16[512,512]{1,0:T(8,128)(2,1)} %refs_0_.3, bf16[512,256]{1,0:T(8,128)(2,1)} %refs_1_.1), custom_call_target="tpu_custom_call" | custom-call | tf_op jit(solution)/shard_map/pick_rows/pallas_call | solution.py:383
  2.3 11.6 %all-to-all-start = ((bf16[32,16,256]{2,1,0:T(8,128)(2,1)}), bf16[32,16,256]{2,1,0:T(8,128)(2,1)S(1)}, u32[]{:S(2)}, u32[]{:S(2)}) async-start(bf16[32,16,256]{2,1,0:T(8,128)(2,1)} %bitcast.45), calls=%async_computation | async-start | bytes 524288 | tf_op jit(solution)/shard_map/all_to_all | solution.py:391
  13.9 0.0 copy-start.3
  13.9 10.9 %local_attention.2 = (bf16[256,512]{1,0:T(8,128)(2,1)}, bf16[96,64,256]{2,1,0:T(8,128)(2,1)}) custom-call(s32[16]{0:T(128)} %prefix_len.3, s32[2048]{0:T(1024)} %resident_len.3, s32[256]{0:T(256)} %table.1, s32[6,256]{1,0:T(8,128)} %bitcast.50, bf16[512,512]{1,0:T(8,128)(2,1)} %refs_0_.3, bf16[512,256]{1,0:T(8,128)(2,1)} %refs_1_.1, ...), custom_call_target="tpu_custom_call" | custom-call | flops 4294967296 | bytes 5242880 | tf_op jit(solution)/shard_map/local_attention/pallas_call | solution.py:397
  24.9 0.5 all-to-all-done
  25.4 5.9 %handed_attention.1 = bf16[512,128]{1,0:T(8,128)(2,1)} custom-call(s32[256]{0:T(256)S(1)} %copy-done.2, s32[256]{0:T(256)S(1)} %copy-done.3, bf16[96,64,256]{2,1,0:T(8,128)(2,1)} %get-tuple-element.40.all_pages, bf16[512,256]{1,0:T(8,128)(2,1)S(1)} %bitcast.35), custom_call_target="tpu_custom_call" | custom-call | tf_op jit(solution)/shard_map/handed_attention/pallas_call | solution.py:427
  31.3 6.3 %all-to-all-start.1 = ((bf16[32,16,128]{2,1,0:T(8,128)(2,1)}), bf16[32,16,128]{2,1,0:T(8,128)(2,1)S(1)}, u32[]{:S(2)}, u32[]{:S(2)}) async-start(bf16[32,16,128]{2,1,0:T(8,128)(2,1)} %bitcast.4), calls=%async_computation.1 | async-start | bytes 262144 | tf_op jit(solution)/shard_map/all_to_all | solution.py:440
  37.6 7.7 %local_attention.3.second = bf16[256,512]{1,0:T(8,128)(2,1)} custom-call(s32[16]{0:T(128)} %prefix_len.3, s32[2048]{0:T(1024)} %resident_len.3, bf16[512,512]{1,0:T(8,128)(2,1)} %refs_0_.3, bf16[512,256]{1,0:T(8,128)(2,1)} %refs_1_.1, bf16[120,64,256]{2,1,0:T(8,128)(2,1)} %refs_2_.3), custom_call_target="tpu_custom_call" | custom-call | flops 4294967296 | bytes 5242880 | tf_op jit(solution)/shard_map/local_attention/pallas_call | solution.py:397
  45.3 1.5 %all-to-all-done.1 = bf16[32,16,128]{2,1,0:T(8,128)(2,1)S(1)} async-done(((bf16[32,16,128]{2,1,0:T(8,128)(2,1)}), bf16[32,16,128]{2,1,0:T(8,128)(2,1)S(1)}, u32[]{:S(2)}, u32[]{:S(2)}) %all-to-all-start.1) | async-done | bytes 131104 | tf_op jit(solution)/shard_map/all_to_all | solution.py:440
  46.9 0.9 copy-done.1
  47.8 5.7 %front_products.1 = (bf16[256,1152]{1,0:T(8,128)(2,1)}, bf16[128,2304]{1,0:T(8,128)(2,1)}, bf16[128,2304]{1,0:T(8,128)(2,1)}, bf16[256,512]{1,0:T(8,128)(2,1)S(1...) custom-call(s32[1,256]{1,0:T(1,128)S(1)} %bitcast.38, ...), custom_call_target="tpu_custom_call" | custom-call | tf_op jit(solution)/shard_map/front_products/pallas_call | solution.py:445
  53.5 3.1 %collective-permute-start.1 = (bf16[2,64,2304]{2,1,0:T(8,128)(2,1)}, bf16[2,64,2304]{2,1,0:T(8,128)(2,1)S(1)}, u32[]{:S(2)}, u32[]{:S(2)}) collective-permute-start(bf16[2,64,2304]{2,1,0:T(8,128)(2,1)} %bitcast.49), channel_id=1, source_target_pairs={{0,3},{1,0},{2,1},{3,2},{4,7},{5,4},{6,5},{7,6},{8,11},{9,8},{10,9... | collective-permute-start | bytes 1769480 | tf_op jit(solution)/shard_map/ppermute | solution.py:377
  56.6 1.0 collective-permute-start.2
  57.5 3.7 %convolution_convert_fusion = bf16[256,4608]{1,0:T(8,128)(2,1)S(1)} fusion(bf16[256,512]{1,0:T(8,128)(2,1)S(1)} %get-tuple-element.45, bf16[512,8192]{1,0:T(8,128)(2,1)} %weight.1), kind=kOutput, calls=%fused_computation | convolution fusion | flops 1209139200 | bytes 7340032 | tf_op jit(solution)/shard_map/dot_general | solution.py:477
  61.3 0.0 slice-start
  61.3 2.7 %convolution_convert_fusion.3 = bf16[256,2432]{1,0:T(8,128)(2,1)S(1)} fusion(bf16[256,512]{1,0:T(8,128)(2,1)S(1)} %get-tuple-element.49, bf16[512,8192]{1,0:T(8,128)(2,1)} %weight.1), kind=kOutput, calls=%fused_computation.5 | convolution fusion | flops 638156800 | bytes 3997696 | tf_op jit(solution)/shard_map/dot_general | solution.py:477
  64.0 6.4 %collective-permute-done.1 = bf16[2,64,2304]{2,1,0:T(8,128)(2,1)S(1)} collective-permute-done((bf16[2,64,2304]{2,1,0:T(8,128)(2,1)}, bf16[2,64,2304]{2,1,0:T(8,128)(2,1)S(1)}, u32[]{:S(2)}, u32[]{:S(2)}) %collective-permute-start.1) | collective-permute-done | bytes 589856 | tf_op jit(solution)/shard_map/ppermute | solution.py:377
  70.4 3.3 %collective-permute-done = bf16[2,64,2304]{2,1,0:T(8,128)(2,1)S(1)} collective-permute-done((bf16[2,64,2304]{2,1,0:T(8,128)(2,1)}, bf16[2,64,2304]{2,1,0:T(8,128)(2,1)S(1)}, u32[]{:S(2)}, u32[]{:S(2)}) %collective-permute-start) | collective-permute-done | bytes 589856 | tf_op jit(solution)/shard_map/ppermute | solution.py:377
  73.7 0.1 fusion.7
  73.8 0.0 slice-start.1
  73.8 0.3 add_convert_fusion.2
  74.1 0.1 pad_maximum_fusion
  74.2 0.1 collective-permute-start.3
  74.3 1.2 collective-permute-start.5
  75.4 0.1 pad_maximum_fusion.1
  75.5 3.2 %collective-permute-start.4 = (bf16[2,64,4608]{2,1,0:T(8,128)(2,1)S(1)}, bf16[2,64,4608]{2,1,0:T(8,128)(2,1)S(1)}, u32[]{:S(2)}, u32[]{:S(2)}) collective-permute-start(bf16[2,64,4608]{2,1,0:T(8,128)(2,1)S(1)} %pad_maximum_fusion.1), channel_id=1, source_target_pairs={{0,3},{1,0},{2,1},{3,2},{4,7},{5,4},{6,5},{7,6},{8,11},{9,8},{10,9... | collective-permute-start | bytes 3538952 | tf_op jit(solution)/shard_map/ppermute | solution.py:377
  78.7 0.9 convolution_convert_fusion.1
  79.6 1.2 convolution_convert_fusion.2
  80.8 22.3 %collective-permute-done.3 = bf16[2,64,4608]{2,1,0:T(8,128)(2,1)S(1)} collective-permute-done((bf16[2,64,4608]{2,1,0:T(8,128)(2,1)S(1)}, bf16[2,64,4608]{2,1,0:T(8,128)(2,1)S(1)}, u32[]{:S(2)}, u32[]{:S(2)}) %collective-permute-start.3) | collective-permute-done | bytes 1179680 | tf_op jit(solution)/shard_map/ppermute | solution.py:377
  103.0 0.3 collective-permute-done.4
  103.4 0.4 add_convert_fusion
  103.8 0.1 slice_bitcast_fusion.4
  104.0 3.8 %collective-permute-start.9 = (bf16[64,1792]{1,0:T(8,128)(2,1)S(1)}, bf16[64,1792]{1,0:T(8,128)(2,1)S(1)}, u32[]{:S(2)}, u32[]{:S(2)}) collective-permute-start(bf16[64,1792]{1,0:T(8,128)(2,1)S(1)} %get-tuple-element.79), channel_id=1, source_target_pairs={{0,3},{1,0},{2,1},{3,2},{4,7},{5,4},{6,5},{7,6},{8,11},{9,8},{10,9... | collective-permute-start | bytes 688136 | tf_op jit(solution)/shard_map/ppermute | solution.py:377
  107.7 0.4 add_convert_fusion.1
  108.2 0.9 collective-permute-start.6
  109.2 0.1 collective-permute-start.7
  109.3 2.0 %collective-permute-done.9 = bf16[64,1792]{1,0:T(8,128)(2,1)S(1)} collective-permute-done((bf16[64,1792]{1,0:T(8,128)(2,1)S(1)}, bf16[64,1792]{1,0:T(8,128)(2,1)S(1)}, u32[]{:S(2)}, u32[]{:S(2)}) %collective-permute-start.9) | collective-permute-done | bytes 229408 | tf_op jit(solution)/shard_map/ppermute | solution.py:377
  111.3 0.1 add_convert_fusion.4
  111.4 3.8 %collective-permute-start.10 = (bf16[64,3584]{1,0:T(8,128)(2,1)S(1)}, bf16[64,3584]{1,0:T(8,128)(2,1)S(1)}, u32[]{:S(2)}, u32[]{:S(2)}) collective-permute-start(bf16[64,3584]{1,0:T(8,128)(2,1)S(1)} %pad_maximum_fusion.4), channel_id=1, source_target_pairs={{0,3},{1,0},{2,1},{3,2},{4,7},{5,4},{6,5},{7,6},{8,11},{9,8},{10,9... | collective-permute-start | bytes 1376264 | tf_op jit(solution)/shard_map/ppermute | solution.py:377
  115.1 1.4 %collective-permute-done.7 = bf16[64,1792]{1,0:T(8,128)(2,1)S(1)} collective-permute-done((bf16[64,1792]{1,0:T(8,128)(2,1)S(1)}, bf16[64,1792]{1,0:T(8,128)(2,1)S(1)}, u32[]{:S(2)}, u32[]{:S(2)}) %collective-permute-start.7) | collective-permute-done | bytes 229408 | tf_op jit(solution)/shard_map/ppermute | solution.py:377
  116.5 0.1 add_convert_fusion.5
  116.6 0.1 collective-permute-start.8
  116.7 4.9 %collective-permute-done.6 = bf16[64,4608]{1,0:T(8,128)(2,1)S(1)} collective-permute-done((bf16[64,4608]{1,0:T(8,128)(2,1)S(1)}, bf16[64,4608]{1,0:T(8,128)(2,1)S(1)}, u32[]{:S(2)}, u32[]{:S(2)}) %collective-permute-start.6) | collective-permute-done | bytes 589856 | tf_op jit(solution)/shard_map/ppermute | solution.py:380
  121.6 0.2 fusion.4
  121.7 0.5 collective-permute-done.10
  122.3 4.6 %collective-permute-done.8 = bf16[64,3584]{1,0:T(8,128)(2,1)S(1)} collective-permute-done((bf16[64,3584]{1,0:T(8,128)(2,1)S(1)}, bf16[64,3584]{1,0:T(8,128)(2,1)S(1)}, u32[]{:S(2)}, u32[]{:S(2)}) %collective-permute-start.8) | collective-permute-done | bytes 458784 | tf_op jit(solution)/shard_map/ppermute | solution.py:377
  126.8 0.2 fusion.6
  127.0 1.0 pad_maximum_fusion.2
  (18 shorter events, 0.2 us)
Async XLA Ops:
  2.3 23.1 %all-to-all-start = ((bf16[32,16,256]{2,1,0:T(8,128)(2,1)}), bf16[32,16,256]{2,1,0:T(8,128)(2,1)S(1)}, u32[]{:S(2)}, u32[]{:S(2)}) async-start(bf16[32,16,256]{2,1,0:T(8,128)(2,1)} %bitcast.45), calls=%async_computation | async-start | bytes 524288 | tf_op jit(solution)/shard_map/all_to_all | solution.py:391
  13.9 11.5 %copy-start.2 = (s32[256]{0:T(256)S(1)}, s32[256]{0:T(256)}, u32[]{:S(2)}) copy-start(s32[256]{0:T(256)} %table.1) | copy-start | bytes 3076
  13.9 11.5 %copy-start.3 = (s32[256]{0:T(256)S(1)}, s32[256]{0:T(256)}, u32[]{:S(2)}) copy-start(s32[256]{0:T(256)} %lengths.1) | copy-start | bytes 3076
  31.3 15.6 %all-to-all-start.1 = ((bf16[32,16,128]{2,1,0:T(8,128)(2,1)}), bf16[32,16,128]{2,1,0:T(8,128)(2,1)S(1)}, u32[]{:S(2)}, u32[]{:S(2)}) async-start(bf16[32,16,128]{2,1,0:T(8,128)(2,1)} %bitcast.4), calls=%async_computation.1 | async-start | bytes 262144 | tf_op jit(solution)/shard_map/all_to_all | solution.py:440
  37.6 9.3 %copy-start = (bf16[256,512]{1,0:T(8,128)(2,1)S(1)}, bf16[256,512]{1,0:T(8,128)(2,1)}, u32[]{:S(2)}) copy-start(bf16[256,512]{1,0:T(8,128)(2,1)} %get-tuple-element.39.first) | copy-start | bytes 786436
  46.9 1.0 copy-start.1
  53.5 16.9 %collective-permute-start.1 = (bf16[2,64,2304]{2,1,0:T(8,128)(2,1)}, bf16[2,64,2304]{2,1,0:T(8,128)(2,1)S(1)}, u32[]{:S(2)}, u32[]{:S(2)}) collective-permute-start(bf16[2,64,2304]{2,1,0:T(8,128)(2,1)} %bitcast.49), channel_id=1, source_target_pairs={{0,3},{1,0},{2,1},{3,2},{4,7},{5,4},{6,5},{7,6},{8,11},{9,8},{10,9... | collective-permute-start | bytes 1769480 | tf_op jit(solution)/shard_map/ppermute | solution.py:377
  56.6 17.1 %collective-permute-start = (bf16[2,64,2304]{2,1,0:T(8,128)(2,1)}, bf16[2,64,2304]{2,1,0:T(8,128)(2,1)S(1)}, u32[]{:S(2)}, u32[]{:S(2)}) collective-permute-start(bf16[2,64,2304]{2,1,0:T(8,128)(2,1)} %bitcast.48), channel_id=1, source_target_pairs={{0,1},{1,2},{2,3},{3,0},{4,5},{5,6},{6,7},{7,4},{8,9},{9,10},{10,1... | collective-permute-start | bytes 1769480 | tf_op jit(solution)/shard_map/ppermute | solution.py:377
  56.6 17.1 %collective-permute-start.2 = (bf16[4,64,1152]{2,1,0:T(8,128)(2,1)}, bf16[4,64,1152]{2,1,0:T(8,128)(2,1)S(1)}, u32[]{:S(2)}, u32[]{:S(2)}) collective-permute-start(bf16[4,64,1152]{2,1,0:T(8,128)(2,1)} %bitcast.47), channel_id=1, source_target_pairs={{0,4},{1,5},{2,6},{3,7},{4,0},{5,1},{6,2},{7,3},{8,12},{9,13},{10,... | collective-permute-start | bytes 1769480 | tf_op jit(solution)/shard_map/ppermute | solution.py:380
  61.3 17.4 %slice-start = ((s8[8388608]{0:T(1024)(128)(4,1)}), s8[4194304]{0:T(1024)(128)(4,1)S(1)}, s32[]{:S(2)}) async-start(s8[8388608]{0:T(1024)(128)(4,1)} %bitcast.39), calls=%async_computation.2 | async-start | bytes 8388608
  73.8 4.9 %slice-start.1 = ((s8[8388608]{0:T(1024)(128)(4,1)}), s8[4194304]{0:T(1024)(128)(4,1)S(1)}, s32[]{:S(2)}) async-start(s8[8388608]{0:T(1024)(128)(4,1)} %bitcast.39), calls=%async_computation.3 | async-start | bytes 8388608
  74.2 28.9 %collective-permute-start.3 = (bf16[2,64,4608]{2,1,0:T(8,128)(2,1)S(1)}, bf16[2,64,4608]{2,1,0:T(8,128)(2,1)S(1)}, u32[]{:S(2)}, u32[]{:S(2)}) collective-permute-start(bf16[2,64,4608]{2,1,0:T(8,128)(2,1)S(1)} %pad_maximum_fusion), channel_id=1, source_target_pairs={{0,1},{1,2},{2,3},{3,0},{4,5},{5,6},{6,7},{7,4},{8,9},{9,10},{10,1... | collective-permute-start | bytes 3538952 | tf_op jit(solution)/shard_map/ppermute | solution.py:377
  74.3 29.1 %collective-permute-start.5 = (bf16[4,64,2432]{2,1,0:T(8,128)(2,1)S(1)}, bf16[4,64,2432]{2,1,0:T(8,128)(2,1)S(1)}, u32[]{:S(2)}, u32[]{:S(2)}) collective-permute-start(bf16[4,64,2432]{2,1,0:T(8,128)(2,1)S(1)} %bitcast.46), channel_id=1, source_target_pairs={{0,4},{1,5},{2,6},{3,7},{4,0},{5,1},{6,2},{7,3},{8,12},{9,13},{10,... | collective-permute-start | bytes 3735560 | tf_op jit(solution)/shard_map/ppermute | solution.py:380
  75.5 27.9 %collective-permute-start.4 = (bf16[2,64,4608]{2,1,0:T(8,128)(2,1)S(1)}, bf16[2,64,4608]{2,1,0:T(8,128)(2,1)S(1)}, u32[]{:S(2)}, u32[]{:S(2)}) collective-permute-start(bf16[2,64,4608]{2,1,0:T(8,128)(2,1)S(1)} %pad_maximum_fusion.1), channel_id=1, source_target_pairs={{0,3},{1,0},{2,1},{3,2},{4,7},{5,4},{6,5},{7,6},{8,11},{9,8},{10,9... | collective-permute-start | bytes 3538952 | tf_op jit(solution)/shard_map/ppermute | solution.py:377
  104.0 7.3 %collective-permute-start.9 = (bf16[64,1792]{1,0:T(8,128)(2,1)S(1)}, bf16[64,1792]{1,0:T(8,128)(2,1)S(1)}, u32[]{:S(2)}, u32[]{:S(2)}) collective-permute-start(bf16[64,1792]{1,0:T(8,128)(2,1)S(1)} %get-tuple-element.79), channel_id=1, source_target_pairs={{0,3},{1,0},{2,1},{3,2},{4,7},{5,4},{6,5},{7,6},{8,11},{9,8},{10,9... | collective-permute-start | bytes 688136 | tf_op jit(solution)/shard_map/ppermute | solution.py:377
  108.2 13.4 %collective-permute-start.6 = (bf16[64,4608]{1,0:T(8,128)(2,1)S(1)}, bf16[64,4608]{1,0:T(8,128)(2,1)S(1)}, u32[]{:S(2)}, u32[]{:S(2)}) collective-permute-start(bf16[64,4608]{1,0:T(8,128)(2,1)S(1)} %slice_bitcast_fusion), channel_id=1, source_target_pairs={{0,4},{1,5},{2,6},{3,7},{4,0},{5,1},{6,2},{7,3},{8,12},{9,13},{10,... | collective-permute-start | bytes 1769480 | tf_op jit(solution)/shard_map/ppermute | solution.py:380
  109.2 7.3 %collective-permute-start.7 = (bf16[64,1792]{1,0:T(8,128)(2,1)S(1)}, bf16[64,1792]{1,0:T(8,128)(2,1)S(1)}, u32[]{:S(2)}, u32[]{:S(2)}) collective-permute-start(bf16[64,1792]{1,0:T(8,128)(2,1)S(1)} %get-tuple-element.78), channel_id=1, source_target_pairs={{0,1},{1,2},{2,3},{3,0},{4,5},{5,6},{6,7},{7,4},{8,9},{9,10},{10,1... | collective-permute-start | bytes 688136 | tf_op jit(solution)/shard_map/ppermute | solution.py:377
  111.4 10.9 %collective-permute-start.10 = (bf16[64,3584]{1,0:T(8,128)(2,1)S(1)}, bf16[64,3584]{1,0:T(8,128)(2,1)S(1)}, u32[]{:S(2)}, u32[]{:S(2)}) collective-permute-start(bf16[64,3584]{1,0:T(8,128)(2,1)S(1)} %pad_maximum_fusion.4), channel_id=1, source_target_pairs={{0,3},{1,0},{2,1},{3,2},{4,7},{5,4},{6,5},{7,6},{8,11},{9,8},{10,9... | collective-permute-start | bytes 1376264 | tf_op jit(solution)/shard_map/ppermute | solution.py:377
  116.6 10.2 %collective-permute-start.8 = (bf16[64,3584]{1,0:T(8,128)(2,1)S(1)}, bf16[64,3584]{1,0:T(8,128)(2,1)S(1)}, u32[]{:S(2)}, u32[]{:S(2)}) collective-permute-start(bf16[64,3584]{1,0:T(8,128)(2,1)S(1)} %pad_maximum_fusion.3), channel_id=1, source_target_pairs={{0,1},{1,2},{2,3},{3,0},{4,5},{5,6},{6,7},{7,4},{8,9},{9,10},{10,1... | collective-permute-start | bytes 1376264 | tf_op jit(solution)/shard_map/ppermute | solution.py:377

commit v5 on v4

--- a/solution.py
+++ b/solution.py
@@ -215,7 +215,7 @@
 def handed_kernel(table, lengths, all_pages, sent, out, slots, pool, sems, *, half, decode_rows, most):
     group = lax.axis_index("group")
     page_len = pool.shape[1]
-    each = 2
+    each = 4
     stack = HEADS * POS
     span = each * stack
     width = each * most * page_len
@@ -265,9 +265,9 @@
 
 
 def front_kernel(
-    table, first, second, back, weight, z_out, r_out, l_out, x_near, x_far, x13, x0, *scratch, half, decode_rows
+    table, first, second, back, weight, z_out, y_outs, x_near, x_far, x13, x0, *scratch, half, decode_rows
 ):
-    whole, held, sems, z_part, y_r, y_l, out_sems = scratch
+    whole, held, sems, z_part, y_parts, out_sems = scratch
     group = lax.axis_index("group")
     tp = lax.axis_index("tp")
     my_y, my_z = lax.rem(tp, 4), tp // 4
@@ -275,11 +275,11 @@
     rows = whole.shape[0]
     slots = half * HEADS * POS
     count, _, part = held.shape
-    mid = y_r.shape[1] // part
-    z_count = count - 2 * mid
+    quarter = y_parts[0].shape[1] // part
+    z_count = count - 4 * quarter
 
     def fetch(n):
-        begin = (2 * mid + n if n < z_count else n - z_count) * part
+        begin = (4 * quarter + n if n < z_count else n - z_count) * part
         return pltpu.make_async_copy(
             weight.at[:, pl.ds(begin, part)], held.at[n], sems.at[n]
         )
@@ -322,11 +322,9 @@
         x0[far * share : (far + 1) * share] = block(0, far)
     x2 = jnp.concatenate([block(2, 0), block(2, 1)], axis=0)
     copies = []
-    for x, begin, held_out, out in (
-        (x_far[...], 0, z_part, z_out),
-        (x2, z_count, y_r, r_out),
-        (x2, z_count + mid, y_l, l_out),
-    ):
+    order = [(x2, z_count + i * quarter, y_parts[i], y_outs[i]) for i in range(4)]
+    order.insert(0, (x_far[...], 0, z_part, z_out))
+    for x, begin, held_out, out in order:
         for n in range(held_out.shape[1] // part):
             fetch(begin + n).wait()
             held_out[:, n * part : (n + 1) * part] = nn_dot(x, held[begin + n]).astype(BF)
@@ -432,7 +430,7 @@
         scratch_shapes=[
             pltpu.SMEM((half,), jnp.int32),
             pltpu.VMEM((half * most, page_len, kv_wide), BF),
-            dma((half // 2,)),
+            dma((half // 4,)),
         ],
         compiler_params=less,
         name="handed_attention",
@@ -441,24 +439,26 @@
     (second,) = attend(1, (queries, fresh_kv, page_pool), [hbm, hbm, hbm], [], [], [])
     share = rows // tp_count
     pieces = (COLS_Y + EARLY) // PIECE
-    sizes = [(4 * share, EARLY), (2 * share, COLS_Y // 2), (2 * share, COLS_Y // 2)]
-    z1_a, y2_r, y2_l, x_near, x_far, x13, x0 = pl.pallas_call(
+    quarter = (2 * share, COLS_Y // 4)
+    z1_a, y2, x_near, x_far, x13, x0 = pl.pallas_call(
         functools.partial(front_kernel, half=half, decode_rows=decode_rows),
         out_shape=[
-            *(made(*size) for size in sizes),
+            made(4 * share, EARLY),
+            [made(*quarter)] * 4,
             made(4 * share, wide),
             made(4 * share, wide),
             made(4 * share, wide),
             made(2 * share, wide),
         ],
         in_specs=[vmem] * 4 + [hbm],
-        out_specs=[hbm] * 3 + [vmem] * 4,
+        out_specs=[hbm, [hbm] * 4] + [vmem] * 4,
         scratch_shapes=[
             pltpu.VMEM((rows, wide), BF),
             pltpu.VMEM((pieces, wide, PIECE), BF),
             dma((pieces,)),
-            *(pltpu.VMEM(size, BF) for size in sizes),
-            dma((3,)),
+            pltpu.VMEM((4 * share, EARLY), BF),
+            [pltpu.VMEM(quarter, BF)] * 4,
+            dma((5,)),
         ],
         compiler_params=less,
         name="front_products",
@@ -467,7 +467,13 @@
     def blocks(x):
         return x.reshape(-1, share, x.shape[1])
 
-    cuts = {"y": (0, COLS_Y), "b": (COLS_Y + EARLY, None), "z": (COLS_Y, None)}
+    cuts = {
+        "p": (0, COLS_Y // 2),
+        "q": (COLS_Y // 2, COLS_Y),
+        "y": (0, COLS_Y),
+        "b": (COLS_Y + EARLY, None),
+        "z": (COLS_Y, None),
+    }
 
     def products(given, names):
         parts = []
@@ -489,16 +495,25 @@
         left = jnp.concatenate([next_l[..., :mid], add(next_l[..., mid:], far_l)], -1)
         return y_step(right, 1), y_step(left, -1)
 
+    far_p = y_step(blocks(y2[0]), 1), y_step(blocks(y2[1]), -1)
     come_a = z_swap(blocks(z1_a))
-    far_y = y_step(blocks(y2_r), 1), y_step(blocks(y2_l), -1)
-    given = {"y13": x13, "b1": x_far, "y0": x0, "z0": x_near}
-    (y13, z1_b), given = products(given, ("y13", "b1"))
-    far_y, come_a, z1_b, given, y13 = lax.optimization_barrier((far_y, come_a, z1_b, given, y13))
+    given = {"p13": x13, "b1": x_far, "q13": x13, "y0": x0, "z0": x_near}
+    (p13,), given = products(given, ("p13",))
+    p13, q_r, q_l = lax.optimization_barrier((p13, y2[2], y2[3]))
+    far_q = y_step(blocks(q_r), 1), y_step(blocks(q_l), -1)
+    (z1_b,), given = products(given, ("b1",))
+    far_p, p13, z1_b, given = lax.optimization_barrier((far_p, p13, z1_b, given))
+    near_p = start_near(p13[0:2], p13[2:4], *far_p)
+    come_a, far_q, z1_b, given = lax.optimization_barrier((come_a, far_q, z1_b, given))
     come_b = z_swap(z1_b)
-    near_y = start_near(y13[0:2], y13[2:4], *far_y)
+    (q13,), given = products(given, ("q13",))
+    near_q = start_near(q13[0:2], q13[2:4], *far_q)
     (y0, z0), given = products(given, ("y0", "z0"))
-    near_y, come_b, y0, z0 = lax.optimization_barrier((near_y, come_b, y0, z0))
-    mine_y = add(y0, *near_y)
+    near_p, near_q, come_b, y0, z0 = lax.optimization_barrier((near_p, near_q, come_b, y0, z0))
+    mid = COLS_Y // 2
+    mine_y = jnp.concatenate(
+        [add(y0[..., :mid], *near_p), add(y0[..., mid:], *near_q)], axis=-1
+    )
     come_y = z_swap(mine_y[1])
     mine_z = add(z0, jnp.concatenate([come_a, come_b], axis=-1))
     far_z = start_far(mine_z[2])

time: 129 us -> 126 us (0.977)
  waiting for transfers between devices: 47.7 us -> 43.6 us
  starting transfers between devices: 35.1 us -> 38.6 us
    ppermute x8 -> x12, waiting for transfers between devices: 40.8 us -> 32.2 us  [y_step(): lax.ppermute(x, 'tp', [(t, t // 4 * 4 + (t + step) % 4) for t in range(tp...]
    ppermute x3, waiting for transfers between devices: 4.89 us -> 9.3 us  [z_swap(): lax.ppermute(x, 'tp', [(t, (t + 4) % tp_count) for t in range(tp_count)])]
    ppermute x8 -> x12, starting transfers between devices: 14.1 us -> 17.5 us  [y_step(): lax.ppermute(x, 'tp', [(t, t // 4 * 4 + (t + step) % 4) for t in range(tp...]
    dot_general x4 -> x5, matrix products: 8.44 us -> 7.82 us  [products(): part = jnp.dot(given[name], weight, preferred_element_type=F32).astype(BF)]
  transfers between devices with their start and end apart: 13 -> 17, of which waited for: 11 -> 13; matrix products, arithmetic and copies ran while one was open for 7% -> 7% of each run, Pallas kernels for 15% -> 15%
where the time goes in v5:
time: 126 us
  waiting for transfers between devices  43.6 us (35%)
  starting transfers between devices  38.6 us (31%)
  Pallas kernels  31.4 us (25%)
  matrix products  7.82 us (6%)
  other arithmetic  2.95 us (2%)
  local copies, waits for them, and re-layouts  1.31 us (1%)
    ppermute x12, waiting for transfers between devices, y_step(): lax.ppermute(x, 'tp', [(t, t // 4 * 4 + (t + step) % 4) for t in range(tp...  32.2 us
    pallas_call x2, Pallas kernels, attend(): pl.pallas_call(functools.partial(local_kernel, half=half, decode_rows=dec...  18.6 us
    ppermute x12, starting transfers between devices, y_step(): lax.ppermute(x, 'tp', [(t, t // 4 * 4 + (t + step) % 4) for t in range(tp...  17.5 us
    all_to_all x1, starting transfers between devices, on_device(): lax.all_to_all(parcel, 'group', split_axis=0, concat_axis=0, tiled=True)  11.6 us
    ppermute x3, waiting for transfers between devices, z_swap(): lax.ppermute(x, 'tp', [(t, (t + 4) % tp_count) for t in range(tp_count)])  9.3 us
    dot_general x5, matrix products, products(): part = jnp.dot(given[name], weight, preferred_element_type=F32).astype(BF)  7.82 us
    all_to_all x1, starting transfers between devices, on_device(): lax.all_to_all(handed, 'group', split_axis=0, concat_axis=0, tiled=True)  6.29 us
    pallas_call x1, Pallas kernels, on_device(): pl.pallas_call(functools.partial(front_kernel, half=half, decode_rows=dec...  5.77 us
  transfers between devices with their start and end apart: 17, of which 13 were waited for; matrix products, arithmetic and copies ran while one was open for 7% of the time, Pallas kernels for 15%

profile of v5, /device:TPU:2, one launch (start us, length us, event | category | flops | bytes accessed | tf_op | source)
XLA Modules:
  0.0 126.1 jit_solution(2932388610186810692)
XLA Ops:
  0.0 2.3 %pick_rows.1 = bf16[512,256]{1,0:T(8,128)(2,1)} custom-call(s32[1,256]{1,0:T(1,128)} %bitcast.42, bf16[512,512]{1,0:T(8,128)(2,1)} %refs_0_.3, bf16[512,256]{1,0:T(8,128)(2,1)} %refs_1_.1), custom_call_target="tpu_custom_call" | custom-call | tf_op jit(solution)/shard_map/pick_rows/pallas_call | solution.py:381
  2.3 11.6 %all-to-all-start = ((bf16[32,16,256]{2,1,0:T(8,128)(2,1)}), bf16[32,16,256]{2,1,0:T(8,128)(2,1)S(1)}, u32[]{:S(2)}, u32[]{:S(2)}) async-start(bf16[32,16,256]{2,1,0:T(8,128)(2,1)} %bitcast.55), calls=%async_computation | async-start | bytes 524288 | tf_op jit(solution)/shard_map/all_to_all | solution.py:389
  13.9 10.9 %local_attention.2 = (bf16[256,512]{1,0:T(8,128)(2,1)}, bf16[96,64,256]{2,1,0:T(8,128)(2,1)}) custom-call(s32[16]{0:T(128)} %prefix_len.3, s32[2048]{0:T(1024)} %resident_len.3, s32[256]{0:T(256)} %table.1, s32[6,256]{1,0:T(8,128)} %bitcast.61, bf16[512,512]{1,0:T(8,128)(2,1)} %refs_0_.3, bf16[512,256]{1,0:T(8,128)(2,1)} %refs_1_.1, ...), custom_call_target="tpu_custom_call" | custom-call | flops 4294967296 | bytes 5242880 | tf_op jit(solution)/shard_map/local_attention/pallas_call | solution.py:395
  24.9 0.5 all-to-all-done
  25.4 4.7 %handed_attention.1 = bf16[512,128]{1,0:T(8,128)(2,1)} custom-call(s32[256]{0:T(256)S(1)} %copy-done.2, s32[256]{0:T(256)S(1)} %copy-done.3, bf16[96,64,256]{2,1,0:T(8,128)(2,1)} %get-tuple-element.59.all_pages, bf16[512,256]{1,0:T(8,128)(2,1)S(1)} %bitcast.40), custom_call_target="tpu_custom_call" | custom-call | tf_op jit(solution)/shard_map/handed_attention/pallas_call | solution.py:425
  30.1 6.3 %all-to-all-start.1 = ((bf16[32,16,128]{2,1,0:T(8,128)(2,1)}), bf16[32,16,128]{2,1,0:T(8,128)(2,1)S(1)}, u32[]{:S(2)}, u32[]{:S(2)}) async-start(bf16[32,16,128]{2,1,0:T(8,128)(2,1)} %bitcast.4), calls=%async_computation.1 | async-start | bytes 262144 | tf_op jit(solution)/shard_map/all_to_all | solution.py:438
  36.4 7.7 %local_attention.3.second = bf16[256,512]{1,0:T(8,128)(2,1)} custom-call(s32[16]{0:T(128)} %prefix_len.3, s32[2048]{0:T(1024)} %resident_len.3, bf16[512,512]{1,0:T(8,128)(2,1)} %refs_0_.3, bf16[512,256]{1,0:T(8,128)(2,1)} %refs_1_.1, bf16[120,64,256]{2,1,0:T(8,128)(2,1)} %refs_2_.3), custom_call_target="tpu_custom_call" | custom-call | flops 4294967296 | bytes 5242880 | tf_op jit(solution)/shard_map/local_attention/pallas_call | solution.py:395
  44.1 1.6 %all-to-all-done.1 = bf16[32,16,128]{2,1,0:T(8,128)(2,1)S(1)} async-done(((bf16[32,16,128]{2,1,0:T(8,128)(2,1)}), bf16[32,16,128]{2,1,0:T(8,128)(2,1)S(1)}, u32[]{:S(2)}, u32[]{:S(2)}) %all-to-all-start.1) | async-done | bytes 131104 | tf_op jit(solution)/shard_map/all_to_all | solution.py:438
  45.7 0.9 copy-done.1
  46.7 5.8 %front_products.1 = (bf16[256,1152]{1,0:T(8,128)(2,1)}, bf16[128,1152]{1,0:T(8,128)(2,1)S(1)}, bf16[128,1152]{1,0:T(8,128)(2,1)}, bf16[128,1152]{1,0:T(8,128)(2,...) custom-call(s32[1,256]{1,0:T(1,128)S(1)} %bitcast.43, ...), custom_call_target="tpu_custom_call" | custom-call | tf_op jit(solution)/shard_map/front_products/pallas_call | solution.py:443
  52.4 3.1 %collective-permute-start.1 = (bf16[2,64,1152]{2,1,0:T(8,128)(2,1)}, bf16[2,64,1152]{2,1,0:T(8,128)(2,1)S(1)}, u32[]{:S(2)}, u32[]{:S(2)}) collective-permute-start(bf16[2,64,1152]{2,1,0:T(8,128)(2,1)} %bitcast.60), channel_id=1, source_target_pairs={{0,3},{1,0},{2,1},{3,2},{4,7},{5,4},{6,5},{7,6},{8,11},{9,8},{10,9... | collective-permute-start | bytes 884744 | tf_op jit(solution)/shard_map/ppermute | solution.py:375
  55.5 1.0 collective-permute-start.4
  56.5 2.6 %convolution_convert_fusion.4 = bf16[256,2304]{1,0:T(8,128)(2,1)S(1)} fusion(bf16[256,512]{1,0:T(8,128)(2,1)S(1)} %get-tuple-element.89, bf16[512,8192]{1,0:T(8,128)(2,1)} %weight.1), kind=kOutput, calls=%fused_computation.5 | convolution fusion | flops 604569600 | bytes 3801088 | tf_op jit(solution)/shard_map/dot_general | solution.py:483
  59.1 0.7 collective-permute-start.5
  59.8 2.7 %collective-permute-start.6 = (bf16[2,64,1152]{2,1,0:T(8,128)(2,1)}, bf16[2,64,1152]{2,1,0:T(8,128)(2,1)S(1)}, u32[]{:S(2)}, u32[]{:S(2)}) collective-permute-start(bf16[2,64,1152]{2,1,0:T(8,128)(2,1)} %bitcast.58), channel_id=1, source_target_pairs={{0,3},{1,0},{2,1},{3,2},{4,7},{5,4},{6,5},{7,6},{8,11},{9,8},{10,9... | collective-permute-start | bytes 884744 | tf_op jit(solution)/shard_map/ppermute | solution.py:375
  62.5 2.5 %convolution_convert_fusion.3 = bf16[256,2432]{1,0:T(8,128)(2,1)S(1)} fusion(bf16[256,512]{1,0:T(8,128)(2,1)S(1)} %get-tuple-element.71, bf16[512,8192]{1,0:T(8,128)(2,1)} %weight.1), kind=kOutput, calls=%fused_computation.4 | convolution fusion | flops 638156800 | bytes 3997696 | tf_op jit(solution)/shard_map/dot_general | solution.py:483
  65.1 1.5 %collective-permute-done = bf16[2,64,1152]{2,1,0:T(8,128)(2,1)S(1)} collective-permute-done((bf16[2,64,1152]{2,1,0:T(8,128)(2,1)S(1)}, bf16[2,64,1152]{2,1,0:T(8,128)(2,1)S(1)}, u32[]{:S(2)}, u32[]{:S(2)}) %collective-permute-start) | collective-permute-done | bytes 294944 | tf_op jit(solution)/shard_map/ppermute | solution.py:375
  66.6 0.2 add_convert_fusion.5
  66.8 0.1 collective-permute-start.2
  67.0 3.3 %collective-permute-start.3 = (bf16[2,64,2304]{2,1,0:T(8,128)(2,1)S(1)}, bf16[2,64,2304]{2,1,0:T(8,128)(2,1)S(1)}, u32[]{:S(2)}, u32[]{:S(2)}) collective-permute-start(bf16[2,64,2304]{2,1,0:T(8,128)(2,1)S(1)} %pad_maximum_fusion.3), channel_id=1, source_target_pairs={{0,3},{1,0},{2,1},{3,2},{4,7},{5,4},{6,5},{7,6},{8,11},{9,8},{10,9... | collective-permute-start | bytes 1769480 | tf_op jit(solution)/shard_map/ppermute | solution.py:375
  70.3 2.6 %collective-permute-done.5 = bf16[2,64,1152]{2,1,0:T(8,128)(2,1)S(1)} collective-permute-done((bf16[2,64,1152]{2,1,0:T(8,128)(2,1)}, bf16[2,64,1152]{2,1,0:T(8,128)(2,1)S(1)}, u32[]{:S(2)}, u32[]{:S(2)}) %collective-permute-start.5) | collective-permute-done | bytes 294944 | tf_op jit(solution)/shard_map/ppermute | solution.py:375
  72.9 0.8 convolution_convert_fusion.2
  73.9 1.0 collective-permute-start.9
  74.9 0.1 add_convert_fusion.4
  75.1 1.7 %collective-permute-start.8 = (bf16[2,64,2304]{2,1,0:T(8,128)(2,1)S(1)}, bf16[2,64,2304]{2,1,0:T(8,128)(2,1)S(1)}, u32[]{:S(2)}, u32[]{:S(2)}) collective-permute-start(bf16[2,64,2304]{2,1,0:T(8,128)(2,1)S(1)} %pad_maximum_fusion.5), channel_id=1, source_target_pairs={{0,3},{1,0},{2,1},{3,2},{4,7},{5,4},{6,5},{7,6},{8,11},{9,8},{10,9... | collective-permute-start | bytes 1769480 | tf_op jit(solution)/shard_map/ppermute | solution.py:375
  76.9 0.5 collective-permute-start.7
  77.3 0.8 convolution_convert_fusion
  78.1 1.1 convolution_convert_fusion.1
  79.2 6.3 %collective-permute-done.2 = bf16[2,64,2304]{2,1,0:T(8,128)(2,1)S(1)} collective-permute-done((bf16[2,64,2304]{2,1,0:T(8,128)(2,1)S(1)}, bf16[2,64,2304]{2,1,0:T(8,128)(2,1)S(1)}, u32[]{:S(2)}, u32[]{:S(2)}) %collective-permute-start.2) | collective-permute-done | bytes 589856 | tf_op jit(solution)/shard_map/ppermute | solution.py:375
  85.5 9.2 %collective-permute-done.8 = bf16[2,64,2304]{2,1,0:T(8,128)(2,1)S(1)} collective-permute-done((bf16[2,64,2304]{2,1,0:T(8,128)(2,1)S(1)}, bf16[2,64,2304]{2,1,0:T(8,128)(2,1)S(1)}, u32[]{:S(2)}, u32[]{:S(2)}) %collective-permute-start.8) | collective-permute-done | bytes 589856 | tf_op jit(solution)/shard_map/ppermute | solution.py:375
  94.7 3.1 %collective-permute-done.7 = bf16[2,64,2304]{2,1,0:T(8,128)(2,1)S(1)} collective-permute-done((bf16[2,64,2304]{2,1,0:T(8,128)(2,1)S(1)}, bf16[2,64,2304]{2,1,0:T(8,128)(2,1)S(1)}, u32[]{:S(2)}, u32[]{:S(2)}) %collective-permute-start.7) | collective-permute-done | bytes 589856 | tf_op jit(solution)/shard_map/ppermute | solution.py:375
  97.7 4.8 %collective-permute-done.9 = bf16[4,64,2432]{2,1,0:T(8,128)(2,1)S(1)} collective-permute-done((bf16[4,64,2432]{2,1,0:T(8,128)(2,1)S(1)}, bf16[4,64,2432]{2,1,0:T(8,128)(2,1)S(1)}, u32[]{:S(2)}, u32[]{:S(2)}) %collective-permute-start.9) | collective-permute-done | bytes 1245216 | tf_op jit(solution)/shard_map/ppermute | solution.py:378
  102.5 0.4 add_convert_fusion
  103.0 0.1 slice_bitcast_fusion.2
  103.1 1.7 %collective-permute-start.13 = (bf16[64,1792]{1,0:T(8,128)(2,1)S(1)}, bf16[64,1792]{1,0:T(8,128)(2,1)S(1)}, u32[]{:S(2)}, u32[]{:S(2)}) collective-permute-start(bf16[64,1792]{1,0:T(8,128)(2,1)S(1)} %get-tuple-element.121), channel_id=1, source_target_pairs={{0,3},{1,0},{2,1},{3,2},{4,7},{5,4},{6,5},{7,6},{8,11},{9,8},{10,9... | collective-permute-start | bytes 688136 | tf_op jit(solution)/shard_map/ppermute | solution.py:375
  104.8 0.4 add_convert_fusion.2
  105.3 1.3 collective-permute-start.10
  106.6 0.7 collective-permute-start.11
  107.3 1.9 %collective-permute-done.13 = bf16[64,1792]{1,0:T(8,128)(2,1)S(1)} collective-permute-done((bf16[64,1792]{1,0:T(8,128)(2,1)S(1)}, bf16[64,1792]{1,0:T(8,128)(2,1)S(1)}, u32[]{:S(2)}, u32[]{:S(2)}) %collective-permute-start.13) | collective-permute-done | bytes 229408 | tf_op jit(solution)/shard_map/ppermute | solution.py:375
  109.3 2.9 %collective-permute-start.14 = (bf16[64,3584]{1,0:T(8,128)(2,1)S(1)}, bf16[64,3584]{1,0:T(8,128)(2,1)S(1)}, u32[]{:S(2)}, u32[]{:S(2)}) collective-permute-start(bf16[64,3584]{1,0:T(8,128)(2,1)S(1)} %pad_maximum_fusion.7), channel_id=1, source_target_pairs={{0,3},{1,0},{2,1},{3,2},{4,7},{5,4},{6,5},{7,6},{8,11},{9,8},{10,9... | collective-permute-start | bytes 1376264 | tf_op jit(solution)/shard_map/ppermute | solution.py:375
  112.2 1.9 %collective-permute-done.11 = bf16[64,1792]{1,0:T(8,128)(2,1)S(1)} collective-permute-done((bf16[64,1792]{1,0:T(8,128)(2,1)S(1)}, bf16[64,1792]{1,0:T(8,128)(2,1)S(1)}, u32[]{:S(2)}, u32[]{:S(2)}) %collective-permute-start.11) | collective-permute-done | bytes 229408 | tf_op jit(solution)/shard_map/ppermute | solution.py:375
  114.2 0.1 collective-permute-start.12
  114.3 4.5 %collective-permute-done.10 = bf16[64,4608]{1,0:T(8,128)(2,1)S(1)} collective-permute-done((bf16[64,4608]{1,0:T(8,128)(2,1)S(1)}, bf16[64,4608]{1,0:T(8,128)(2,1)S(1)}, u32[]{:S(2)}, u32[]{:S(2)}) %collective-permute-start.10) | collective-permute-done | bytes 589856 | tf_op jit(solution)/shard_map/ppermute | solution.py:378
  118.8 0.1 fusion.5
  119.0 0.5 collective-permute-done.14
  119.5 5.3 %collective-permute-done.12 = bf16[64,3584]{1,0:T(8,128)(2,1)S(1)} collective-permute-done((bf16[64,3584]{1,0:T(8,128)(2,1)S(1)}, bf16[64,3584]{1,0:T(8,128)(2,1)S(1)}, u32[]{:S(2)}, u32[]{:S(2)}) %collective-permute-start.12) | collective-permute-done | bytes 458784 | tf_op jit(solution)/shard_map/ppermute | solution.py:375
  124.8 0.2 fusion.7
  125.0 1.0 pad_maximum_fusion
  (34 shorter events, 0.8 us)
Async XLA Ops:
  2.3 23.1 %all-to-all-start = ((bf16[32,16,256]{2,1,0:T(8,128)(2,1)}), bf16[32,16,256]{2,1,0:T(8,128)(2,1)S(1)}, u32[]{:S(2)}, u32[]{:S(2)}) async-start(bf16[32,16,256]{2,1,0:T(8,128)(2,1)} %bitcast.55), calls=%async_computation | async-start | bytes 524288 | tf_op jit(solution)/shard_map/all_to_all | solution.py:389
  13.9 11.5 %copy-start.2 = (s32[256]{0:T(256)S(1)}, s32[256]{0:T(256)}, u32[]{:S(2)}) copy-start(s32[256]{0:T(256)} %table.1) | copy-start | bytes 3076
  13.9 11.5 %copy-start.3 = (s32[256]{0:T(256)S(1)}, s32[256]{0:T(256)}, u32[]{:S(2)}) copy-start(s32[256]{0:T(256)} %lengths.1) | copy-start | bytes 3076
  30.1 15.6 %all-to-all-start.1 = ((bf16[32,16,128]{2,1,0:T(8,128)(2,1)}), bf16[32,16,128]{2,1,0:T(8,128)(2,1)S(1)}, u32[]{:S(2)}, u32[]{:S(2)}) async-start(bf16[32,16,128]{2,1,0:T(8,128)(2,1)} %bitcast.4), calls=%async_computation.1 | async-start | bytes 262144 | tf_op jit(solution)/shard_map/all_to_all | solution.py:438
  36.4 9.3 %copy-start = (bf16[256,512]{1,0:T(8,128)(2,1)S(1)}, bf16[256,512]{1,0:T(8,128)(2,1)}, u32[]{:S(2)}) copy-start(bf16[256,512]{1,0:T(8,128)(2,1)} %get-tuple-element.58.first) | copy-start | bytes 786436
  45.7 1.0 copy-start.1
  46.6 26.2 %slice-start = ((s8[8388608]{0:T(1024)(128)(4,1)}), s8[4194304]{0:T(1024)(128)(4,1)S(1)}, s32[]{:S(2)}) async-start(s8[8388608]{0:T(1024)(128)(4,1)} %bitcast.45), calls=%async_computation.2 | async-start | bytes 8388608
  52.4 12.6 %collective-permute-start.1 = (bf16[2,64,1152]{2,1,0:T(8,128)(2,1)}, bf16[2,64,1152]{2,1,0:T(8,128)(2,1)S(1)}, u32[]{:S(2)}, u32[]{:S(2)}) collective-permute-start(bf16[2,64,1152]{2,1,0:T(8,128)(2,1)} %bitcast.60), channel_id=1, source_target_pairs={{0,3},{1,0},{2,1},{3,2},{4,7},{5,4},{6,5},{7,6},{8,11},{9,8},{10,9... | collective-permute-start | bytes 884744 | tf_op jit(solution)/shard_map/ppermute | solution.py:375
  55.5 11.0 %collective-permute-start = (bf16[2,64,1152]{2,1,0:T(8,128)(2,1)S(1)}, bf16[2,64,1152]{2,1,0:T(8,128)(2,1)S(1)}, u32[]{:S(2)}, u32[]{:S(2)}) collective-permute-start(bf16[2,64,1152]{2,1,0:T(8,128)(2,1)S(1)} %bitcast.44), channel_id=1, source_target_pairs={{0,1},{1,2},{2,3},{3,0},{4,5},{5,6},{6,7},{7,4},{8,9},{9,10},{10,1... | collective-permute-start | bytes 884744 | tf_op jit(solution)/shard_map/ppermute | solution.py:375
  55.5 17.3 %collective-permute-start.4 = (bf16[4,64,1152]{2,1,0:T(8,128)(2,1)}, bf16[4,64,1152]{2,1,0:T(8,128)(2,1)S(1)}, u32[]{:S(2)}, u32[]{:S(2)}) collective-permute-start(bf16[4,64,1152]{2,1,0:T(8,128)(2,1)} %bitcast.57), channel_id=1, source_target_pairs={{0,4},{1,5},{2,6},{3,7},{4,0},{5,1},{6,2},{7,3},{8,12},{9,13},{10,... | collective-permute-start | bytes 1769480 | tf_op jit(solution)/shard_map/ppermute | solution.py:378
  56.5 16.4 %slice-start.1 = ((s8[8388608]{0:T(1024)(128)(4,1)}), s8[4194304]{0:T(1024)(128)(4,1)S(1)}, s32[]{:S(2)}) async-start(s8[8388608]{0:T(1024)(128)(4,1)} %bitcast.45), calls=%async_computation.3 | async-start | bytes 8388608
  59.1 13.8 %collective-permute-start.5 = (bf16[2,64,1152]{2,1,0:T(8,128)(2,1)}, bf16[2,64,1152]{2,1,0:T(8,128)(2,1)S(1)}, u32[]{:S(2)}, u32[]{:S(2)}) collective-permute-start(bf16[2,64,1152]{2,1,0:T(8,128)(2,1)} %bitcast.59), channel_id=1, source_target_pairs={{0,1},{1,2},{2,3},{3,0},{4,5},{5,6},{6,7},{7,4},{8,9},{9,10},{10,1... | collective-permute-start | bytes 884744 | tf_op jit(solution)/shard_map/ppermute | solution.py:375
  59.8 13.1 %collective-permute-start.6 = (bf16[2,64,1152]{2,1,0:T(8,128)(2,1)}, bf16[2,64,1152]{2,1,0:T(8,128)(2,1)S(1)}, u32[]{:S(2)}, u32[]{:S(2)}) collective-permute-start(bf16[2,64,1152]{2,1,0:T(8,128)(2,1)} %bitcast.58), channel_id=1, source_target_pairs={{0,3},{1,0},{2,1},{3,2},{4,7},{5,4},{6,5},{7,6},{8,11},{9,8},{10,9... | collective-permute-start | bytes 884744 | tf_op jit(solution)/shard_map/ppermute | solution.py:375
  66.8 18.7 %collective-permute-start.2 = (bf16[2,64,2304]{2,1,0:T(8,128)(2,1)S(1)}, bf16[2,64,2304]{2,1,0:T(8,128)(2,1)S(1)}, u32[]{:S(2)}, u32[]{:S(2)}) collective-permute-start(bf16[2,64,2304]{2,1,0:T(8,128)(2,1)S(1)} %pad_maximum_fusion.2), channel_id=1, source_target_pairs={{0,1},{1,2},{2,3},{3,0},{4,5},{5,6},{6,7},{7,4},{8,9},{9,10},{10,1... | collective-permute-start | bytes 1769480 | tf_op jit(solution)/shard_map/ppermute | solution.py:375
  67.0 18.5 %collective-permute-start.3 = (bf16[2,64,2304]{2,1,0:T(8,128)(2,1)S(1)}, bf16[2,64,2304]{2,1,0:T(8,128)(2,1)S(1)}, u32[]{:S(2)}, u32[]{:S(2)}) collective-permute-start(bf16[2,64,2304]{2,1,0:T(8,128)(2,1)S(1)} %pad_maximum_fusion.3), channel_id=1, source_target_pairs={{0,3},{1,0},{2,1},{3,2},{4,7},{5,4},{6,5},{7,6},{8,11},{9,8},{10,9... | collective-permute-start | bytes 1769480 | tf_op jit(solution)/shard_map/ppermute | solution.py:375
  73.9 28.7 %collective-permute-start.9 = (bf16[4,64,2432]{2,1,0:T(8,128)(2,1)S(1)}, bf16[4,64,2432]{2,1,0:T(8,128)(2,1)S(1)}, u32[]{:S(2)}, u32[]{:S(2)}) collective-permute-start(bf16[4,64,2432]{2,1,0:T(8,128)(2,1)S(1)} %bitcast.56), channel_id=1, source_target_pairs={{0,4},{1,5},{2,6},{3,7},{4,0},{5,1},{6,2},{7,3},{8,12},{9,13},{10,... | collective-permute-start | bytes 3735560 | tf_op jit(solution)/shard_map/ppermute | solution.py:378
  75.1 19.6 %collective-permute-start.8 = (bf16[2,64,2304]{2,1,0:T(8,128)(2,1)S(1)}, bf16[2,64,2304]{2,1,0:T(8,128)(2,1)S(1)}, u32[]{:S(2)}, u32[]{:S(2)}) collective-permute-start(bf16[2,64,2304]{2,1,0:T(8,128)(2,1)S(1)} %pad_maximum_fusion.5), channel_id=1, source_target_pairs={{0,3},{1,0},{2,1},{3,2},{4,7},{5,4},{6,5},{7,6},{8,11},{9,8},{10,9... | collective-permute-start | bytes 1769480 | tf_op jit(solution)/shard_map/ppermute | solution.py:375
  76.9 20.9 %collective-permute-start.7 = (bf16[2,64,2304]{2,1,0:T(8,128)(2,1)S(1)}, bf16[2,64,2304]{2,1,0:T(8,128)(2,1)S(1)}, u32[]{:S(2)}, u32[]{:S(2)}) collective-permute-start(bf16[2,64,2304]{2,1,0:T(8,128)(2,1)S(1)} %pad_maximum_fusion.4), channel_id=1, source_target_pairs={{0,1},{1,2},{2,3},{3,0},{4,5},{5,6},{6,7},{7,4},{8,9},{9,10},{10,1... | collective-permute-start | bytes 1769480 | tf_op jit(solution)/shard_map/ppermute | solution.py:375
  103.1 6.1 %collective-permute-start.13 = (bf16[64,1792]{1,0:T(8,128)(2,1)S(1)}, bf16[64,1792]{1,0:T(8,128)(2,1)S(1)}, u32[]{:S(2)}, u32[]{:S(2)}) collective-permute-start(bf16[64,1792]{1,0:T(8,128)(2,1)S(1)} %get-tuple-element.121), channel_id=1, source_target_pairs={{0,3},{1,0},{2,1},{3,2},{4,7},{5,4},{6,5},{7,6},{8,11},{9,8},{10,9... | collective-permute-start | bytes 688136 | tf_op jit(solution)/shard_map/ppermute | solution.py:375
  105.3 13.5 %collective-permute-start.10 = (bf16[64,4608]{1,0:T(8,128)(2,1)S(1)}, bf16[64,4608]{1,0:T(8,128)(2,1)S(1)}, u32[]{:S(2)}, u32[]{:S(2)}) collective-permute-start(bf16[64,4608]{1,0:T(8,128)(2,1)S(1)} %fusion.10), channel_id=1, source_target_pairs={{0,4},{1,5},{2,6},{3,7},{4,0},{5,1},{6,2},{7,3},{8,12},{9,13},{10,... | collective-permute-start | bytes 1769480 | tf_op jit(solution)/shard_map/ppermute | solution.py:378
  106.6 7.5 %collective-permute-start.11 = (bf16[64,1792]{1,0:T(8,128)(2,1)S(1)}, bf16[64,1792]{1,0:T(8,128)(2,1)S(1)}, u32[]{:S(2)}, u32[]{:S(2)}) collective-permute-start(bf16[64,1792]{1,0:T(8,128)(2,1)S(1)} %get-tuple-element.120), channel_id=1, source_target_pairs={{0,1},{1,2},{2,3},{3,0},{4,5},{5,6},{6,7},{7,4},{8,9},{9,10},{10,1... | collective-permute-start | bytes 688136 | tf_op jit(solution)/shard_map/ppermute | solution.py:375
  109.3 10.2 %collective-permute-start.14 = (bf16[64,3584]{1,0:T(8,128)(2,1)S(1)}, bf16[64,3584]{1,0:T(8,128)(2,1)S(1)}, u32[]{:S(2)}, u32[]{:S(2)}) collective-permute-start(bf16[64,3584]{1,0:T(8,128)(2,1)S(1)} %pad_maximum_fusion.7), channel_id=1, source_target_pairs={{0,3},{1,0},{2,1},{3,2},{4,7},{5,4},{6,5},{7,6},{8,11},{9,8},{10,9... | collective-permute-start | bytes 1376264 | tf_op jit(solution)/shard_map/ppermute | solution.py:375
  114.2 10.6 %collective-permute-start.12 = (bf16[64,3584]{1,0:T(8,128)(2,1)S(1)}, bf16[64,3584]{1,0:T(8,128)(2,1)S(1)}, u32[]{:S(2)}, u32[]{:S(2)}) collective-permute-start(bf16[64,3584]{1,0:T(8,128)(2,1)S(1)} %pad_maximum_fusion.6), channel_id=1, source_target_pairs={{0,1},{1,2},{2,3},{3,0},{4,5},{5,6},{6,7},{7,4},{8,9},{9,10},{10,1... | collective-permute-start | bytes 1376264 | tf_op jit(solution)/shard_map/ppermute | solution.py:375

commit v6 on v5

--- a/solution.py
+++ b/solution.py
@@ -15,7 +15,7 @@
 NEG = -1e30
 COLS_Y = 4608
 PIECE = 384
-EARLY = 1152
+EARLY = 1536
 FIRST = 4
 LIMIT = 54
 LESS = 52

time: 126 us -> 126 us (level)
  waiting for transfers between devices: 43.6 us -> 40.5 us
  starting transfers between devices: 38.6 us -> 40.9 us
    ppermute x12, waiting for transfers between devices: 32.2 us -> 28.4 us  [y_step(): lax.ppermute(x, 'tp', [(t, t // 4 * 4 + (t + step) % 4) for t in range(tp...]
    ppermute x12, starting transfers between devices: 17.5 us -> 19.7 us  [y_step(): lax.ppermute(x, 'tp', [(t, t // 4 * 4 + (t + step) % 4) for t in range(tp...]
  transfers between devices with their start and end apart: 17 -> 17, of which waited for: 13 -> 14; matrix products, arithmetic and copies ran while one was open for 7% -> 7% of each run, Pallas kernels for 15% -> 15%
where the time goes in v6:
time: 126 us; the launch traced here: 125 us
  starting transfers between devices  40.9 us (32%)
  waiting for transfers between devices  40.5 us (32%)
  Pallas kernels  31.7 us (25%)
  matrix products  7.58 us (6%)
  other arithmetic  2.98 us (2%)
  local copies, waits for them, and re-layouts  1.31 us (1%)
    ppermute x12, waiting for transfers between devices, y_step(): lax.ppermute(x, 'tp', [(t, t // 4 * 4 + (t + step) % 4) for t in range(tp...  28.4 us
    ppermute x12, starting transfers between devices, y_step(): lax.ppermute(x, 'tp', [(t, t // 4 * 4 + (t + step) % 4) for t in range(tp...  19.7 us
    pallas_call x2, Pallas kernels, attend(): pl.pallas_call(functools.partial(local_kernel, half=half, decode_rows=dec...  18.6 us
    all_to_all x1, starting transfers between devices, on_device(): lax.all_to_all(parcel, 'group', split_axis=0, concat_axis=0, tiled=True)  11.6 us
    ppermute x3, waiting for transfers between devices, z_swap(): lax.ppermute(x, 'tp', [(t, (t + 4) % tp_count) for t in range(tp_count)])  10 us
    dot_general x5, matrix products, products(): part = jnp.dot(given[name], weight, preferred_element_type=F32).astype(BF)  7.58 us
    all_to_all x1, starting transfers between devices, on_device(): lax.all_to_all(handed, 'group', split_axis=0, concat_axis=0, tiled=True)  6.29 us
    pallas_call x1, Pallas kernels, on_device(): pl.pallas_call(functools.partial(front_kernel, half=half, decode_rows=dec...  6.08 us
  transfers between devices with their start and end apart: 17, of which 14 were waited for; matrix products, arithmetic and copies ran while one was open for 7% of the time, Pallas kernels for 15%

profile of v6, /device:TPU:2, one launch (start us, length us, event | category | flops | bytes accessed | tf_op | source)
XLA Modules:
  0.0 125.3 jit_solution(7883598613937594496)
XLA Ops:
  0.0 2.3 %pick_rows.1 = bf16[512,256]{1,0:T(8,128)(2,1)} custom-call(s32[1,256]{1,0:T(1,128)} %bitcast.42, bf16[512,512]{1,0:T(8,128)(2,1)} %refs_0_.3, bf16[512,256]{1,0:T(8,128)(2,1)} %refs_1_.1), custom_call_target="tpu_custom_call" | custom-call | tf_op jit(solution)/shard_map/pick_rows/pallas_call | solution.py:381
  2.3 11.6 %all-to-all-start = ((bf16[32,16,256]{2,1,0:T(8,128)(2,1)}), bf16[32,16,256]{2,1,0:T(8,128)(2,1)S(1)}, u32[]{:S(2)}, u32[]{:S(2)}) async-start(bf16[32,16,256]{2,1,0:T(8,128)(2,1)} %bitcast.55), calls=%async_computation | async-start | bytes 524288 | tf_op jit(solution)/shard_map/all_to_all | solution.py:389
  13.9 10.9 %local_attention.2 = (bf16[256,512]{1,0:T(8,128)(2,1)}, bf16[96,64,256]{2,1,0:T(8,128)(2,1)}) custom-call(s32[16]{0:T(128)} %prefix_len.3, s32[2048]{0:T(1024)} %resident_len.3, s32[256]{0:T(256)} %table.1, s32[6,256]{1,0:T(8,128)} %bitcast.61, bf16[512,512]{1,0:T(8,128)(2,1)} %refs_0_.3, bf16[512,256]{1,0:T(8,128)(2,1)} %refs_1_.1, ...), custom_call_target="tpu_custom_call" | custom-call | flops 4294967296 | bytes 5242880 | tf_op jit(solution)/shard_map/local_attention/pallas_call | solution.py:395
  24.9 0.5 all-to-all-done
  25.4 4.7 %handed_attention.1 = bf16[512,128]{1,0:T(8,128)(2,1)} custom-call(s32[256]{0:T(256)S(1)} %copy-done.2, s32[256]{0:T(256)S(1)} %copy-done.3, bf16[96,64,256]{2,1,0:T(8,128)(2,1)} %get-tuple-element.59.all_pages, bf16[512,256]{1,0:T(8,128)(2,1)S(1)} %bitcast.40), custom_call_target="tpu_custom_call" | custom-call | tf_op jit(solution)/shard_map/handed_attention/pallas_call | solution.py:425
  30.1 6.3 %all-to-all-start.1 = ((bf16[32,16,128]{2,1,0:T(8,128)(2,1)}), bf16[32,16,128]{2,1,0:T(8,128)(2,1)S(1)}, u32[]{:S(2)}, u32[]{:S(2)}) async-start(bf16[32,16,128]{2,1,0:T(8,128)(2,1)} %bitcast.4), calls=%async_computation.1 | async-start | bytes 262144 | tf_op jit(solution)/shard_map/all_to_all | solution.py:438
  36.4 7.7 %local_attention.3.second = bf16[256,512]{1,0:T(8,128)(2,1)} custom-call(s32[16]{0:T(128)} %prefix_len.3, s32[2048]{0:T(1024)} %resident_len.3, bf16[512,512]{1,0:T(8,128)(2,1)} %refs_0_.3, bf16[512,256]{1,0:T(8,128)(2,1)} %refs_1_.1, bf16[120,64,256]{2,1,0:T(8,128)(2,1)} %refs_2_.3), custom_call_target="tpu_custom_call" | custom-call | flops 4294967296 | bytes 5242880 | tf_op jit(solution)/shard_map/local_attention/pallas_call | solution.py:395
  44.1 1.6 %all-to-all-done.1 = bf16[32,16,128]{2,1,0:T(8,128)(2,1)S(1)} async-done(((bf16[32,16,128]{2,1,0:T(8,128)(2,1)}), bf16[32,16,128]{2,1,0:T(8,128)(2,1)S(1)}, u32[]{:S(2)}, u32[]{:S(2)}) %all-to-all-start.1) | async-done | bytes 131104 | tf_op jit(solution)/shard_map/all_to_all | solution.py:438
  45.7 0.9 copy-done.1
  46.7 6.1 %front_products.1 = (bf16[256,1536]{1,0:T(8,128)(2,1)}, bf16[128,1152]{1,0:T(8,128)(2,1)S(1)}, bf16[128,1152]{1,0:T(8,128)(2,1)}, bf16[128,1152]{1,0:T(8,128)(2,...) custom-call(s32[1,256]{1,0:T(1,128)S(1)} %bitcast.43, ...), custom_call_target="tpu_custom_call" | custom-call | tf_op jit(solution)/shard_map/front_products/pallas_call | solution.py:443
  52.7 3.1 %collective-permute-start.1 = (bf16[2,64,1152]{2,1,0:T(8,128)(2,1)}, bf16[2,64,1152]{2,1,0:T(8,128)(2,1)S(1)}, u32[]{:S(2)}, u32[]{:S(2)}) collective-permute-start(bf16[2,64,1152]{2,1,0:T(8,128)(2,1)} %bitcast.60), channel_id=1, source_target_pairs={{0,3},{1,0},{2,1},{3,2},{4,7},{5,4},{6,5},{7,6},{8,11},{9,8},{10,9... | collective-permute-start | bytes 884744 | tf_op jit(solution)/shard_map/ppermute | solution.py:375
  55.8 1.0 collective-permute-start.4
  56.8 2.6 %convolution_convert_fusion.3 = bf16[256,2304]{1,0:T(8,128)(2,1)S(1)} fusion(bf16[256,512]{1,0:T(8,128)(2,1)S(1)} %get-tuple-element.89, bf16[512,8192]{1,0:T(8,128)(2,1)} %weight.1), kind=kOutput, calls=%fused_computation.4 | convolution fusion | flops 604569600 | bytes 3801088 | tf_op jit(solution)/shard_map/dot_general | solution.py:483
  59.4 0.7 collective-permute-start.5
  60.1 2.7 %collective-permute-start.6 = (bf16[2,64,1152]{2,1,0:T(8,128)(2,1)}, bf16[2,64,1152]{2,1,0:T(8,128)(2,1)S(1)}, u32[]{:S(2)}, u32[]{:S(2)}) collective-permute-start(bf16[2,64,1152]{2,1,0:T(8,128)(2,1)} %bitcast.58), channel_id=1, source_target_pairs={{0,3},{1,0},{2,1},{3,2},{4,7},{5,4},{6,5},{7,6},{8,11},{9,8},{10,9... | collective-permute-start | bytes 884744 | tf_op jit(solution)/shard_map/ppermute | solution.py:375
  62.8 2.3 %convolution_convert_fusion.4 = bf16[256,2048]{1,0:T(8,128)(2,1)S(1)} fusion(bf16[256,512]{1,0:T(8,128)(2,1)S(1)} %get-tuple-element.71, bf16[512,8192]{1,0:T(8,128)(2,1)} %weight.1), kind=kOutput, calls=%fused_computation.7 | convolution fusion | flops 537395200 | bytes 3407872 | tf_op jit(solution)/shard_map/dot_general | solution.py:483
  65.1 1.7 %collective-permute-done = bf16[2,64,1152]{2,1,0:T(8,128)(2,1)S(1)} collective-permute-done((bf16[2,64,1152]{2,1,0:T(8,128)(2,1)S(1)}, bf16[2,64,1152]{2,1,0:T(8,128)(2,1)S(1)}, u32[]{:S(2)}, u32[]{:S(2)}) %collective-permute-start) | collective-permute-done | bytes 294944 | tf_op jit(solution)/shard_map/ppermute | solution.py:375
  66.9 0.1 add_convert_fusion.5
  67.1 0.1 collective-permute-start.2
  67.3 3.3 %collective-permute-start.3 = (bf16[2,64,2304]{2,1,0:T(8,128)(2,1)S(1)}, bf16[2,64,2304]{2,1,0:T(8,128)(2,1)S(1)}, u32[]{:S(2)}, u32[]{:S(2)}) collective-permute-start(bf16[2,64,2304]{2,1,0:T(8,128)(2,1)S(1)} %pad_maximum_fusion.3), channel_id=1, source_target_pairs={{0,3},{1,0},{2,1},{3,2},{4,7},{5,4},{6,5},{7,6},{8,11},{9,8},{10,9... | collective-permute-start | bytes 1769480 | tf_op jit(solution)/shard_map/ppermute | solution.py:375
  70.5 2.6 %collective-permute-done.5 = bf16[2,64,1152]{2,1,0:T(8,128)(2,1)S(1)} collective-permute-done((bf16[2,64,1152]{2,1,0:T(8,128)(2,1)}, bf16[2,64,1152]{2,1,0:T(8,128)(2,1)S(1)}, u32[]{:S(2)}, u32[]{:S(2)}) %collective-permute-start.5) | collective-permute-done | bytes 294944 | tf_op jit(solution)/shard_map/ppermute | solution.py:375
  73.2 2.8 %collective-permute-done.4 = bf16[4,64,1536]{2,1,0:T(8,128)(2,1)S(1)} collective-permute-done((bf16[4,64,1536]{2,1,0:T(8,128)(2,1)}, bf16[4,64,1536]{2,1,0:T(8,128)(2,1)S(1)}, u32[]{:S(2)}, u32[]{:S(2)}) %collective-permute-start.4) | collective-permute-done | bytes 786464 | tf_op jit(solution)/shard_map/ppermute | solution.py:378
  76.0 1.1 collective-permute-start.9
  77.0 0.8 convolution_convert_fusion.2
  78.0 0.1 add_convert_fusion.4
  78.2 3.0 %collective-permute-start.8 = (bf16[2,64,2304]{2,1,0:T(8,128)(2,1)S(1)}, bf16[2,64,2304]{2,1,0:T(8,128)(2,1)S(1)}, u32[]{:S(2)}, u32[]{:S(2)}) collective-permute-start(bf16[2,64,2304]{2,1,0:T(8,128)(2,1)S(1)} %pad_maximum_fusion.5), channel_id=1, source_target_pairs={{0,3},{1,0},{2,1},{3,2},{4,7},{5,4},{6,5},{7,6},{8,11},{9,8},{10,9... | collective-permute-start | bytes 1769480 | tf_op jit(solution)/shard_map/ppermute | solution.py:375
  81.4 0.8 convolution_convert_fusion
  82.2 1.1 convolution_convert_fusion.1
  83.3 2.5 %collective-permute-done.2 = bf16[2,64,2304]{2,1,0:T(8,128)(2,1)S(1)} collective-permute-done((bf16[2,64,2304]{2,1,0:T(8,128)(2,1)S(1)}, bf16[2,64,2304]{2,1,0:T(8,128)(2,1)S(1)}, u32[]{:S(2)}, u32[]{:S(2)}) %collective-permute-start.2) | collective-permute-done | bytes 589856 | tf_op jit(solution)/shard_map/ppermute | solution.py:375
  85.8 9.2 %collective-permute-done.8 = bf16[2,64,2304]{2,1,0:T(8,128)(2,1)S(1)} collective-permute-done((bf16[2,64,2304]{2,1,0:T(8,128)(2,1)S(1)}, bf16[2,64,2304]{2,1,0:T(8,128)(2,1)S(1)}, u32[]{:S(2)}, u32[]{:S(2)}) %collective-permute-start.8) | collective-permute-done | bytes 589856 | tf_op jit(solution)/shard_map/ppermute | solution.py:375
  95.0 3.1 %collective-permute-done.7 = bf16[2,64,2304]{2,1,0:T(8,128)(2,1)S(1)} collective-permute-done((bf16[2,64,2304]{2,1,0:T(8,128)(2,1)S(1)}, bf16[2,64,2304]{2,1,0:T(8,128)(2,1)S(1)}, u32[]{:S(2)}, u32[]{:S(2)}) %collective-permute-start.7) | collective-permute-done | bytes 589856 | tf_op jit(solution)/shard_map/ppermute | solution.py:375
  98.1 2.7 %collective-permute-done.9 = bf16[4,64,2048]{2,1,0:T(8,128)(2,1)S(1)} collective-permute-done((bf16[4,64,2048]{2,1,0:T(8,128)(2,1)S(1)}, bf16[4,64,2048]{2,1,0:T(8,128)(2,1)S(1)}, u32[]{:S(2)}, u32[]{:S(2)}) %collective-permute-start.9) | collective-permute-done | bytes 1048608 | tf_op jit(solution)/shard_map/ppermute | solution.py:378
  100.8 0.5 add_convert_fusion
  101.2 0.1 slice_bitcast_fusion.2
  101.4 2.7 %collective-permute-start.13 = (bf16[64,1792]{1,0:T(8,128)(2,1)S(1)}, bf16[64,1792]{1,0:T(8,128)(2,1)S(1)}, u32[]{:S(2)}, u32[]{:S(2)}) collective-permute-start(bf16[64,1792]{1,0:T(8,128)(2,1)S(1)} %get-tuple-element.121), channel_id=1, source_target_pairs={{0,3},{1,0},{2,1},{3,2},{4,7},{5,4},{6,5},{7,6},{8,11},{9,8},{10,9... | collective-permute-start | bytes 688136 | tf_op jit(solution)/shard_map/ppermute | solution.py:375
  104.1 0.4 add_convert_fusion.2
  104.6 1.2 collective-permute-start.10
  105.9 0.3 collective-permute-start.11
  106.2 1.6 %collective-permute-done.13 = bf16[64,1792]{1,0:T(8,128)(2,1)S(1)} collective-permute-done((bf16[64,1792]{1,0:T(8,128)(2,1)S(1)}, bf16[64,1792]{1,0:T(8,128)(2,1)S(1)}, u32[]{:S(2)}, u32[]{:S(2)}) %collective-permute-start.13) | collective-permute-done | bytes 229408 | tf_op jit(solution)/shard_map/ppermute | solution.py:375
  107.9 3.6 %collective-permute-start.14 = (bf16[64,3584]{1,0:T(8,128)(2,1)S(1)}, bf16[64,3584]{1,0:T(8,128)(2,1)S(1)}, u32[]{:S(2)}, u32[]{:S(2)}) collective-permute-start(bf16[64,3584]{1,0:T(8,128)(2,1)S(1)} %pad_maximum_fusion.7), channel_id=1, source_target_pairs={{0,3},{1,0},{2,1},{3,2},{4,7},{5,4},{6,5},{7,6},{8,11},{9,8},{10,9... | collective-permute-start | bytes 1376264 | tf_op jit(solution)/shard_map/ppermute | solution.py:375
  111.5 1.9 %collective-permute-done.11 = bf16[64,1792]{1,0:T(8,128)(2,1)S(1)} collective-permute-done((bf16[64,1792]{1,0:T(8,128)(2,1)S(1)}, bf16[64,1792]{1,0:T(8,128)(2,1)S(1)}, u32[]{:S(2)}, u32[]{:S(2)}) %collective-permute-start.11) | collective-permute-done | bytes 229408 | tf_op jit(solution)/shard_map/ppermute | solution.py:375
  113.5 0.1 collective-permute-start.12
  113.6 4.5 %collective-permute-done.10 = bf16[64,4608]{1,0:T(8,128)(2,1)S(1)} collective-permute-done((bf16[64,4608]{1,0:T(8,128)(2,1)S(1)}, bf16[64,4608]{1,0:T(8,128)(2,1)S(1)}, u32[]{:S(2)}, u32[]{:S(2)}) %collective-permute-start.10) | collective-permute-done | bytes 589856 | tf_op jit(solution)/shard_map/ppermute | solution.py:378
  118.1 0.1 fusion.5
  118.2 0.5 collective-permute-done.14
  118.8 5.3 %collective-permute-done.12 = bf16[64,3584]{1,0:T(8,128)(2,1)S(1)} collective-permute-done((bf16[64,3584]{1,0:T(8,128)(2,1)S(1)}, bf16[64,3584]{1,0:T(8,128)(2,1)S(1)}, u32[]{:S(2)}, u32[]{:S(2)}) %collective-permute-start.12) | collective-permute-done | bytes 458784 | tf_op jit(solution)/shard_map/ppermute | solution.py:375
  124.1 0.2 fusion.7
  124.3 1.0 pad_maximum_fusion
  (34 shorter events, 0.8 us)
Async XLA Ops:
  2.3 23.1 %all-to-all-start = ((bf16[32,16,256]{2,1,0:T(8,128)(2,1)}), bf16[32,16,256]{2,1,0:T(8,128)(2,1)S(1)}, u32[]{:S(2)}, u32[]{:S(2)}) async-start(bf16[32,16,256]{2,1,0:T(8,128)(2,1)} %bitcast.55), calls=%async_computation | async-start | bytes 524288 | tf_op jit(solution)/shard_map/all_to_all | solution.py:389
  13.9 11.5 %copy-start.2 = (s32[256]{0:T(256)S(1)}, s32[256]{0:T(256)}, u32[]{:S(2)}) copy-start(s32[256]{0:T(256)} %table.1) | copy-start | bytes 3076
  13.9 11.5 %copy-start.3 = (s32[256]{0:T(256)S(1)}, s32[256]{0:T(256)}, u32[]{:S(2)}) copy-start(s32[256]{0:T(256)} %lengths.1) | copy-start | bytes 3076
  30.1 15.6 %all-to-all-start.1 = ((bf16[32,16,128]{2,1,0:T(8,128)(2,1)}), bf16[32,16,128]{2,1,0:T(8,128)(2,1)S(1)}, u32[]{:S(2)}, u32[]{:S(2)}) async-start(bf16[32,16,128]{2,1,0:T(8,128)(2,1)} %bitcast.4), calls=%async_computation.1 | async-start | bytes 262144 | tf_op jit(solution)/shard_map/all_to_all | solution.py:438
  36.4 9.3 %copy-start = (bf16[256,512]{1,0:T(8,128)(2,1)S(1)}, bf16[256,512]{1,0:T(8,128)(2,1)}, u32[]{:S(2)}) copy-start(bf16[256,512]{1,0:T(8,128)(2,1)} %get-tuple-element.58.first) | copy-start | bytes 786436
  45.7 1.0 copy-start.1
  46.6 30.4 %slice-start = ((s8[8388608]{0:T(1024)(128)(4,1)}), s8[4194304]{0:T(1024)(128)(4,1)S(1)}, s32[]{:S(2)}) async-start(s8[8388608]{0:T(1024)(128)(4,1)} %bitcast.45), calls=%async_computation.2 | async-start | bytes 8388608
  52.7 12.4 %collective-permute-start.1 = (bf16[2,64,1152]{2,1,0:T(8,128)(2,1)}, bf16[2,64,1152]{2,1,0:T(8,128)(2,1)S(1)}, u32[]{:S(2)}, u32[]{:S(2)}) collective-permute-start(bf16[2,64,1152]{2,1,0:T(8,128)(2,1)} %bitcast.60), channel_id=1, source_target_pairs={{0,3},{1,0},{2,1},{3,2},{4,7},{5,4},{6,5},{7,6},{8,11},{9,8},{10,9... | collective-permute-start | bytes 884744 | tf_op jit(solution)/shard_map/ppermute | solution.py:375
  55.8 11.0 %collective-permute-start = (bf16[2,64,1152]{2,1,0:T(8,128)(2,1)S(1)}, bf16[2,64,1152]{2,1,0:T(8,128)(2,1)S(1)}, u32[]{:S(2)}, u32[]{:S(2)}) collective-permute-start(bf16[2,64,1152]{2,1,0:T(8,128)(2,1)S(1)} %bitcast.44), channel_id=1, source_target_pairs={{0,1},{1,2},{2,3},{3,0},{4,5},{5,6},{6,7},{7,4},{8,9},{9,10},{10,1... | collective-permute-start | bytes 884744 | tf_op jit(solution)/shard_map/ppermute | solution.py:375
  55.8 20.1 %collective-permute-start.4 = (bf16[4,64,1536]{2,1,0:T(8,128)(2,1)}, bf16[4,64,1536]{2,1,0:T(8,128)(2,1)S(1)}, u32[]{:S(2)}, u32[]{:S(2)}) collective-permute-start(bf16[4,64,1536]{2,1,0:T(8,128)(2,1)} %bitcast.57), channel_id=1, source_target_pairs={{0,4},{1,5},{2,6},{3,7},{4,0},{5,1},{6,2},{7,3},{8,12},{9,13},{10,... | collective-permute-start | bytes 2359304 | tf_op jit(solution)/shard_map/ppermute | solution.py:378
  56.8 20.2 %slice-start.1 = ((s8[8388608]{0:T(1024)(128)(4,1)}), s8[4194304]{0:T(1024)(128)(4,1)S(1)}, s32[]{:S(2)}) async-start(s8[8388608]{0:T(1024)(128)(4,1)} %bitcast.45), calls=%async_computation.3 | async-start | bytes 8388608
  59.4 13.8 %collective-permute-start.5 = (bf16[2,64,1152]{2,1,0:T(8,128)(2,1)}, bf16[2,64,1152]{2,1,0:T(8,128)(2,1)S(1)}, u32[]{:S(2)}, u32[]{:S(2)}) collective-permute-start(bf16[2,64,1152]{2,1,0:T(8,128)(2,1)} %bitcast.59), channel_id=1, source_target_pairs={{0,1},{1,2},{2,3},{3,0},{4,5},{5,6},{6,7},{7,4},{8,9},{9,10},{10,1... | collective-permute-start | bytes 884744 | tf_op jit(solution)/shard_map/ppermute | solution.py:375
  60.1 13.1 %collective-permute-start.6 = (bf16[2,64,1152]{2,1,0:T(8,128)(2,1)}, bf16[2,64,1152]{2,1,0:T(8,128)(2,1)S(1)}, u32[]{:S(2)}, u32[]{:S(2)}) collective-permute-start(bf16[2,64,1152]{2,1,0:T(8,128)(2,1)} %bitcast.58), channel_id=1, source_target_pairs={{0,3},{1,0},{2,1},{3,2},{4,7},{5,4},{6,5},{7,6},{8,11},{9,8},{10,9... | collective-permute-start | bytes 884744 | tf_op jit(solution)/shard_map/ppermute | solution.py:375
  67.1 18.7 %collective-permute-start.2 = (bf16[2,64,2304]{2,1,0:T(8,128)(2,1)S(1)}, bf16[2,64,2304]{2,1,0:T(8,128)(2,1)S(1)}, u32[]{:S(2)}, u32[]{:S(2)}) collective-permute-start(bf16[2,64,2304]{2,1,0:T(8,128)(2,1)S(1)} %pad_maximum_fusion.2), channel_id=1, source_target_pairs={{0,1},{1,2},{2,3},{3,0},{4,5},{5,6},{6,7},{7,4},{8,9},{9,10},{10,1... | collective-permute-start | bytes 1769480 | tf_op jit(solution)/shard_map/ppermute | solution.py:375
  67.3 18.6 %collective-permute-start.3 = (bf16[2,64,2304]{2,1,0:T(8,128)(2,1)S(1)}, bf16[2,64,2304]{2,1,0:T(8,128)(2,1)S(1)}, u32[]{:S(2)}, u32[]{:S(2)}) collective-permute-start(bf16[2,64,2304]{2,1,0:T(8,128)(2,1)S(1)} %pad_maximum_fusion.3), channel_id=1, source_target_pairs={{0,3},{1,0},{2,1},{3,2},{4,7},{5,4},{6,5},{7,6},{8,11},{9,8},{10,9... | collective-permute-start | bytes 1769480 | tf_op jit(solution)/shard_map/ppermute | solution.py:375
  76.0 24.8 %collective-permute-start.9 = (bf16[4,64,2048]{2,1,0:T(8,128)(2,1)S(1)}, bf16[4,64,2048]{2,1,0:T(8,128)(2,1)S(1)}, u32[]{:S(2)}, u32[]{:S(2)}) collective-permute-start(bf16[4,64,2048]{2,1,0:T(8,128)(2,1)S(1)} %bitcast.56), channel_id=1, source_target_pairs={{0,4},{1,5},{2,6},{3,7},{4,0},{5,1},{6,2},{7,3},{8,12},{9,13},{10,... | collective-permute-start | bytes 3145736 | tf_op jit(solution)/shard_map/ppermute | solution.py:378
  78.2 16.8 %collective-permute-start.8 = (bf16[2,64,2304]{2,1,0:T(8,128)(2,1)S(1)}, bf16[2,64,2304]{2,1,0:T(8,128)(2,1)S(1)}, u32[]{:S(2)}, u32[]{:S(2)}) collective-permute-start(bf16[2,64,2304]{2,1,0:T(8,128)(2,1)S(1)} %pad_maximum_fusion.5), channel_id=1, source_target_pairs={{0,3},{1,0},{2,1},{3,2},{4,7},{5,4},{6,5},{7,6},{8,11},{9,8},{10,9... | collective-permute-start | bytes 1769480 | tf_op jit(solution)/shard_map/ppermute | solution.py:375
  81.3 16.8 %collective-permute-start.7 = (bf16[2,64,2304]{2,1,0:T(8,128)(2,1)S(1)}, bf16[2,64,2304]{2,1,0:T(8,128)(2,1)S(1)}, u32[]{:S(2)}, u32[]{:S(2)}) collective-permute-start(bf16[2,64,2304]{2,1,0:T(8,128)(2,1)S(1)} %pad_maximum_fusion.4), channel_id=1, source_target_pairs={{0,1},{1,2},{2,3},{3,0},{4,5},{5,6},{6,7},{7,4},{8,9},{9,10},{10,1... | collective-permute-start | bytes 1769480 | tf_op jit(solution)/shard_map/ppermute | solution.py:375
  101.4 6.4 %collective-permute-start.13 = (bf16[64,1792]{1,0:T(8,128)(2,1)S(1)}, bf16[64,1792]{1,0:T(8,128)(2,1)S(1)}, u32[]{:S(2)}, u32[]{:S(2)}) collective-permute-start(bf16[64,1792]{1,0:T(8,128)(2,1)S(1)} %get-tuple-element.121), channel_id=1, source_target_pairs={{0,3},{1,0},{2,1},{3,2},{4,7},{5,4},{6,5},{7,6},{8,11},{9,8},{10,9... | collective-permute-start | bytes 688136 | tf_op jit(solution)/shard_map/ppermute | solution.py:375
  104.6 13.5 %collective-permute-start.10 = (bf16[64,4608]{1,0:T(8,128)(2,1)S(1)}, bf16[64,4608]{1,0:T(8,128)(2,1)S(1)}, u32[]{:S(2)}, u32[]{:S(2)}) collective-permute-start(bf16[64,4608]{1,0:T(8,128)(2,1)S(1)} %fusion.10), channel_id=1, source_target_pairs={{0,4},{1,5},{2,6},{3,7},{4,0},{5,1},{6,2},{7,3},{8,12},{9,13},{10,... | collective-permute-start | bytes 1769480 | tf_op jit(solution)/shard_map/ppermute | solution.py:378
  105.9 7.5 %collective-permute-start.11 = (bf16[64,1792]{1,0:T(8,128)(2,1)S(1)}, bf16[64,1792]{1,0:T(8,128)(2,1)S(1)}, u32[]{:S(2)}, u32[]{:S(2)}) collective-permute-start(bf16[64,1792]{1,0:T(8,128)(2,1)S(1)} %get-tuple-element.120), channel_id=1, source_target_pairs={{0,1},{1,2},{2,3},{3,0},{4,5},{5,6},{6,7},{7,4},{8,9},{9,10},{10,1... | collective-permute-start | bytes 688136 | tf_op jit(solution)/shard_map/ppermute | solution.py:375
  107.9 10.9 %collective-permute-start.14 = (bf16[64,3584]{1,0:T(8,128)(2,1)S(1)}, bf16[64,3584]{1,0:T(8,128)(2,1)S(1)}, u32[]{:S(2)}, u32[]{:S(2)}) collective-permute-start(bf16[64,3584]{1,0:T(8,128)(2,1)S(1)} %pad_maximum_fusion.7), channel_id=1, source_target_pairs={{0,3},{1,0},{2,1},{3,2},{4,7},{5,4},{6,5},{7,6},{8,11},{9,8},{10,9... | collective-permute-start | bytes 1376264 | tf_op jit(solution)/shard_map/ppermute | solution.py:375
  113.5 10.6 %collective-permute-start.12 = (bf16[64,3584]{1,0:T(8,128)(2,1)S(1)}, bf16[64,3584]{1,0:T(8,128)(2,1)S(1)}, u32[]{:S(2)}, u32[]{:S(2)}) collective-permute-start(bf16[64,3584]{1,0:T(8,128)(2,1)S(1)} %pad_maximum_fusion.6), channel_id=1, source_target_pairs={{0,1},{1,2},{2,3},{3,0},{4,5},{5,6},{6,7},{7,4},{8,9},{9,10},{10,1... | collective-permute-start | bytes 1376264 | tf_op jit(solution)/shard_map/ppermute | solution.py:375

commit v7 on v6

--- a/solution.py
+++ b/solution.py
@@ -244,6 +244,8 @@
             f_row // stack == f_col // stack, lax.rem(f_col, stack) <= lax.rem(f_row, POS)
         )
         for b in range(half // each):
+            fetch(b).wait()
+        for b in range(half // each):
             length = jnp.zeros((1, width), jnp.int32)
             for e in range(each):
                 request = slots[b * each + e]
@@ -253,7 +255,6 @@
             q = new[:, 0:HD]
             key_n = new[:, HD : 2 * HD]
             val_n = pltpu.roll(key_n.astype(F32), span - POS, 0).astype(BF)
-            fetch(b).wait()
             own = slice(b * each * most, (b + 1) * each * most)
             key_c = pool[own, :, 0:HD].reshape(width, HD)
             val_c = pool[own, :, HD : 2 * HD].reshape(width, HD)
@@ -460,7 +461,7 @@
             [pltpu.VMEM(quarter, BF)] * 4,
             dma((5,)),
         ],
-        compiler_params=less,
+        compiler_params=params,
         name="front_products",
     )(table, first, second, back, out_weight)
 

time: 126 us -> 128 us (1.016)
  Pallas kernels: 31.7 us -> 33.9 us
    pallas_call x1, Pallas kernels: 6.08 us -> 8.29 us  [on_device(): pl.pallas_call(functools.partial(front_kernel, half=half, decode_rows=dec...]
where the time goes in v7:
time: 128 us; the launch traced here: 127 us
  starting transfers between devices  40.9 us (32%)
  waiting for transfers between devices  40.2 us (31%)
  Pallas kernels  33.9 us (26%)
  matrix products  7.89 us (6%)
  other arithmetic  2.99 us (2%)
    ppermute x12, waiting for transfers between devices, y_step(): lax.ppermute(x, 'tp', [(t, t // 4 * 4 + (t + step) % 4) for t in range(tp...  28.4 us
    ppermute x12, starting transfers between devices, y_step(): lax.ppermute(x, 'tp', [(t, t // 4 * 4 + (t + step) % 4) for t in range(tp...  19.7 us
    pallas_call x2, Pallas kernels, attend(): pl.pallas_call(functools.partial(local_kernel, half=half, decode_rows=dec...  18.5 us
    all_to_all x1, starting transfers between devices, on_device(): lax.all_to_all(parcel, 'group', split_axis=0, concat_axis=0, tiled=True)  11.6 us
    ppermute x3, waiting for transfers between devices, z_swap(): lax.ppermute(x, 'tp', [(t, (t + 4) % tp_count) for t in range(tp_count)])  9.59 us
    pallas_call x1, Pallas kernels, on_device(): pl.pallas_call(functools.partial(front_kernel, half=half, decode_rows=dec...  8.29 us
    dot_general x5, matrix products, products(): part = jnp.dot(given[name], weight, preferred_element_type=F32).astype(BF)  7.89 us
    all_to_all x1, starting transfers between devices, on_device(): lax.all_to_all(handed, 'group', split_axis=0, concat_axis=0, tiled=True)  6.3 us
  transfers between devices with their start and end apart: 17, of which 14 were waited for; matrix products, arithmetic and copies ran while one was open for 7% of the time, Pallas kernels for 15%

profile of v7, /device:TPU:2, one launch (start us, length us, event | category | flops | bytes accessed | tf_op | source)
XLA Modules:
  0.0 127.3 jit_solution(14881821926139364758)
XLA Ops:
  0.0 2.3 %pick_rows.1 = bf16[512,256]{1,0:T(8,128)(2,1)} custom-call(s32[1,256]{1,0:T(1,128)} %bitcast.41, bf16[512,512]{1,0:T(8,128)(2,1)} %refs_0_.3, bf16[512,256]{1,0:T(8,128)(2,1)} %refs_1_.1), custom_call_target="tpu_custom_call" | custom-call | tf_op jit(solution)/shard_map/pick_rows/pallas_call | solution.py:382
  2.3 11.6 %all-to-all-start = ((bf16[32,16,256]{2,1,0:T(8,128)(2,1)}), bf16[32,16,256]{2,1,0:T(8,128)(2,1)S(1)}, u32[]{:S(2)}, u32[]{:S(2)}) async-start(bf16[32,16,256]{2,1,0:T(8,128)(2,1)} %bitcast.53), calls=%async_computation | async-start | bytes 524288 | tf_op jit(solution)/shard_map/all_to_all | solution.py:390
  13.9 10.9 %local_attention.2 = (bf16[256,512]{1,0:T(8,128)(2,1)}, bf16[96,64,256]{2,1,0:T(8,128)(2,1)}) custom-call(s32[16]{0:T(128)} %prefix_len.3, s32[2048]{0:T(1024)} %resident_len.3, s32[256]{0:T(256)} %table.1, s32[6,256]{1,0:T(8,128)} %bitcast.61, bf16[512,512]{1,0:T(8,128)(2,1)} %refs_0_.3, bf16[512,256]{1,0:T(8,128)(2,1)} %refs_1_.1, ...), custom_call_target="tpu_custom_call" | custom-call | flops 4294967296 | bytes 5242880 | tf_op jit(solution)/shard_map/local_attention/pallas_call | solution.py:396
  24.9 0.5 all-to-all-done
  25.4 4.9 %handed_attention.1 = bf16[512,128]{1,0:T(8,128)(2,1)} custom-call(s32[256]{0:T(256)S(1)} %copy-done, s32[256]{0:T(256)S(1)} %copy-done.1, bf16[96,64,256]{2,1,0:T(8,128)(2,1)} %get-tuple-element.59.all_pages, bf16[512,256]{1,0:T(8,128)(2,1)S(1)} %bitcast.40), custom_call_target="tpu_custom_call" | custom-call | tf_op jit(solution)/shard_map/handed_attention/pallas_call | solution.py:426
  30.2 6.3 %all-to-all-start.1 = ((bf16[32,16,128]{2,1,0:T(8,128)(2,1)}), bf16[32,16,128]{2,1,0:T(8,128)(2,1)S(1)}, u32[]{:S(2)}, u32[]{:S(2)}) async-start(bf16[32,16,128]{2,1,0:T(8,128)(2,1)} %bitcast.4), calls=%async_computation.1 | async-start | bytes 262144 | tf_op jit(solution)/shard_map/all_to_all | solution.py:439
  36.6 7.6 %local_attention.3.second = bf16[256,512]{1,0:T(8,128)(2,1)} custom-call(s32[16]{0:T(128)} %prefix_len.3, s32[2048]{0:T(1024)} %resident_len.3, bf16[512,512]{1,0:T(8,128)(2,1)} %refs_0_.3, bf16[512,256]{1,0:T(8,128)(2,1)} %refs_1_.1, bf16[120,64,256]{2,1,0:T(8,128)(2,1)} %refs_2_.3), custom_call_target="tpu_custom_call" | custom-call | flops 4294967296 | bytes 5242880 | tf_op jit(solution)/shard_map/local_attention/pallas_call | solution.py:396
  44.1 1.7 %all-to-all-done.1 = bf16[32,16,128]{2,1,0:T(8,128)(2,1)S(1)} async-done(((bf16[32,16,128]{2,1,0:T(8,128)(2,1)}), bf16[32,16,128]{2,1,0:T(8,128)(2,1)S(1)}, u32[]{:S(2)}, u32[]{:S(2)}) %all-to-all-start.1) | async-done | bytes 131104 | tf_op jit(solution)/shard_map/all_to_all | solution.py:439
  45.8 0.6 copy-done.2
  46.5 8.3 %front_products.1 = (bf16[256,1536]{1,0:T(8,128)(2,1)}, bf16[128,1152]{1,0:T(8,128)(2,1)}, bf16[128,1152]{1,0:T(8,128)(2,1)}, bf16[128,1152]{1,0:T(8,128)(2,1)},...) custom-call(s32[1,256]{1,0:T(1,128)} %bitcast.42, ...), custom_call_target="tpu_custom_call" | custom-call | tf_op jit(solution)/shard_map/front_products/pallas_call | solution.py:444
  54.8 3.1 %collective-permute-start.1 = (bf16[2,64,1152]{2,1,0:T(8,128)(2,1)}, bf16[2,64,1152]{2,1,0:T(8,128)(2,1)S(1)}, u32[]{:S(2)}, u32[]{:S(2)}) collective-permute-start(bf16[2,64,1152]{2,1,0:T(8,128)(2,1)} %bitcast.60), channel_id=1, source_target_pairs={{0,3},{1,0},{2,1},{3,2},{4,7},{5,4},{6,5},{7,6},{8,11},{9,8},{10,9... | collective-permute-start | bytes 884744 | tf_op jit(solution)/shard_map/ppermute | solution.py:376
  57.9 1.0 collective-permute-start.4
  58.9 2.7 %convolution_convert_fusion.3 = bf16[256,2304]{1,0:T(8,128)(2,1)S(1)} fusion(bf16[256,512]{1,0:T(8,128)(2,1)} %get-tuple-element.89, bf16[512,8192]{1,0:T(8,128)(2,1)} %weight.1), kind=kOutput, calls=%fused_computation.4 | convolution fusion | flops 604569600 | bytes 3801088 | tf_op jit(solution)/shard_map/dot_general | solution.py:484
  61.5 0.7 collective-permute-start.5
  62.2 2.7 %collective-permute-start.6 = (bf16[2,64,1152]{2,1,0:T(8,128)(2,1)}, bf16[2,64,1152]{2,1,0:T(8,128)(2,1)S(1)}, u32[]{:S(2)}, u32[]{:S(2)}) collective-permute-start(bf16[2,64,1152]{2,1,0:T(8,128)(2,1)} %bitcast.57), channel_id=1, source_target_pairs={{0,3},{1,0},{2,1},{3,2},{4,7},{5,4},{6,5},{7,6},{8,11},{9,8},{10,9... | collective-permute-start | bytes 884744 | tf_op jit(solution)/shard_map/ppermute | solution.py:376
  64.9 2.4 %convolution_convert_fusion.4 = bf16[256,2048]{1,0:T(8,128)(2,1)S(1)} fusion(bf16[256,512]{1,0:T(8,128)(2,1)} %get-tuple-element.71, bf16[512,8192]{1,0:T(8,128)(2,1)} %weight.1), kind=kOutput, calls=%fused_computation.7 | convolution fusion | flops 537395200 | bytes 3407872 | tf_op jit(solution)/shard_map/dot_general | solution.py:484
  67.4 1.7 %collective-permute-done = bf16[2,64,1152]{2,1,0:T(8,128)(2,1)S(1)} collective-permute-done((bf16[2,64,1152]{2,1,0:T(8,128)(2,1)}, bf16[2,64,1152]{2,1,0:T(8,128)(2,1)S(1)}, u32[]{:S(2)}, u32[]{:S(2)}) %collective-permute-start) | collective-permute-done | bytes 294944 | tf_op jit(solution)/shard_map/ppermute | solution.py:376
  69.1 0.1 add_convert_fusion.5
  69.4 0.1 collective-permute-start.2
  69.5 3.3 %collective-permute-start.3 = (bf16[2,64,2304]{2,1,0:T(8,128)(2,1)S(1)}, bf16[2,64,2304]{2,1,0:T(8,128)(2,1)S(1)}, u32[]{:S(2)}, u32[]{:S(2)}) collective-permute-start(bf16[2,64,2304]{2,1,0:T(8,128)(2,1)S(1)} %pad_maximum_fusion.3), channel_id=1, source_target_pairs={{0,3},{1,0},{2,1},{3,2},{4,7},{5,4},{6,5},{7,6},{8,11},{9,8},{10,9... | collective-permute-start | bytes 1769480 | tf_op jit(solution)/shard_map/ppermute | solution.py:376
  72.8 2.6 %collective-permute-done.5 = bf16[2,64,1152]{2,1,0:T(8,128)(2,1)S(1)} collective-permute-done((bf16[2,64,1152]{2,1,0:T(8,128)(2,1)}, bf16[2,64,1152]{2,1,0:T(8,128)(2,1)S(1)}, u32[]{:S(2)}, u32[]{:S(2)}) %collective-permute-start.5) | collective-permute-done | bytes 294944 | tf_op jit(solution)/shard_map/ppermute | solution.py:376
  75.4 2.6 %collective-permute-done.4 = bf16[4,64,1536]{2,1,0:T(8,128)(2,1)S(1)} collective-permute-done((bf16[4,64,1536]{2,1,0:T(8,128)(2,1)}, bf16[4,64,1536]{2,1,0:T(8,128)(2,1)S(1)}, u32[]{:S(2)}, u32[]{:S(2)}) %collective-permute-start.4) | collective-permute-done | bytes 786464 | tf_op jit(solution)/shard_map/ppermute | solution.py:379
  78.0 1.1 collective-permute-start.9
  79.1 0.8 convolution_convert_fusion.2
  80.0 0.1 add_convert_fusion.4
  80.3 3.0 %collective-permute-start.8 = (bf16[2,64,2304]{2,1,0:T(8,128)(2,1)S(1)}, bf16[2,64,2304]{2,1,0:T(8,128)(2,1)S(1)}, u32[]{:S(2)}, u32[]{:S(2)}) collective-permute-start(bf16[2,64,2304]{2,1,0:T(8,128)(2,1)S(1)} %pad_maximum_fusion.5), channel_id=1, source_target_pairs={{0,3},{1,0},{2,1},{3,2},{4,7},{5,4},{6,5},{7,6},{8,11},{9,8},{10,9... | collective-permute-start | bytes 1769480 | tf_op jit(solution)/shard_map/ppermute | solution.py:376
  83.4 0.1 collective-permute-start.7
  83.5 0.9 convolution_convert_fusion
  84.4 1.2 convolution_convert_fusion.1
  85.5 2.5 %collective-permute-done.2 = bf16[2,64,2304]{2,1,0:T(8,128)(2,1)S(1)} collective-permute-done((bf16[2,64,2304]{2,1,0:T(8,128)(2,1)S(1)}, bf16[2,64,2304]{2,1,0:T(8,128)(2,1)S(1)}, u32[]{:S(2)}, u32[]{:S(2)}) %collective-permute-start.2) | collective-permute-done | bytes 589856 | tf_op jit(solution)/shard_map/ppermute | solution.py:376
  88.1 9.2 %collective-permute-done.8 = bf16[2,64,2304]{2,1,0:T(8,128)(2,1)S(1)} collective-permute-done((bf16[2,64,2304]{2,1,0:T(8,128)(2,1)S(1)}, bf16[2,64,2304]{2,1,0:T(8,128)(2,1)S(1)}, u32[]{:S(2)}, u32[]{:S(2)}) %collective-permute-start.8) | collective-permute-done | bytes 589856 | tf_op jit(solution)/shard_map/ppermute | solution.py:376
  97.2 3.1 %collective-permute-done.7 = bf16[2,64,2304]{2,1,0:T(8,128)(2,1)S(1)} collective-permute-done((bf16[2,64,2304]{2,1,0:T(8,128)(2,1)S(1)}, bf16[2,64,2304]{2,1,0:T(8,128)(2,1)S(1)}, u32[]{:S(2)}, u32[]{:S(2)}) %collective-permute-start.7) | collective-permute-done | bytes 589856 | tf_op jit(solution)/shard_map/ppermute | solution.py:376
  100.3 2.5 %collective-permute-done.9 = bf16[4,64,2048]{2,1,0:T(8,128)(2,1)S(1)} collective-permute-done((bf16[4,64,2048]{2,1,0:T(8,128)(2,1)S(1)}, bf16[4,64,2048]{2,1,0:T(8,128)(2,1)S(1)}, u32[]{:S(2)}, u32[]{:S(2)}) %collective-permute-start.9) | collective-permute-done | bytes 1048608 | tf_op jit(solution)/shard_map/ppermute | solution.py:379
  102.8 0.5 add_convert_fusion
  103.3 0.1 slice_bitcast_fusion.2
  103.4 2.7 %collective-permute-start.13 = (bf16[64,1792]{1,0:T(8,128)(2,1)S(1)}, bf16[64,1792]{1,0:T(8,128)(2,1)S(1)}, u32[]{:S(2)}, u32[]{:S(2)}) collective-permute-start(bf16[64,1792]{1,0:T(8,128)(2,1)S(1)} %get-tuple-element.121), channel_id=1, source_target_pairs={{0,3},{1,0},{2,1},{3,2},{4,7},{5,4},{6,5},{7,6},{8,11},{9,8},{10,9... | collective-permute-start | bytes 688136 | tf_op jit(solution)/shard_map/ppermute | solution.py:376
  106.1 0.4 add_convert_fusion.2
  106.6 1.3 collective-permute-start.10
  107.9 0.3 collective-permute-start.11
  108.2 1.6 %collective-permute-done.13 = bf16[64,1792]{1,0:T(8,128)(2,1)S(1)} collective-permute-done((bf16[64,1792]{1,0:T(8,128)(2,1)S(1)}, bf16[64,1792]{1,0:T(8,128)(2,1)S(1)}, u32[]{:S(2)}, u32[]{:S(2)}) %collective-permute-start.13) | collective-permute-done | bytes 229408 | tf_op jit(solution)/shard_map/ppermute | solution.py:376
  109.9 3.6 %collective-permute-start.14 = (bf16[64,3584]{1,0:T(8,128)(2,1)S(1)}, bf16[64,3584]{1,0:T(8,128)(2,1)S(1)}, u32[]{:S(2)}, u32[]{:S(2)}) collective-permute-start(bf16[64,3584]{1,0:T(8,128)(2,1)S(1)} %pad_maximum_fusion.7), channel_id=1, source_target_pairs={{0,3},{1,0},{2,1},{3,2},{4,7},{5,4},{6,5},{7,6},{8,11},{9,8},{10,9... | collective-permute-start | bytes 1376264 | tf_op jit(solution)/shard_map/ppermute | solution.py:376
  113.5 1.9 %collective-permute-done.11 = bf16[64,1792]{1,0:T(8,128)(2,1)S(1)} collective-permute-done((bf16[64,1792]{1,0:T(8,128)(2,1)S(1)}, bf16[64,1792]{1,0:T(8,128)(2,1)S(1)}, u32[]{:S(2)}, u32[]{:S(2)}) %collective-permute-start.11) | collective-permute-done | bytes 229408 | tf_op jit(solution)/shard_map/ppermute | solution.py:376
  115.6 4.5 %collective-permute-done.10 = bf16[64,4608]{1,0:T(8,128)(2,1)S(1)} collective-permute-done((bf16[64,4608]{1,0:T(8,128)(2,1)S(1)}, bf16[64,4608]{1,0:T(8,128)(2,1)S(1)}, u32[]{:S(2)}, u32[]{:S(2)}) %collective-permute-start.10) | collective-permute-done | bytes 589856 | tf_op jit(solution)/shard_map/ppermute | solution.py:379
  120.1 0.1 fusion.5
  120.3 0.5 collective-permute-done.14
  120.8 5.3 %collective-permute-done.12 = bf16[64,3584]{1,0:T(8,128)(2,1)S(1)} collective-permute-done((bf16[64,3584]{1,0:T(8,128)(2,1)S(1)}, bf16[64,3584]{1,0:T(8,128)(2,1)S(1)}, u32[]{:S(2)}, u32[]{:S(2)}) %collective-permute-start.12) | collective-permute-done | bytes 458784 | tf_op jit(solution)/shard_map/ppermute | solution.py:376
  126.1 0.2 fusion.7
  126.3 1.0 pad_maximum_fusion
  (38 shorter events, 0.8 us)
Async XLA Ops:
  2.3 23.1 %all-to-all-start = ((bf16[32,16,256]{2,1,0:T(8,128)(2,1)}), bf16[32,16,256]{2,1,0:T(8,128)(2,1)S(1)}, u32[]{:S(2)}, u32[]{:S(2)}) async-start(bf16[32,16,256]{2,1,0:T(8,128)(2,1)} %bitcast.53), calls=%async_computation | async-start | bytes 524288 | tf_op jit(solution)/shard_map/all_to_all | solution.py:390
  13.9 11.5 %copy-start = (s32[256]{0:T(256)S(1)}, s32[256]{0:T(256)}, u32[]{:S(2)}) copy-start(s32[256]{0:T(256)} %table.1) | copy-start | bytes 3076
  13.9 11.5 %copy-start.1 = (s32[256]{0:T(256)S(1)}, s32[256]{0:T(256)}, u32[]{:S(2)}) copy-start(s32[256]{0:T(256)} %lengths.1) | copy-start | bytes 3076
  30.2 15.6 %all-to-all-start.1 = ((bf16[32,16,128]{2,1,0:T(8,128)(2,1)}), bf16[32,16,128]{2,1,0:T(8,128)(2,1)S(1)}, u32[]{:S(2)}, u32[]{:S(2)}) async-start(bf16[32,16,128]{2,1,0:T(8,128)(2,1)} %bitcast.4), calls=%async_computation.1 | async-start | bytes 262144 | tf_op jit(solution)/shard_map/all_to_all | solution.py:439
  45.8 0.6 copy-start.2
  46.5 32.6 %slice-start = ((s8[8388608]{0:T(1024)(128)(4,1)}), s8[4194304]{0:T(1024)(128)(4,1)S(1)}, s32[]{:S(2)}) async-start(s8[8388608]{0:T(1024)(128)(4,1)} %bitcast.43), calls=%async_computation.2 | async-start | bytes 8388608
  54.8 12.6 %collective-permute-start.1 = (bf16[2,64,1152]{2,1,0:T(8,128)(2,1)}, bf16[2,64,1152]{2,1,0:T(8,128)(2,1)S(1)}, u32[]{:S(2)}, u32[]{:S(2)}) collective-permute-start(bf16[2,64,1152]{2,1,0:T(8,128)(2,1)} %bitcast.60), channel_id=1, source_target_pairs={{0,3},{1,0},{2,1},{3,2},{4,7},{5,4},{6,5},{7,6},{8,11},{9,8},{10,9... | collective-permute-start | bytes 884744 | tf_op jit(solution)/shard_map/ppermute | solution.py:376
  57.9 11.2 %collective-permute-start = (bf16[2,64,1152]{2,1,0:T(8,128)(2,1)}, bf16[2,64,1152]{2,1,0:T(8,128)(2,1)S(1)}, u32[]{:S(2)}, u32[]{:S(2)}) collective-permute-start(bf16[2,64,1152]{2,1,0:T(8,128)(2,1)} %bitcast.59), channel_id=1, source_target_pairs={{0,1},{1,2},{2,3},{3,0},{4,5},{5,6},{6,7},{7,4},{8,9},{9,10},{10,1... | collective-permute-start | bytes 884744 | tf_op jit(solution)/shard_map/ppermute | solution.py:376
  57.9 20.1 %collective-permute-start.4 = (bf16[4,64,1536]{2,1,0:T(8,128)(2,1)}, bf16[4,64,1536]{2,1,0:T(8,128)(2,1)S(1)}, u32[]{:S(2)}, u32[]{:S(2)}) collective-permute-start(bf16[4,64,1536]{2,1,0:T(8,128)(2,1)} %bitcast.56), channel_id=1, source_target_pairs={{0,4},{1,5},{2,6},{3,7},{4,0},{5,1},{6,2},{7,3},{8,12},{9,13},{10,... | collective-permute-start | bytes 2359304 | tf_op jit(solution)/shard_map/ppermute | solution.py:379
  58.9 20.2 %slice-start.1 = ((s8[8388608]{0:T(1024)(128)(4,1)}), s8[4194304]{0:T(1024)(128)(4,1)S(1)}, s32[]{:S(2)}) async-start(s8[8388608]{0:T(1024)(128)(4,1)} %bitcast.43), calls=%async_computation.3 | async-start | bytes 8388608
  61.5 13.9 %collective-permute-start.5 = (bf16[2,64,1152]{2,1,0:T(8,128)(2,1)}, bf16[2,64,1152]{2,1,0:T(8,128)(2,1)S(1)}, u32[]{:S(2)}, u32[]{:S(2)}) collective-permute-start(bf16[2,64,1152]{2,1,0:T(8,128)(2,1)} %bitcast.58), channel_id=1, source_target_pairs={{0,1},{1,2},{2,3},{3,0},{4,5},{5,6},{6,7},{7,4},{8,9},{9,10},{10,1... | collective-permute-start | bytes 884744 | tf_op jit(solution)/shard_map/ppermute | solution.py:376
  62.2 13.2 %collective-permute-start.6 = (bf16[2,64,1152]{2,1,0:T(8,128)(2,1)}, bf16[2,64,1152]{2,1,0:T(8,128)(2,1)S(1)}, u32[]{:S(2)}, u32[]{:S(2)}) collective-permute-start(bf16[2,64,1152]{2,1,0:T(8,128)(2,1)} %bitcast.57), channel_id=1, source_target_pairs={{0,3},{1,0},{2,1},{3,2},{4,7},{5,4},{6,5},{7,6},{8,11},{9,8},{10,9... | collective-permute-start | bytes 884744 | tf_op jit(solution)/shard_map/ppermute | solution.py:376
  69.2 9.9 %copy-start.4 = (bf16[256,512]{1,0:T(8,128)(2,1)S(1)}, bf16[256,512]{1,0:T(8,128)(2,1)}, u32[]{:S(2)}) copy-start(bf16[256,512]{1,0:T(8,128)(2,1)} %get-tuple-element.89) | copy-start | bytes 786436
  69.4 18.7 %collective-permute-start.2 = (bf16[2,64,2304]{2,1,0:T(8,128)(2,1)S(1)}, bf16[2,64,2304]{2,1,0:T(8,128)(2,1)S(1)}, u32[]{:S(2)}, u32[]{:S(2)}) collective-permute-start(bf16[2,64,2304]{2,1,0:T(8,128)(2,1)S(1)} %pad_maximum_fusion.2), channel_id=1, source_target_pairs={{0,1},{1,2},{2,3},{3,0},{4,5},{5,6},{6,7},{7,4},{8,9},{9,10},{10,1... | collective-permute-start | bytes 1769480 | tf_op jit(solution)/shard_map/ppermute | solution.py:376
  69.5 18.6 %collective-permute-start.3 = (bf16[2,64,2304]{2,1,0:T(8,128)(2,1)S(1)}, bf16[2,64,2304]{2,1,0:T(8,128)(2,1)S(1)}, u32[]{:S(2)}, u32[]{:S(2)}) collective-permute-start(bf16[2,64,2304]{2,1,0:T(8,128)(2,1)S(1)} %pad_maximum_fusion.3), channel_id=1, source_target_pairs={{0,3},{1,0},{2,1},{3,2},{4,7},{5,4},{6,5},{7,6},{8,11},{9,8},{10,9... | collective-permute-start | bytes 1769480 | tf_op jit(solution)/shard_map/ppermute | solution.py:376
  78.0 24.8 %collective-permute-start.9 = (bf16[4,64,2048]{2,1,0:T(8,128)(2,1)S(1)}, bf16[4,64,2048]{2,1,0:T(8,128)(2,1)S(1)}, u32[]{:S(2)}, u32[]{:S(2)}) collective-permute-start(bf16[4,64,2048]{2,1,0:T(8,128)(2,1)S(1)} %bitcast.55), channel_id=1, source_target_pairs={{0,4},{1,5},{2,6},{3,7},{4,0},{5,1},{6,2},{7,3},{8,12},{9,13},{10,... | collective-permute-start | bytes 3145736 | tf_op jit(solution)/shard_map/ppermute | solution.py:379
  80.1 3.4 %copy-start.5 = (bf16[128,512]{1,0:T(8,128)(2,1)S(1)}, bf16[128,512]{1,0:T(8,128)(2,1)}, u32[]{:S(2)}) copy-start(bf16[128,512]{1,0:T(8,128)(2,1)} %get-tuple-element.96) | copy-start | bytes 393220
  80.3 16.9 %collective-permute-start.8 = (bf16[2,64,2304]{2,1,0:T(8,128)(2,1)S(1)}, bf16[2,64,2304]{2,1,0:T(8,128)(2,1)S(1)}, u32[]{:S(2)}, u32[]{:S(2)}) collective-permute-start(bf16[2,64,2304]{2,1,0:T(8,128)(2,1)S(1)} %pad_maximum_fusion.5), channel_id=1, source_target_pairs={{0,3},{1,0},{2,1},{3,2},{4,7},{5,4},{6,5},{7,6},{8,11},{9,8},{10,9... | collective-permute-start | bytes 1769480 | tf_op jit(solution)/shard_map/ppermute | solution.py:376
  83.4 1.0 copy-start.3
  83.4 16.9 %collective-permute-start.7 = (bf16[2,64,2304]{2,1,0:T(8,128)(2,1)S(1)}, bf16[2,64,2304]{2,1,0:T(8,128)(2,1)S(1)}, u32[]{:S(2)}, u32[]{:S(2)}) collective-permute-start(bf16[2,64,2304]{2,1,0:T(8,128)(2,1)S(1)} %pad_maximum_fusion.4), channel_id=1, source_target_pairs={{0,1},{1,2},{2,3},{3,0},{4,5},{5,6},{6,7},{7,4},{8,9},{9,10},{10,1... | collective-permute-start | bytes 1769480 | tf_op jit(solution)/shard_map/ppermute | solution.py:376
  103.4 6.4 %collective-permute-start.13 = (bf16[64,1792]{1,0:T(8,128)(2,1)S(1)}, bf16[64,1792]{1,0:T(8,128)(2,1)S(1)}, u32[]{:S(2)}, u32[]{:S(2)}) collective-permute-start(bf16[64,1792]{1,0:T(8,128)(2,1)S(1)} %get-tuple-element.121), channel_id=1, source_target_pairs={{0,3},{1,0},{2,1},{3,2},{4,7},{5,4},{6,5},{7,6},{8,11},{9,8},{10,9... | collective-permute-start | bytes 688136 | tf_op jit(solution)/shard_map/ppermute | solution.py:376
  106.6 13.5 %collective-permute-start.10 = (bf16[64,4608]{1,0:T(8,128)(2,1)S(1)}, bf16[64,4608]{1,0:T(8,128)(2,1)S(1)}, u32[]{:S(2)}, u32[]{:S(2)}) collective-permute-start(bf16[64,4608]{1,0:T(8,128)(2,1)S(1)} %fusion.10), channel_id=1, source_target_pairs={{0,4},{1,5},{2,6},{3,7},{4,0},{5,1},{6,2},{7,3},{8,12},{9,13},{10,... | collective-permute-start | bytes 1769480 | tf_op jit(solution)/shard_map/ppermute | solution.py:379
  107.9 7.5 %collective-permute-start.11 = (bf16[64,1792]{1,0:T(8,128)(2,1)S(1)}, bf16[64,1792]{1,0:T(8,128)(2,1)S(1)}, u32[]{:S(2)}, u32[]{:S(2)}) collective-permute-start(bf16[64,1792]{1,0:T(8,128)(2,1)S(1)} %get-tuple-element.120), channel_id=1, source_target_pairs={{0,1},{1,2},{2,3},{3,0},{4,5},{5,6},{6,7},{7,4},{8,9},{9,10},{10,1... | collective-permute-start | bytes 688136 | tf_op jit(solution)/shard_map/ppermute | solution.py:376
  109.9 10.9 %collective-permute-start.14 = (bf16[64,3584]{1,0:T(8,128)(2,1)S(1)}, bf16[64,3584]{1,0:T(8,128)(2,1)S(1)}, u32[]{:S(2)}, u32[]{:S(2)}) collective-permute-start(bf16[64,3584]{1,0:T(8,128)(2,1)S(1)} %pad_maximum_fusion.7), channel_id=1, source_target_pairs={{0,3},{1,0},{2,1},{3,2},{4,7},{5,4},{6,5},{7,6},{8,11},{9,8},{10,9... | collective-permute-start | bytes 1376264 | tf_op jit(solution)/shard_map/ppermute | solution.py:376
  115.5 10.6 %collective-permute-start.12 = (bf16[64,3584]{1,0:T(8,128)(2,1)S(1)}, bf16[64,3584]{1,0:T(8,128)(2,1)S(1)}, u32[]{:S(2)}, u32[]{:S(2)}) collective-permute-start(bf16[64,3584]{1,0:T(8,128)(2,1)S(1)} %pad_maximum_fusion.6), channel_id=1, source_target_pairs={{0,1},{1,2},{2,3},{3,0},{4,5},{5,6},{6,7},{7,4},{8,9},{9,10},{10,1... | collective-permute-start | bytes 1376264 | tf_op jit(solution)/shard_map/ppermute | solution.py:376
